TPU v7x, 32 devices: a whole 2x2x4 slice. The times are simulated.
32 devices in a mesh: seg: 4 (over y, x), bond: 8 (over z, core).
Axes of the slice: x: 2, y: 2, z: 4, core: 2. Of those that a mesh axis runs over, the one named last changes fastest.
Arguments:
- sites: float32 [4, 2, 8192, 8192], P('seg', None, 'bond'), may hold values from -0.6629126 to 0.6629126, as said below
- boundary: float32 [8192], P('bond'), may hold values from -6 to 6
- bits: int32 [32, 4], P(None, 'seg'), may hold values from 0 to 1
- order: int32 [32], replicated, may hold values from 0 to 31, each once
Outputs:
- probs: float32 [32, 4], P(None, 'seg')
Inputs may be any that keep to these rules, and one draw needn't show every extreme that they name: `order`: each slot number appears once. `sites`: real entries.
All inputs are finite; a program needn't handle non-finite values.
Results may differ from a plain program's by a relative error of at most 0.0001.
Values sent between devices are 32-bit elements; how exact they have to be, the bound alone decides.
No kernel may reach another device: no remote copies, remote signals or barrier semaphores. Data moves between devices by JAX's collectives and lax.ppermute only.
A program may use at most 128 MiB of HBM per device.

v0:
```python
import jax
import jax.numpy as jnp
from jax import lax
from jax.sharding import PartitionSpec as P

D = 8192
ROWS = 32
MB = 32


EPSILON = 1e-06


def shifted(array, axis, by):
    count = lax.axis_size(axis)
    pairs = [(i, i + by) for i in range(count) if 0 <= i + by < count]
    return lax.ppermute(array, axis, pairs)


def advance(site_piece, env_cols, scale, outcome):
    slots = env_cols.shape[1]
    term = jnp.einsum(
        "slr,lm->rsm",
        site_piece,
        env_cols,
        precision=lax.Precision.HIGHEST,
        preferred_element_type=jnp.float32,
    )
    shard = lax.psum_scatter(
        term.reshape(lax.axis_size("bond") * site_piece.shape[1], 2 * slots),
        "bond",
        scatter_dimension=0,
        tiled=True,
    )
    amps = shard.reshape(shard.shape[0], 2, slots)
    local_sq = jnp.sum(amps * amps, axis=0)
    totals = lax.psum(local_sq, "bond")
    means = totals / (D * scale)[None, :] + EPSILON
    picked = outcome == 1
    chosen = jnp.where(picked[None, :], amps[:, 1, :], amps[:, 0, :])
    weight = jnp.where(picked, means[1], means[0])
    probs = weight / (means[0] + means[1])
    env_next = chosen * lax.rsqrt(scale * weight)[None, :]
    scale_next = jnp.ones_like(scale)
    return (env_next, scale_next, probs)


def on_device(sites, boundary, bits, order):
    group = lax.axis_index("seg")
    sections = lax.axis_size("seg")
    block = MB
    count = ROWS // block
    steps = count + sections - 1
    slot_bits = jnp.take(bits, order, axis=0)
    local_width = sites.shape[2]
    start_env = jnp.broadcast_to(boundary[:, None], (local_width, block))
    unit_scale = jnp.ones((block,), jnp.float32)

    def one_step(step, carry):
        env_in, scale_in, table = carry
        batch = step - group
        valid = jnp.logical_and(batch >= 0, batch < count)
        clipped = jnp.clip(batch, 0, count - 1)
        first = group == 0
        env_cols = jnp.where(first, start_env, env_in)
        scale = jnp.where(first, unit_scale, scale_in)
        env_cols, scale, probs = advance(sites[0], env_cols, scale, slot_bits[:, 0])
        columns = [probs]
        block_probs = jnp.stack(columns, axis=1)
        updated = lax.dynamic_update_slice(table, block_probs, (clipped * block, jnp.int32(0)))
        table = jnp.where(valid, updated, table)
        env_out = shifted(env_cols, "seg", 1)
        return (env_out, scale, table)

    table_init = jnp.zeros((ROWS, sites.shape[0]), jnp.float32)
    env_init = jnp.zeros((local_width, block), jnp.float32)
    final = lax.fori_loop(0, steps, one_step, (env_init, unit_scale, table_init))
    return final[2]


def solution(mesh):
    return jax.shard_map(
        on_device,
        mesh=mesh,
        in_specs=(P("seg", None, "bond", None), P("bond"), P(None, "seg"), P()),
        out_specs=P(None, "seg"),
        check_vma=False,
    )
```

profile of v0, /device:TPU:6, one launch (start us, length us, event | category | flops | bytes accessed | tf_op | source)
XLA Modules:
  0.0 430.4 jit_solution(5708988542913449083)
XLA Ops:
  6.5 0.0 copy-start
  6.5 0.7 compare_select_fusion
  7.2 0.0 copy-done
  7.2 0.7 gather_fusion
  7.9 0.7 fusion.14
  8.6 414.7 %while.17 = (s32[]{:T(128)}, f32[1024,32]{0,1:T(8,128)S(1)}, f32[32,1]{0,1:T(1,128)S(1)}, s32[32,1]{0,1:T(1,128)S(1)}, pred[]{:T(512)}, /*index=5*/f32[1,2,1024,...) while((s32[]{:T(128)}, f32[1024,32]{0,1:T(8,128)S(1)}, ...), condition=%wide.region_4.5_spmd.clone, body=%wide.region_0.4_spmd.clone.sunk | while | flops 6442680320 | bytes 77602208 | solution.py:77
  8.6 0.0 reduce-scatter.2.cloned.1.call-start
  8.7 45.1 %fusion.23 = f32[32,2,8192]{2,0,1:T(8,128)} fusion(f32[1,2,1024,8192]{3,2,1,0:T(8,128)} %get-tuple-element.283, f32[1024,32]{0,1:T(8,128)S(1)} %get-tuple-element.269, f32[1024]{0:T(1024)} %get-tuple-element.285, pred[]{:T(512)} %get-tuple-element.282), kind=kOutput, calls=%fused_computation.2.clone.1 | convolution fusion | flops 6442483712 | bytes 69341184 | tf_op jit(solution)/shard_map/while/body/eval_jaxpr/slr,lm->rsm/dot_general | solution.py:22
  53.8 0.0 reduce-scatter.2.cloned.1.call-update
  53.8 37.1 %reduce-scatter.2.cloned.1.call-done = f32[1024,64]{0,1:T(8,128)} async-done(((f32[8192,64]{0,1:T(8,128)}), f32[1024,64]{0,1:T(8,128)}) %reduce-scatter.2.cloned.1.call-update) | async-done | bytes 262160 | tf_op jit(solution)/shard_map/while/body/eval_jaxpr/reduce_scatter | solution.py:29
  90.9 1.1 multiply_reduce_fusion.2
  92.0 0.1 reduce_sum.19
  92.1 14.7 %psum.14 = f32[2,32]{1,0:T(2,128)S(1)} all-reduce(f32[2,32]{1,0:T(2,128)S(1)} %reduce_sum.19), channel_id=1, replica_groups=mesh['seg'=4,'bond'=8] {'bond'}, use_global_device_ids=true, to_apply=%region_3.3 | all-reduce | flops 64 | bytes 512 | tf_op jit(solution)/shard_map/while/body/eval_jaxpr/psum | solution.py:37
  106.8 1.1 fusion.26
  107.9 1.3 collective-permute-start
  109.2 5.5 %collective-permute-done = f32[1024,32]{0,1:T(8,128)S(1)} collective-permute-done((f32[1024,32]{0,1:T(8,128)S(1)}, f32[1024,32]{0,1:T(8,128)S(1)}, u32[]{:S(2)}, u32[]{:S(2)}) %collective-permute-start) | collective-permute-done | bytes 131104 | tf_op jit(solution)/shard_map/while/body/eval_jaxpr/ppermute | solution.py:17
  114.7 0.0 reduce-scatter.2.cloned.1.call-start
  114.7 45.1 %fusion.23 = f32[32,2,8192]{2,0,1:T(8,128)} fusion(f32[1,2,1024,8192]{3,2,1,0:T(8,128)} %get-tuple-element.283, f32[1024,32]{0,1:T(8,128)S(1)} %get-tuple-element.269, f32[1024]{0:T(1024)} %get-tuple-element.285, pred[]{:T(512)} %get-tuple-element.282), kind=kOutput, calls=%fused_computation.2.clone.1 | convolution fusion | flops 6442483712 | bytes 69341184 | tf_op jit(solution)/shard_map/while/body/eval_jaxpr/slr,lm->rsm/dot_general | solution.py:22
  159.8 0.0 reduce-scatter.2.cloned.1.call-update
  159.9 34.1 %reduce-scatter.2.cloned.1.call-done = f32[1024,64]{0,1:T(8,128)} async-done(((f32[8192,64]{0,1:T(8,128)}), f32[1024,64]{0,1:T(8,128)}) %reduce-scatter.2.cloned.1.call-update) | async-done | bytes 262160 | tf_op jit(solution)/shard_map/while/body/eval_jaxpr/reduce_scatter | solution.py:29
  193.9 1.1 multiply_reduce_fusion.2
  195.0 0.1 reduce_sum.19
  195.1 14.5 %psum.14 = f32[2,32]{1,0:T(2,128)S(1)} all-reduce(f32[2,32]{1,0:T(2,128)S(1)} %reduce_sum.19), channel_id=1, replica_groups=mesh['seg'=4,'bond'=8] {'bond'}, use_global_device_ids=true, to_apply=%region_3.3 | all-reduce | flops 64 | bytes 512 | tf_op jit(solution)/shard_map/while/body/eval_jaxpr/psum | solution.py:37
  209.6 1.1 fusion.26
  210.7 1.3 collective-permute-start
  212.0 5.5 %collective-permute-done = f32[1024,32]{0,1:T(8,128)S(1)} collective-permute-done((f32[1024,32]{0,1:T(8,128)S(1)}, f32[1024,32]{0,1:T(8,128)S(1)}, u32[]{:S(2)}, u32[]{:S(2)}) %collective-permute-start) | collective-permute-done | bytes 131104 | tf_op jit(solution)/shard_map/while/body/eval_jaxpr/ppermute | solution.py:17
  217.6 0.0 reduce-scatter.2.cloned.1.call-start
  217.6 45.1 %fusion.23 = f32[32,2,8192]{2,0,1:T(8,128)} fusion(f32[1,2,1024,8192]{3,2,1,0:T(8,128)} %get-tuple-element.283, f32[1024,32]{0,1:T(8,128)S(1)} %get-tuple-element.269, f32[1024]{0:T(1024)} %get-tuple-element.285, pred[]{:T(512)} %get-tuple-element.282), kind=kOutput, calls=%fused_computation.2.clone.1 | convolution fusion | flops 6442483712 | bytes 69341184 | tf_op jit(solution)/shard_map/while/body/eval_jaxpr/slr,lm->rsm/dot_general | solution.py:22
  262.7 0.0 reduce-scatter.2.cloned.1.call-update
  262.7 34.1 %reduce-scatter.2.cloned.1.call-done = f32[1024,64]{0,1:T(8,128)} async-done(((f32[8192,64]{0,1:T(8,128)}), f32[1024,64]{0,1:T(8,128)}) %reduce-scatter.2.cloned.1.call-update) | async-done | bytes 262160 | tf_op jit(solution)/shard_map/while/body/eval_jaxpr/reduce_scatter | solution.py:29
  296.8 1.1 multiply_reduce_fusion.2
  297.9 0.1 reduce_sum.19
  298.0 14.6 %psum.14 = f32[2,32]{1,0:T(2,128)S(1)} all-reduce(f32[2,32]{1,0:T(2,128)S(1)} %reduce_sum.19), channel_id=1, replica_groups=mesh['seg'=4,'bond'=8] {'bond'}, use_global_device_ids=true, to_apply=%region_3.3 | all-reduce | flops 64 | bytes 512 | tf_op jit(solution)/shard_map/while/body/eval_jaxpr/psum | solution.py:37
  312.6 1.1 fusion.26
  313.6 1.3 collective-permute-start
  315.0 5.5 %collective-permute-done = f32[1024,32]{0,1:T(8,128)S(1)} collective-permute-done((f32[1024,32]{0,1:T(8,128)S(1)}, f32[1024,32]{0,1:T(8,128)S(1)}, u32[]{:S(2)}, u32[]{:S(2)}) %collective-permute-start) | collective-permute-done | bytes 131104 | tf_op jit(solution)/shard_map/while/body/eval_jaxpr/ppermute | solution.py:17
  320.5 0.0 reduce-scatter.2.cloned.1.call-start
  320.5 45.1 %fusion.23 = f32[32,2,8192]{2,0,1:T(8,128)} fusion(f32[1,2,1024,8192]{3,2,1,0:T(8,128)} %get-tuple-element.283, f32[1024,32]{0,1:T(8,128)S(1)} %get-tuple-element.269, f32[1024]{0:T(1024)} %get-tuple-element.285, pred[]{:T(512)} %get-tuple-element.282), kind=kOutput, calls=%fused_computation.2.clone.1 | convolution fusion | flops 6442483712 | bytes 69341184 | tf_op jit(solution)/shard_map/while/body/eval_jaxpr/slr,lm->rsm/dot_general | solution.py:22
  365.6 0.0 reduce-scatter.2.cloned.1.call-update
  365.7 34.1 %reduce-scatter.2.cloned.1.call-done = f32[1024,64]{0,1:T(8,128)} async-done(((f32[8192,64]{0,1:T(8,128)}), f32[1024,64]{0,1:T(8,128)}) %reduce-scatter.2.cloned.1.call-update) | async-done | bytes 262160 | tf_op jit(solution)/shard_map/while/body/eval_jaxpr/reduce_scatter | solution.py:29
  399.8 1.1 multiply_reduce_fusion.2
  400.8 0.1 reduce_sum.19
  400.9 14.5 %psum.14 = f32[2,32]{1,0:T(2,128)S(1)} all-reduce(f32[2,32]{1,0:T(2,128)S(1)} %reduce_sum.19), channel_id=1, replica_groups=mesh['seg'=4,'bond'=8] {'bond'}, use_global_device_ids=true, to_apply=%region_3.3 | all-reduce | flops 64 | bytes 512 | tf_op jit(solution)/shard_map/while/body/eval_jaxpr/psum | solution.py:37
  415.4 1.1 fusion.26
  416.5 1.3 collective-permute-start
  417.8 5.5 %collective-permute-done = f32[1024,32]{0,1:T(8,128)S(1)} collective-permute-done((f32[1024,32]{0,1:T(8,128)S(1)}, f32[1024,32]{0,1:T(8,128)S(1)}, u32[]{:S(2)}, u32[]{:S(2)}) %collective-permute-start) | collective-permute-done | bytes 131104 | tf_op jit(solution)/shard_map/while/body/eval_jaxpr/ppermute | solution.py:17
  423.3 0.0 copy-start.1
  423.4 0.5 copy-done.1
  (19 shorter events, 0.2 us)
Async XLA Ops:
  6.5 0.7 copy-start
  8.6 82.3 %reduce-scatter.2.cloned.1.call-start = ((), (), s32[]{:S(2)}) async-start(), calls=%async_computation.1 | async-start | bytes 2359296 | tf_op jit(solution)/shard_map/while/body/eval_jaxpr/reduce_scatter | solution.py:29
  107.9 6.9 %collective-permute-start = (f32[1024,32]{0,1:T(8,128)S(1)}, f32[1024,32]{0,1:T(8,128)S(1)}, u32[]{:S(2)}, u32[]{:S(2)}) collective-permute-start(f32[1024,32]{0,1:T(8,128)S(1)} %fusion.26), channel_id=1, source_target_pairs={{0,8},{8,16},{16,24},{1,9},{9,17},{17,25},{2,10},{10,18},{18,26},{... | collective-permute-start | bytes 393224 | tf_op jit(solution)/shard_map/while/body/eval_jaxpr/ppermute | solution.py:17
  114.7 79.2 %reduce-scatter.2.cloned.1.call-start = ((), (), s32[]{:S(2)}) async-start(), calls=%async_computation.1 | async-start | bytes 2359296 | tf_op jit(solution)/shard_map/while/body/eval_jaxpr/reduce_scatter | solution.py:29
  210.7 6.9 %collective-permute-start = (f32[1024,32]{0,1:T(8,128)S(1)}, f32[1024,32]{0,1:T(8,128)S(1)}, u32[]{:S(2)}, u32[]{:S(2)}) collective-permute-start(f32[1024,32]{0,1:T(8,128)S(1)} %fusion.26), channel_id=1, source_target_pairs={{0,8},{8,16},{16,24},{1,9},{9,17},{17,25},{2,10},{10,18},{18,26},{... | collective-permute-start | bytes 393224 | tf_op jit(solution)/shard_map/while/body/eval_jaxpr/ppermute | solution.py:17
  217.6 79.3 %reduce-scatter.2.cloned.1.call-start = ((), (), s32[]{:S(2)}) async-start(), calls=%async_computation.1 | async-start | bytes 2359296 | tf_op jit(solution)/shard_map/while/body/eval_jaxpr/reduce_scatter | solution.py:29
  313.6 6.9 %collective-permute-start = (f32[1024,32]{0,1:T(8,128)S(1)}, f32[1024,32]{0,1:T(8,128)S(1)}, u32[]{:S(2)}, u32[]{:S(2)}) collective-permute-start(f32[1024,32]{0,1:T(8,128)S(1)} %fusion.26), channel_id=1, source_target_pairs={{0,8},{8,16},{16,24},{1,9},{9,17},{17,25},{2,10},{10,18},{18,26},{... | collective-permute-start | bytes 393224 | tf_op jit(solution)/shard_map/while/body/eval_jaxpr/ppermute | solution.py:17
  320.5 79.3 %reduce-scatter.2.cloned.1.call-start = ((), (), s32[]{:S(2)}) async-start(), calls=%async_computation.1 | async-start | bytes 2359296 | tf_op jit(solution)/shard_map/while/body/eval_jaxpr/reduce_scatter | solution.py:29
  416.5 6.9 %collective-permute-start = (f32[1024,32]{0,1:T(8,128)S(1)}, f32[1024,32]{0,1:T(8,128)S(1)}, u32[]{:S(2)}, u32[]{:S(2)}) collective-permute-start(f32[1024,32]{0,1:T(8,128)S(1)} %fusion.26), channel_id=1, source_target_pairs={{0,8},{8,16},{16,24},{1,9},{9,17},{17,25},{2,10},{10,18},{18,26},{... | collective-permute-start | bytes 393224 | tf_op jit(solution)/shard_map/while/body/eval_jaxpr/ppermute | solution.py:17
  423.3 0.5 copy-start.1
Sparse Core Ops, SparseCore 0:
  53.9 36.9 reduce-scatter.1
  160.0 33.9 reduce-scatter.1
  262.8 33.9 reduce-scatter.1
  365.8 33.9 reduce-scatter.1
where the time goes:
time: 432 us; the launch traced here: 430 us
  matrix products  180 us (42%)
  waiting for transfers between devices  162 us (38%)
  blocking collectives  58.3 us (13%)
  between operations  13.1 us (3%)
  other arithmetic  9.98 us (2%)
  starting transfers between devices  5.22 us (1%)
    dot_general x4, matrix products, advance(): jnp.einsum('slr,lm->rsm', site_piece, env_cols, precision=lax.Precision.H...  180 us
    reduce_scatter x4, waiting for transfers between devices, advance(): lax.psum_scatter(term.reshape(lax.axis_size('bond') * site_piece.shape[1]...  139 us
    psum x4, blocking collectives, advance(): totals = lax.psum(local_sq, 'bond')  58.3 us
    ppermute x4, waiting for transfers between devices, shifted(): return lax.ppermute(array, axis, pairs)  22.2 us
  transfers between devices with their start and end apart: 8, of which 8 were waited for; matrix products, arithmetic and copies ran while one was open for 0% of the time, Pallas kernels for 0%

commit v1 on v0

v1 whole, which is shorter than its diff:
```python
import functools

import jax
import jax.numpy as jnp
from jax import lax
from jax.experimental import pallas as pl
from jax.experimental.pallas import tpu as pltpu
from jax.sharding import PartitionSpec as P

EPSILON = 1e-06
AXES = ("seg", "bond")
LANES = 128
MIB = 2**20
HELD_BYTES = 48 * MIB
BLOCK = 2048
RING = 4
SCOPE = 12 * MIB
F32 = jnp.float32
BF16 = jnp.bfloat16
VMEM = pl.BlockSpec(memory_space=pltpu.VMEM)
ANY = pl.BlockSpec(memory_space=pl.ANY)


class Sizes:
    def __init__(self, sites, bits):
        assert sites.shape[0] == 1
        self.segs = lax.axis_size("seg")
        self.bonds = lax.axis_size("bond")
        self.half = self.bonds // 2
        self.left, self.right = sites.shape[2], sites.shape[3]
        self.chunk = self.right // self.bonds
        assert self.chunk == self.left and self.bonds % 2 == 0
        self.rows = bits.shape[0]
        self.most = 2**self.segs
        need = max(2 * self.most - 2, self.rows * self.segs)
        self.extra = -(-need // LANES) * LANES
        self.width = self.chunk + self.extra
        self.block = min(BLOCK, self.right)
        self.per_bit = self.right // self.block
        self.blocks = 2 * self.per_bit
        self.held = min(self.blocks, HELD_BYTES // (self.left * self.block * 4))
        self.piece = min(512, self.chunk)
        self.pieces = self.block // self.piece

    def place(self, column):
        owner = column // self.chunk
        return owner // 2, owner % 2


def split(x):
    high = x.astype(BF16)
    return high, (x - high.astype(F32)).astype(BF16)


def piece_copy(sz, site, ring, sems, index):
    per = sz.right // sz.piece
    column = pl.multiple_of((index % per) * sz.piece, sz.piece)
    slot = index % RING
    return pltpu.make_async_copy(
        site.at[index // per, :, pl.ds(column, sz.piece)], ring.at[slot], sems.at[slot]
    )


def bit_row(sz, bits_ref, group, extra):
    mine = bits_ref[...].astype(F32)
    wide = jnp.concatenate([mine] * (sz.extra // sz.rows), axis=1) if sz.extra > sz.rows else mine
    lane = lax.broadcasted_iota(jnp.int32, (1, sz.extra), 1)
    return extra + jnp.where(lane // sz.rows == group, wide, 0.0)


def first_kernel(sz, bits_ref, start_ref, site, keep, give, fin_keep, fin_give, *rest):
    highs, lows = rest[: sz.held], rest[sz.held : 2 * sz.held]
    ring, spread, out, sems = rest[2 * sz.held :]
    group = lax.axis_index("seg")
    bond = lax.axis_index("bond")
    core = bond % 2
    copy = functools.partial(piece_copy, sz, site, ring, sems)

    @pl.when(group == 0)
    def _():
        total = 2 * sz.right // sz.piece
        for i in range(RING):
            copy(i).start()
        turned = jnp.transpose(jnp.broadcast_to(start_ref[...], (8, sz.left)))
        spread[...] = jnp.broadcast_to(turned[:, 0:1], (sz.left, LANES))
        out[...] = jnp.zeros_like(out)
        per = sz.right // sz.piece
        for bit in range(2):

            def body(i, _):
                index = bit * per + i
                slot = index % RING
                copy(index).wait()
                sums = [None] * (sz.piece // LANES)
                for g in range(sz.left // 8):
                    env = spread[g * 8 : (g + 1) * 8, :]
                    for j in range(len(sums)):
                        term = ring[slot, g * 8 : (g + 1) * 8, j * LANES : (j + 1) * LANES] * env
                        sums[j] = term if g == 0 else sums[j] + term

                @pl.when(index + RING < total)
                def _():
                    copy(index + RING).start()

                column = i * sz.piece
                pair, side = sz.place(column)
                offset = pl.multiple_of(column % sz.chunk, sz.piece)
                row = jnp.concatenate([jnp.sum(s, axis=0, keepdims=True) for s in sums], axis=1)
                out[side, pair, bit : bit + 1, pl.ds(offset, sz.piece)] = row
                return 0

            lax.fori_loop(0, per, body, 0)
        none = jnp.zeros((1, sz.extra), F32)
        row = jnp.where(bond == 0, bit_row(sz, bits_ref, group, none), 0.0)
        for side in range(2):
            for pair in range(sz.half):
                out[side, pair, 1:2, sz.chunk :] = row
        keep[...] = out[core]
        give[...] = out[1 - core]
        fin_keep[...] = jnp.zeros_like(fin_keep)
        fin_give[...] = jnp.zeros_like(fin_give)
        fin_keep[:, 0:2, :] = out[core]
        fin_give[:, 0:2, :] = out[1 - core]

    @pl.when(group != 0)
    def _():
        total = sz.held * sz.pieces
        for i in range(min(RING, total)):
            copy(i).start()
        for b in range(sz.held):

            def body(i, _):
                index = b * sz.pieces + i
                slot = index % RING
                copy(index).wait()
                high, low = split(ring[slot])
                column = pl.multiple_of(i * sz.piece, sz.piece)
                highs[b][:, pl.ds(column, sz.piece)] = high
                lows[b][:, pl.ds(column, sz.piece)] = low

                @pl.when(index + RING < total)
                def _():
                    copy(index + RING).start()

                return 0

            lax.fori_loop(0, sz.pieces, body, 0)
        keep[...] = jnp.zeros_like(keep)
        give[...] = jnp.zeros_like(give)
        fin_keep[...] = jnp.zeros_like(fin_keep)
        fin_give[...] = jnp.zeros_like(fin_give)


def place_norms(sz, env, level):
    norms = jnp.sum(env * env, axis=1, keepdims=True)
    shape = (env.shape[0], sz.extra)
    lane = lax.broadcasted_iota(jnp.int32, shape, 1)
    row = lax.broadcasted_iota(jnp.int32, shape, 0)
    first = 2 * lax.shift_left(1, level) - 2
    return jnp.sum(jnp.where(lane == row + first, norms, 0.0), axis=0, keepdims=True)


def site_kernel(sz, step, *refs):
    last = step == sz.segs - 1
    refs = list(refs)
    bits_ref, site = refs[:2]
    messages = refs[2 : 2 + sz.half]
    refs = refs[2 + sz.half :]
    highs, lows = refs[: sz.held], refs[sz.held : 2 * sz.held]
    old_keep, old_give = refs[2 * sz.held : 2 * sz.held + 2]
    refs = refs[2 * sz.held + 2 :]
    if last:
        fin_keep, fin_give = refs[:2]
        refs = refs[2:]
    else:
        keep, give, fin_keep, fin_give = refs[:4]
        refs = refs[4:]
    ring, lhs_ref, out, sems = refs
    group = lax.axis_index("seg")
    bond = lax.axis_index("bond")
    core = bond % 2
    rows = 2**step
    copy = functools.partial(piece_copy, sz, site, ring, sems)

    @pl.when(group == step)
    def _():
        streamed = range(sz.held * sz.pieces, sz.blocks * sz.pieces)
        for i in streamed[:RING]:
            copy(i).start()
        total = messages[0][...]
        for m in messages[1:]:
            total = total + m[...]
        env = total[:, : sz.chunk]
        norms = total[0:1, sz.chunk :]
        taken = total[1:2, sz.chunk :]
        high, low = split(env)
        lhs_ref[...] = jnp.zeros_like(lhs_ref)
        lhs_ref[0:rows, :] = high.astype(F32)
        lhs_ref[rows : 2 * rows, :] = low.astype(F32)
        lhs = lhs_ref[...].astype(BF16)
        out[...] = jnp.zeros_like(out)

        def product(w_high, w_low, bit, column, columns):
            acc = jnp.dot(lhs, w_high, preferred_element_type=F32)
            acc = acc + jnp.dot(lhs, w_low, preferred_element_type=F32)
            amp = acc[0:rows] + acc[rows : 2 * rows]
            size = min(columns, sz.chunk)
            for start in range(0, columns, size):
                pair, side = sz.place(column + start)
                offset = (column + start) % sz.chunk
                out[side, pair, bit * rows : (bit + 1) * rows, offset : offset + size] = amp[
                    :, start : start + size
                ]

        def stream(index):
            copy(index).wait()
            w_high, w_low = split(ring[index % RING])
            per = sz.right // sz.piece
            product(w_high, w_low, index // per, (index % per) * sz.piece, sz.piece)
            if index + RING in streamed:
                copy(index + RING).start()

        waiting = list(streamed)
        share = -(-len(waiting) // max(sz.held, 1))
        for b in range(sz.held):
            bit, column = b // sz.per_bit, (b % sz.per_bit) * sz.block
            product(highs[b][...], lows[b][...], bit, column, sz.block)
            for index in waiting[:share]:
                stream(index)
            waiting = waiting[share:]
        for index in waiting:
            stream(index)

        partial = place_norms(sz, env, step - 1) + jnp.where(bond == 0, norms, 0.0)
        row = jnp.where(bond == 0, bit_row(sz, bits_ref, group, taken), 0.0)
        for side in range(2):
            for pair in range(sz.half):
                out[side, pair, 0:1, sz.chunk :] = partial
                out[side, pair, 1:2, sz.chunk :] = row
        if not last:
            keep[...] = out[core]
            give[...] = out[1 - core]
            fin_keep[...] = jnp.zeros_like(fin_keep)
            fin_give[...] = jnp.zeros_like(fin_give)
        fin_keep[:, 0 : 2 * rows, :] = out[core]
        fin_give[:, 0 : 2 * rows, :] = out[1 - core]

    @pl.when(group != step)
    def _():
        fin_keep[...] = old_keep[...]
        fin_give[...] = old_give[...]


def add_kernel(sz, keep, came, *outs):
    pair = lax.axis_index("bond") // 2
    for t, out in enumerate(outs):
        target = lax.rem(pair + t, sz.half)
        out[...] = keep[target] + came[target]


def norm_kernel(sz, *refs):
    parts, out = refs[:-1], refs[-1]
    bond = lax.axis_index("bond")
    total = parts[0][...]
    for m in parts[1:]:
        total = total + m[...]
    norms = place_norms(sz, total[:, : sz.chunk], lax.axis_index("seg"))
    known = jnp.where(bond == 0, total[0:2, sz.chunk :], 0.0)
    out[0:1, :] = known[0:1] + norms
    out[1:2, :] = known[1:2]


def sum_kernel(left, right, out):
    out[...] = left[...] + right[...]


def final_kernel(sz, order_ref, *refs):
    parts, out = refs[:-1], refs[-1]
    total = parts[0][...]
    for m in parts[1:]:
        total = total + m[...]
    shape = (sz.rows, sz.extra)
    norms = jnp.broadcast_to(total[0:1], shape)
    taken = jnp.broadcast_to(total[1:2], shape)
    lane = lax.broadcasted_iota(jnp.int32, shape, 1)
    row = lax.broadcasted_iota(jnp.int32, shape, 0)
    group = lax.axis_index("seg")
    prefix = jnp.zeros((sz.rows, 1), jnp.int32)
    square = jnp.ones((sz.rows, 1), F32)
    chosen = jnp.zeros((sz.rows, 1), F32)
    for level in range(sz.segs):
        bit = jnp.sum(jnp.where(lane == row + level * sz.rows, taken, 0.0), axis=1, keepdims=True)
        bit = bit.astype(jnp.int32)
        first = 2 * 2**level - 2
        own = first + prefix + bit * 2**level
        other = first + prefix + (1 - bit) * 2**level
        sum_own = jnp.sum(jnp.where(lane == own, norms, 0.0), axis=1, keepdims=True)
        sum_other = jnp.sum(jnp.where(lane == other, norms, 0.0), axis=1, keepdims=True)
        scale = square * sz.right
        mean_own = sum_own / scale + EPSILON
        mean_other = sum_other / scale + EPSILON
        chosen = jnp.where(group == level, mean_own / (mean_own + mean_other), chosen)
        square = square * mean_own
        prefix = prefix + bit * 2**level
    slots = (sz.rows, sz.rows)
    which = lax.broadcasted_iota(jnp.int32, slots, 0) == jnp.broadcast_to(order_ref[...], slots)
    out[...] = jnp.sum(jnp.where(which, chosen, 0.0), axis=0, keepdims=True)


def shape_of(*dims, dtype=F32):
    return jax.ShapeDtypeStruct(dims, dtype)


def params(limit):
    return pltpu.CompilerParams(vmem_limit_bytes=limit)


def on_device(sites, boundary, bits, order):
    sz = Sizes(sites, bits)
    site = sites.reshape(sites.shape[1:])
    bits = bits.reshape(1, sz.rows)
    half, bonds = sz.half, sz.bonds

    def swap_cores(x, segs):
        return lax.ppermute(x, AXES, [(k * bonds + j, k * bonds + (j ^ 1)) for k in segs for j in range(bonds)])

    def to_pair(x, t, segs, ahead):
        pairs = [
            (k * bonds + j, (k + ahead) * bonds + ((j // 2 + t) % half) * 2 + j % 2)
            for k in segs
            for j in range(bonds)
        ]
        return lax.ppermute(x, AXES, pairs)

    def add(keep, came):
        rows = keep.shape[1]
        return pl.pallas_call(
            functools.partial(add_kernel, sz),
            out_shape=tuple(shape_of(rows, sz.width) for _ in range(half)),
            in_specs=[VMEM, VMEM],
            out_specs=(VMEM,) * half,
            compiler_params=params(MIB),
            name="add_pair",
        )(keep, came)

    part = (sz.left, sz.block)
    fins = (shape_of(half, sz.most, sz.width),) * 2
    ring = pltpu.VMEM((RING, sz.left, sz.piece), F32)
    sems = pltpu.SemaphoreType.DMA((RING,))
    outs = pl.pallas_call(
        functools.partial(first_kernel, sz),
        out_shape=(shape_of(half, 2, sz.width),) * 2 + fins + (pltpu.VMEM(part, BF16),) * (2 * sz.held),
        in_specs=[VMEM, VMEM, ANY],
        out_specs=(VMEM,) * (4 + 2 * sz.held),
        scratch_shapes=[
            ring,
            pltpu.VMEM((sz.left, LANES), F32),
            pltpu.VMEM((2, half, 2, sz.width), F32),
            sems,
        ],
        compiler_params=params(SCOPE),
        name="first_site",
    )(bits, boundary.reshape(1, sz.left), site)
    keep, give, *fin = outs[:4]
    held = [pltpu.with_memory_space_constraint(x, pltpu.VMEM) for x in outs[4:]]

    for step in range(1, sz.segs):
        sums = add(keep, swap_cores(give, [step - 1]))
        messages = [to_pair(x, t, [step - 1], 1) for t, x in enumerate(sums)]
        rows = 2**step
        last = step == sz.segs - 1
        shapes = fins if last else (shape_of(half, 2 * rows, sz.width),) * 2 + fins
        given = 2 + half + 2 * sz.held
        outs = pl.pallas_call(
            functools.partial(site_kernel, sz, step),
            out_shape=shapes,
            in_specs=[VMEM, ANY] + [VMEM] * (half + 2 * sz.held + 2),
            out_specs=(VMEM,) * len(shapes),
            input_output_aliases={given: len(shapes) - 2, given + 1: len(shapes) - 1},
            scratch_shapes=[
                ring,
                pltpu.VMEM((max(16, 2 * rows), sz.left), F32),
                pltpu.VMEM((2, half, 2 * rows, sz.width), F32),
                sems,
            ],
            compiler_params=params(SCOPE),
            name="site_" + str(step),
        )(bits, site, *messages, *held, *fin)
        fin = outs[-2:]
        if not last:
            keep, give = outs[:2]

    every = range(sz.segs)
    sums = add(fin[0], swap_cores(fin[1], every))
    parts = [sums[0]] + [to_pair(sums[t], t, every, 0) for t in range(1, half)]
    tail = pl.pallas_call(
        functools.partial(norm_kernel, sz),
        out_shape=shape_of(2, sz.extra),
        in_specs=[VMEM] * half,
        out_specs=VMEM,
        compiler_params=params(2 * MIB),
        name="norms",
    )(*parts)
    tail = pl.pallas_call(
        sum_kernel,
        out_shape=shape_of(2, sz.extra),
        in_specs=[VMEM] * 2,
        out_specs=VMEM,
        compiler_params=params(MIB),
        name="norms_pair",
    )(tail, swap_cores(tail, every))
    parts = [tail] + [to_pair(tail, t, every, 0) for t in range(1, half)]
    probs = pl.pallas_call(
        functools.partial(final_kernel, sz),
        out_shape=shape_of(1, sz.rows),
        in_specs=[VMEM] * (1 + half),
        out_specs=VMEM,
        compiler_params=params(MIB),
        name="probs",
    )(order.reshape(1, sz.rows), *parts)
    return probs.reshape(sz.rows, 1)


def solution(mesh):
    return jax.shard_map(
        on_device,
        mesh=mesh,
        in_specs=(P("seg", None, "bond", None), P("bond"), P(None, "seg"), P()),
        out_specs=P(None, "seg"),
        check_vma=False,
    )
```

time: 432 us -> 129 us (0.30)
  matrix products: 180 us -> 0 us
  waiting for transfers between devices: 162 us -> 65.4 us
  blocking collectives: 58.3 us -> 0 us
  Pallas kernels: 0 us -> 36.8 us
  starting transfers between devices: 5.22 us -> 20.1 us
  between operations: 13.1 us -> 0.37 us
  other arithmetic: 9.98 us -> 0 us
    dot_general x4 -> x0, matrix products: 180 us -> none  [advance(): jnp.einsum('slr,lm->rsm', site_piece, env_cols, precision=lax.Precision.H...]
    reduce_scatter x4 -> x0, waiting for transfers between devices: 139 us -> none  [advance(): lax.psum_scatter(term.reshape(lax.axis_size('bond') * site_piece.shape[1]...]
    psum x4 -> x0, blocking collectives: 58.3 us -> none  [advance(): totals = lax.psum(local_sq, 'bond')]
    ppermute x4 -> x23, waiting for transfers between devices: 22.2 us -> 65.4 us  [the longest x18 62.5 us: to_pair(): return lax.ppermute(x, AXES, pairs)]
    pallas_call x0 -> x11, Pallas kernels: none -> 36.8 us  [the longest x3 18.2 us: on_device(): pl.pallas_call(functools.partial(site_kernel, sz, step), out_shape=shapes...]
    ppermute x4 -> x23, starting transfers between devices: 5.17 us -> 20.1 us  [the longest x18 18 us: to_pair(): return lax.ppermute(x, AXES, pairs)]
    unnamed x4 -> x34, local copies, waits for them, and re-layouts: 0.51 us -> 5.3 us
  transfers between devices with their start and end apart: 8 -> 23, of which waited for: 8 -> 11; matrix products, arithmetic and copies ran while one was open for 0% -> 0% of each run, Pallas kernels for 0% -> 0%
where the time goes in v1:
time: 129 us; the launch traced here: 128 us
  waiting for transfers between devices  65.4 us (51%)
  Pallas kernels  36.8 us (29%)
  starting transfers between devices  20.1 us (16%)
  local copies, waits for them, and re-layouts  5.3 us (4%)
    ppermute x18, waiting for transfers between devices, to_pair(): return lax.ppermute(x, AXES, pairs)  62.5 us
    pallas_call x3, Pallas kernels, on_device(): pl.pallas_call(functools.partial(site_kernel, sz, step), out_shape=shapes...  18.2 us
    ppermute x18, starting transfers between devices, to_pair(): return lax.ppermute(x, AXES, pairs)  18 us
    pallas_call x1, Pallas kernels, on_device(): pl.pallas_call(functools.partial(first_kernel, sz), out_shape=(shape_of(h...  17.7 us
    unnamed x34, local copies, waits for them, and re-layouts  5.3 us
    ppermute x5, waiting for transfers between devices, swap_cores(): lax.ppermute(x, AXES, [(k * bonds + j, k * bonds + (j ^ 1)) for k in segs...  2.92 us
  transfers between devices with their start and end apart: 23, of which 11 were waited for; matrix products, arithmetic and copies ran while one was open for 0% of the time, Pallas kernels for 0%

profile of v1, /device:TPU:6, one launch (start us, length us, event | category | flops | bytes accessed | tf_op | source)
XLA Modules:
  0.0 128.0 jit_solution(12446909157801757303)
XLA Ops:
  0.0 17.7 %first_site.1 = (f32[4,2,1152]{2,1,0:T(2,128)}, f32[4,2,1152]{2,1,0:T(2,128)}, f32[4,16,1152]{2,1,0:T(8,128)}, f32[4,16,1152]{2,1,0:T(8,128)}, bf16[1024,2048]{1...) custom-call(s32[1,32]{1,0:T(1,128)} %bitcast.6, ...), custom_call_target="tpu_custom_call" | custom-call | tf_op jit(solution)/shard_map/first_site/pallas_call | solution.py:350
  17.7 0.7 collective-permute-start
  18.4 0.0 collective-permute-done.came
  18.4 0.8 copy-done.3
  19.2 0.7 collective-permute-start.1
  19.9 0.7 collective-permute-start.2
  20.6 0.7 collective-permute-start.3
  21.2 0.7 collective-permute-start.4
  21.9 0.0 collective-permute-done.1.refs_2_
  21.9 0.0 collective-permute-done.2.refs_3_
  21.9 0.0 collective-permute-done.3.refs_4_
  22.0 0.0 collective-permute-done.4.refs_5_
  22.0 0.5 copy-done.13
  22.5 0.0 copy-done.14
  22.5 0.0 copy-done.15
  22.5 0.0 copy-done.16
  22.6 2.2 %site_1.1 = (f32[4,4,1152]{2,1,0:T(4,128)}, f32[4,4,1152]{2,1,0:T(4,128)}, f32[4,16,1152]{2,1,0:T(8,128)}, f32[4,16,1152]{2,1,0:T(8,128)}) custom-call(s32[1,32]{1,0:T(1,128)} %bitcast.7, f32[2,1024,8192]{2,1,0:T(8,128)} %bitcast.2.site.refs_1_, f32[2,1152]{1,0:T(2,128)} %copy-done.13, ...), custom_call_target="tpu_custom_call", output_to_operand_aliasing={{2}: (18, {}), {3}: (19, {})} | custom-call | tf_op jit(solution)/shard_map/site_1/pallas_call | solution.py:374
  24.8 0.7 collective-permute-start.5
  25.4 0.0 collective-permute-done.5.came
  25.5 0.9 copy-done.2
  26.4 0.7 collective-permute-start.6
  27.0 0.7 collective-permute-start.7
  27.7 0.7 collective-permute-start.8
  28.4 0.7 collective-permute-start.9
  29.0 0.0 collective-permute-done.6.refs_2_
  29.1 0.0 collective-permute-done.7.refs_3_
  29.1 0.0 collective-permute-done.8.refs_4_
  29.1 0.0 collective-permute-done.9.refs_5_
  29.1 0.5 copy-done.9
  29.7 0.0 copy-done.10
  29.7 0.0 copy-done.11
  29.7 0.0 copy-done.12
  29.7 2.1 %site_2.1 = (f32[4,8,1152]{2,1,0:T(8,128)}, f32[4,8,1152]{2,1,0:T(8,128)}, f32[4,16,1152]{2,1,0:T(8,128)}, f32[4,16,1152]{2,1,0:T(8,128)}) custom-call(s32[1,32]{1,0:T(1,128)} %bitcast.8, f32[2,1024,8192]{2,1,0:T(8,128)} %bitcast.2.site.refs_1_, f32[4,1152]{1,0:T(4,128)} %copy-done.9, ...), custom_call_target="tpu_custom_call", output_to_operand_aliasing={{2}: (18, {}), {3}: (19, {})} | custom-call | tf_op jit(solution)/shard_map/site_2/pallas_call | solution.py:374
  31.8 0.7 collective-permute-start.10
  32.5 0.0 collective-permute-done.10.came
  32.5 0.9 copy-done.1
  33.4 1.3 %collective-permute-start.11 = (f32[8,1152]{1,0:T(8,128)S(1)}, f32[8,1152]{1,0:T(8,128)S(1)}, u32[]{:S(2)}, u32[]{:S(2)}) collective-permute-start(f32[8,1152]{1,0:T(8,128)S(1)} %get-tuple-element.77), channel_id=1, source_target_pairs={{16,24},{17,25},{18,26},{19,27},{20,28},{21,29},{22,30},{23,31}} | collective-permute-start | bytes 110600 | tf_op jit(solution)/shard_map/ppermute | solution.py:333
  34.7 1.3 %collective-permute-start.12 = (f32[8,1152]{1,0:T(8,128)S(1)}, f32[8,1152]{1,0:T(8,128)S(1)}, u32[]{:S(2)}, u32[]{:S(2)}) collective-permute-start(f32[8,1152]{1,0:T(8,128)S(1)} %get-tuple-element.78), channel_id=1, source_target_pairs={{16,26},{17,27},{18,28},{19,29},{20,30},{21,31},{22,24},{23,25}} | collective-permute-start | bytes 110600 | tf_op jit(solution)/shard_map/ppermute | solution.py:333
  36.0 1.3 %collective-permute-start.13 = (f32[8,1152]{1,0:T(8,128)S(1)}, f32[8,1152]{1,0:T(8,128)S(1)}, u32[]{:S(2)}, u32[]{:S(2)}) collective-permute-start(f32[8,1152]{1,0:T(8,128)S(1)} %get-tuple-element.79), channel_id=1, source_target_pairs={{16,28},{17,29},{18,30},{19,31},{20,24},{21,25},{22,26},{23,27}} | collective-permute-start | bytes 110600 | tf_op jit(solution)/shard_map/ppermute | solution.py:333
  37.3 1.3 %collective-permute-start.14 = (f32[8,1152]{1,0:T(8,128)S(1)}, f32[8,1152]{1,0:T(8,128)S(1)}, u32[]{:S(2)}, u32[]{:S(2)}) collective-permute-start(f32[8,1152]{1,0:T(8,128)S(1)} %get-tuple-element.80), channel_id=1, source_target_pairs={{16,30},{17,31},{18,24},{19,25},{20,26},{21,27},{22,28},{23,29}} | collective-permute-start | bytes 110600 | tf_op jit(solution)/shard_map/ppermute | solution.py:333
  38.6 47.6 %collective-permute-done.11.refs_2_ = f32[8,1152]{1,0:T(8,128)S(1)} collective-permute-done((f32[8,1152]{1,0:T(8,128)S(1)}, f32[8,1152]{1,0:T(8,128)S(1)}, u32[]{:S(2)}, u32[]{:S(2)}) %collective-permute-start.11) | collective-permute-done | bytes 36896 | tf_op jit(solution)/shard_map/ppermute | solution.py:333
  86.2 3.0 %collective-permute-done.12.refs_3_ = f32[8,1152]{1,0:T(8,128)S(1)} collective-permute-done((f32[8,1152]{1,0:T(8,128)S(1)}, f32[8,1152]{1,0:T(8,128)S(1)}, u32[]{:S(2)}, u32[]{:S(2)}) %collective-permute-start.12) | collective-permute-done | bytes 36896 | tf_op jit(solution)/shard_map/ppermute | solution.py:333
  89.2 0.2 collective-permute-done.13.refs_4_
  89.4 1.7 %collective-permute-done.14.refs_5_ = f32[8,1152]{1,0:T(8,128)S(1)} collective-permute-done((f32[8,1152]{1,0:T(8,128)S(1)}, f32[8,1152]{1,0:T(8,128)S(1)}, u32[]{:S(2)}, u32[]{:S(2)}) %collective-permute-start.14) | collective-permute-done | bytes 36896 | tf_op jit(solution)/shard_map/ppermute | solution.py:333
  91.1 0.6 copy-done.8
  91.7 13.9 %site_3.1 = (f32[4,16,1152]{2,1,0:T(8,128)}, f32[4,16,1152]{2,1,0:T(8,128)}) custom-call(s32[1,32]{1,0:T(1,128)} %bitcast.9, f32[2,1024,8192]{2,1,0:T(8,128)} %bitcast.2.site.refs_1_, f32[8,1152]{1,0:T(8,128)} %copy-done.5, f32[8,1152]{1,0:T(8,128)} %copy-done.6, f32[8,1152]{1,0:T(8,128)} %copy-done.7, ...), custom_call_target="tpu_custom_call", output_to_operand_aliasing={{0}: (18, {}), {1}: (19, {})} | custom-call | tf_op jit(solution)/shard_map/site_3/pallas_call | solution.py:374
  105.6 0.1 collective-permute-start.15
  105.7 1.8 %collective-permute-done.15.came = f32[4,16,1152]{2,1,0:T(8,128)S(1)} collective-permute-done((f32[4,16,1152]{2,1,0:T(8,128)}, f32[4,16,1152]{2,1,0:T(8,128)S(1)}, u32[]{:S(2)}, u32[]{:S(2)}) %collective-permute-start.15) | collective-permute-done | bytes 294944 | tf_op jit(solution)/shard_map/ppermute | solution.py:325
  107.5 1.0 copy-done
  108.5 0.4 collective-permute-start.16
  108.8 2.7 %collective-permute-start.17 = (f32[16,1152]{1,0:T(8,128)S(1)}, f32[16,1152]{1,0:T(8,128)S(1)}, u32[]{:S(2)}, u32[]{:S(2)}) collective-permute-start(f32[16,1152]{1,0:T(8,128)S(1)} %get-tuple-element.87), channel_id=1, source_target_pairs={{0,4},{1,5},{2,6},{3,7},{4,0},{5,1},{6,2},{7,3},{8,12},{9,13},{10,... | collective-permute-start | bytes 221192 | tf_op jit(solution)/shard_map/ppermute | solution.py:333
  111.5 1.2 collective-permute-start.18
  112.7 2.8 %collective-permute-done.16.refs_1_ = f32[16,1152]{1,0:T(8,128)S(1)} collective-permute-done((f32[16,1152]{1,0:T(8,128)S(1)}, f32[16,1152]{1,0:T(8,128)S(1)}, u32[]{:S(2)}, u32[]{:S(2)}) %collective-permute-start.16) | collective-permute-done | bytes 73760 | tf_op jit(solution)/shard_map/ppermute | solution.py:333
  115.5 2.2 %collective-permute-done.17.refs_2_ = f32[16,1152]{1,0:T(8,128)S(1)} collective-permute-done((f32[16,1152]{1,0:T(8,128)S(1)}, f32[16,1152]{1,0:T(8,128)S(1)}, u32[]{:S(2)}, u32[]{:S(2)}) %collective-permute-start.17) | collective-permute-done | bytes 73760 | tf_op jit(solution)/shard_map/ppermute | solution.py:333
  117.7 0.0 collective-permute-done.18.refs_3_
  117.7 0.1 norms.1.left
  117.8 1.1 collective-permute-done.19.right
  119.0 2.7 %collective-permute-start.22 = (f32[2,128]{1,0:T(2,128)S(1)}, f32[2,128]{1,0:T(2,128)S(1)}, u32[]{:S(2)}, u32[]{:S(2)}) collective-permute-start(f32[2,128]{1,0:T(2,128)S(1)} %norms_pair.1.refs_0_), channel_id=1, source_target_pairs={{0,6},{1,7},{2,0},{3,1},{4,2},{5,3},{6,4},{7,5},{8,14},{9,15},{10,... | collective-permute-start | bytes 3080 | tf_op jit(solution)/shard_map/ppermute | solution.py:333
  121.7 0.2 collective-permute-start.21
  121.9 0.4 collective-permute-start.20
  122.3 0.7 collective-permute-done.22.refs_3_
  123.0 3.2 %collective-permute-done.21.refs_2_ = f32[2,128]{1,0:T(2,128)S(1)} collective-permute-done((f32[2,128]{1,0:T(2,128)S(1)}, f32[2,128]{1,0:T(2,128)S(1)}, u32[]{:S(2)}, u32[]{:S(2)}) %collective-permute-start.21) | collective-permute-done | bytes 1056 | tf_op jit(solution)/shard_map/ppermute | solution.py:333
  126.2 1.1 collective-permute-done.20.refs_1_
  127.2 0.7 probs.1
  (27 shorter events, 0.1 us)
Async XLA Ops:
  17.7 0.7 collective-permute-start
  18.4 0.8 copy-start.3
  19.2 2.7 %collective-permute-start.1 = (f32[2,1152]{1,0:T(2,128)S(1)}, f32[2,1152]{1,0:T(2,128)S(1)}, u32[]{:S(2)}, u32[]{:S(2)}) collective-permute-start(f32[2,1152]{1,0:T(2,128)S(1)} %get-tuple-element.49), channel_id=1, source_target_pairs={{0,8},{1,9},{2,10},{3,11},{4,12},{5,13},{6,14},{7,15}} | collective-permute-start | bytes 27656 | tf_op jit(solution)/shard_map/ppermute | solution.py:333
  19.9 2.0 %collective-permute-start.2 = (f32[2,1152]{1,0:T(2,128)S(1)}, f32[2,1152]{1,0:T(2,128)S(1)}, u32[]{:S(2)}, u32[]{:S(2)}) collective-permute-start(f32[2,1152]{1,0:T(2,128)S(1)} %get-tuple-element.50), channel_id=1, source_target_pairs={{0,10},{1,11},{2,12},{3,13},{4,14},{5,15},{6,8},{7,9}} | collective-permute-start | bytes 27656 | tf_op jit(solution)/shard_map/ppermute | solution.py:333
  20.6 1.4 %collective-permute-start.3 = (f32[2,1152]{1,0:T(2,128)S(1)}, f32[2,1152]{1,0:T(2,128)S(1)}, u32[]{:S(2)}, u32[]{:S(2)}) collective-permute-start(f32[2,1152]{1,0:T(2,128)S(1)} %get-tuple-element.51), channel_id=1, source_target_pairs={{0,12},{1,13},{2,14},{3,15},{4,8},{5,9},{6,10},{7,11}} | collective-permute-start | bytes 27656 | tf_op jit(solution)/shard_map/ppermute | solution.py:333
  21.2 0.7 collective-permute-start.4
  21.9 0.6 copy-start.13
  21.9 0.6 copy-start.14
  21.9 0.6 copy-start.15
  22.0 0.6 copy-start.16
  24.8 0.7 collective-permute-start.5
  25.5 0.9 copy-start.2
  26.4 2.7 %collective-permute-start.6 = (f32[4,1152]{1,0:T(4,128)S(1)}, f32[4,1152]{1,0:T(4,128)S(1)}, u32[]{:S(2)}, u32[]{:S(2)}) collective-permute-start(f32[4,1152]{1,0:T(4,128)S(1)} %get-tuple-element.69), channel_id=1, source_target_pairs={{8,16},{9,17},{10,18},{11,19},{12,20},{13,21},{14,22},{15,23}} | collective-permute-start | bytes 55304 | tf_op jit(solution)/shard_map/ppermute | solution.py:333
  27.0 2.0 %collective-permute-start.7 = (f32[4,1152]{1,0:T(4,128)S(1)}, f32[4,1152]{1,0:T(4,128)S(1)}, u32[]{:S(2)}, u32[]{:S(2)}) collective-permute-start(f32[4,1152]{1,0:T(4,128)S(1)} %get-tuple-element.70), channel_id=1, source_target_pairs={{8,18},{9,19},{10,20},{11,21},{12,22},{13,23},{14,16},{15,17}} | collective-permute-start | bytes 55304 | tf_op jit(solution)/shard_map/ppermute | solution.py:333
  27.7 1.4 %collective-permute-start.8 = (f32[4,1152]{1,0:T(4,128)S(1)}, f32[4,1152]{1,0:T(4,128)S(1)}, u32[]{:S(2)}, u32[]{:S(2)}) collective-permute-start(f32[4,1152]{1,0:T(4,128)S(1)} %get-tuple-element.71), channel_id=1, source_target_pairs={{8,20},{9,21},{10,22},{11,23},{12,16},{13,17},{14,18},{15,19}} | collective-permute-start | bytes 55304 | tf_op jit(solution)/shard_map/ppermute | solution.py:333
  28.4 0.7 collective-permute-start.9
  29.1 0.6 copy-start.9
  29.1 0.6 copy-start.10
  29.1 0.6 copy-start.11
  29.1 0.6 copy-start.12
  31.8 0.7 collective-permute-start.10
  32.5 0.9 copy-start.1
  33.4 52.8 %collective-permute-start.11 = (f32[8,1152]{1,0:T(8,128)S(1)}, f32[8,1152]{1,0:T(8,128)S(1)}, u32[]{:S(2)}, u32[]{:S(2)}) collective-permute-start(f32[8,1152]{1,0:T(8,128)S(1)} %get-tuple-element.77), channel_id=1, source_target_pairs={{16,24},{17,25},{18,26},{19,27},{20,28},{21,29},{22,30},{23,31}} | collective-permute-start | bytes 110600 | tf_op jit(solution)/shard_map/ppermute | solution.py:333
  34.7 54.5 %collective-permute-start.12 = (f32[8,1152]{1,0:T(8,128)S(1)}, f32[8,1152]{1,0:T(8,128)S(1)}, u32[]{:S(2)}, u32[]{:S(2)}) collective-permute-start(f32[8,1152]{1,0:T(8,128)S(1)} %get-tuple-element.78), channel_id=1, source_target_pairs={{16,26},{17,27},{18,28},{19,29},{20,30},{21,31},{22,24},{23,25}} | collective-permute-start | bytes 110600 | tf_op jit(solution)/shard_map/ppermute | solution.py:333
  36.0 53.3 %collective-permute-start.13 = (f32[8,1152]{1,0:T(8,128)S(1)}, f32[8,1152]{1,0:T(8,128)S(1)}, u32[]{:S(2)}, u32[]{:S(2)}) collective-permute-start(f32[8,1152]{1,0:T(8,128)S(1)} %get-tuple-element.79), channel_id=1, source_target_pairs={{16,28},{17,29},{18,30},{19,31},{20,24},{21,25},{22,26},{23,27}} | collective-permute-start | bytes 110600 | tf_op jit(solution)/shard_map/ppermute | solution.py:333
  37.3 53.8 %collective-permute-start.14 = (f32[8,1152]{1,0:T(8,128)S(1)}, f32[8,1152]{1,0:T(8,128)S(1)}, u32[]{:S(2)}, u32[]{:S(2)}) collective-permute-start(f32[8,1152]{1,0:T(8,128)S(1)} %get-tuple-element.80), channel_id=1, source_target_pairs={{16,30},{17,31},{18,24},{19,25},{20,26},{21,27},{22,28},{23,29}} | collective-permute-start | bytes 110600 | tf_op jit(solution)/shard_map/ppermute | solution.py:333
  86.2 4.9 %copy-start.5 = (f32[8,1152]{1,0:T(8,128)}, f32[8,1152]{1,0:T(8,128)S(1)}, u32[]{:S(2)}) copy-start(f32[8,1152]{1,0:T(8,128)S(1)} %collective-permute-done.11.refs_2_) | copy-start | bytes 110596
  89.2 1.9 %copy-start.6 = (f32[8,1152]{1,0:T(8,128)}, f32[8,1152]{1,0:T(8,128)S(1)}, u32[]{:S(2)}) copy-start(f32[8,1152]{1,0:T(8,128)S(1)} %collective-permute-done.12.refs_3_) | copy-start | bytes 110596
  89.4 1.8 %copy-start.7 = (f32[8,1152]{1,0:T(8,128)}, f32[8,1152]{1,0:T(8,128)S(1)}, u32[]{:S(2)}) copy-start(f32[8,1152]{1,0:T(8,128)S(1)} %collective-permute-done.13.refs_4_) | copy-start | bytes 110596
  91.1 0.6 copy-start.8
  91.7 35.5 %copy-start.4 = (s32[32]{0:T(128)S(1)}, s32[32]{0:T(128)}, u32[]{:S(2)}) copy-start(s32[32]{0:T(128)} %param.7) | copy-start | bytes 388
  105.6 1.9 %collective-permute-start.15 = (f32[4,16,1152]{2,1,0:T(8,128)}, f32[4,16,1152]{2,1,0:T(8,128)S(1)}, u32[]{:S(2)}, u32[]{:S(2)}) collective-permute-start(f32[4,16,1152]{2,1,0:T(8,128)} %get-tuple-element.84), channel_id=1, source_target_pairs={{0,1},{1,0},{2,3},{3,2},{4,5},{5,4},{6,7},{7,6},{8,9},{9,8},{10,11... | collective-permute-start | bytes 884744 | tf_op jit(solution)/shard_map/ppermute | solution.py:325
  107.5 1.0 copy-start
  108.5 7.0 %collective-permute-start.16 = (f32[16,1152]{1,0:T(8,128)S(1)}, f32[16,1152]{1,0:T(8,128)S(1)}, u32[]{:S(2)}, u32[]{:S(2)}) collective-permute-start(f32[16,1152]{1,0:T(8,128)S(1)} %get-tuple-element.86), channel_id=1, source_target_pairs={{0,2},{1,3},{2,4},{3,5},{4,6},{5,7},{6,0},{7,1},{8,10},{9,11},{10,... | collective-permute-start | bytes 221192 | tf_op jit(solution)/shard_map/ppermute | solution.py:333
  108.8 8.9 %collective-permute-start.17 = (f32[16,1152]{1,0:T(8,128)S(1)}, f32[16,1152]{1,0:T(8,128)S(1)}, u32[]{:S(2)}, u32[]{:S(2)}) collective-permute-start(f32[16,1152]{1,0:T(8,128)S(1)} %get-tuple-element.87), channel_id=1, source_target_pairs={{0,4},{1,5},{2,6},{3,7},{4,0},{5,1},{6,2},{7,3},{8,12},{9,13},{10,... | collective-permute-start | bytes 221192 | tf_op jit(solution)/shard_map/ppermute | solution.py:333
  111.5 6.2 %collective-permute-start.18 = (f32[16,1152]{1,0:T(8,128)S(1)}, f32[16,1152]{1,0:T(8,128)S(1)}, u32[]{:S(2)}, u32[]{:S(2)}) collective-permute-start(f32[16,1152]{1,0:T(8,128)S(1)} %get-tuple-element.88), channel_id=1, source_target_pairs={{0,6},{1,7},{2,0},{3,1},{4,2},{5,3},{6,4},{7,5},{8,14},{9,15},{10,... | collective-permute-start | bytes 221192 | tf_op jit(solution)/shard_map/ppermute | solution.py:333
  117.8 1.1 collective-permute-start.19
  119.0 4.0 %collective-permute-start.22 = (f32[2,128]{1,0:T(2,128)S(1)}, f32[2,128]{1,0:T(2,128)S(1)}, u32[]{:S(2)}, u32[]{:S(2)}) collective-permute-start(f32[2,128]{1,0:T(2,128)S(1)} %norms_pair.1.refs_0_), channel_id=1, source_target_pairs={{0,6},{1,7},{2,0},{3,1},{4,2},{5,3},{6,4},{7,5},{8,14},{9,15},{10,... | collective-permute-start | bytes 3080 | tf_op jit(solution)/shard_map/ppermute | solution.py:333
  121.7 4.5 %collective-permute-start.21 = (f32[2,128]{1,0:T(2,128)S(1)}, f32[2,128]{1,0:T(2,128)S(1)}, u32[]{:S(2)}, u32[]{:S(2)}) collective-permute-start(f32[2,128]{1,0:T(2,128)S(1)} %norms_pair.1.refs_0_), channel_id=1, source_target_pairs={{0,4},{1,5},{2,6},{3,7},{4,0},{5,1},{6,2},{7,3},{8,12},{9,13},{10,... | collective-permute-start | bytes 3080 | tf_op jit(solution)/shard_map/ppermute | solution.py:333
  121.9 5.4 %collective-permute-start.20 = (f32[2,128]{1,0:T(2,128)S(1)}, f32[2,128]{1,0:T(2,128)S(1)}, u32[]{:S(2)}, u32[]{:S(2)}) collective-permute-start(f32[2,128]{1,0:T(2,128)S(1)} %norms_pair.1.refs_0_), channel_id=1, source_target_pairs={{0,2},{1,3},{2,4},{3,5},{4,6},{5,7},{6,0},{7,1},{8,10},{9,11},{10,... | collective-permute-start | bytes 3080 | tf_op jit(solution)/shard_map/ppermute | solution.py:333

commit v2 on v1

--- a/solution.py
+++ b/solution.py
@@ -11,12 +11,15 @@
 AXES = ("seg", "bond")
 LANES = 128
 MIB = 2**20
-HELD_BYTES = 48 * MIB
 BLOCK = 2048
 RING = 4
-SCOPE = 12 * MIB
+RINGS = (1, 2)
+SCOPE = 43 * MIB // 4
 F32 = jnp.float32
 BF16 = jnp.bfloat16
+F8 = jnp.float8_e4m3fn
+TOP = 256.0
+TINY = 1e-30
 VMEM = pl.BlockSpec(memory_space=pltpu.VMEM)
 ANY = pl.BlockSpec(memory_space=pl.ANY)
 
@@ -37,8 +40,8 @@
         self.width = self.chunk + self.extra
         self.block = min(BLOCK, self.right)
         self.per_bit = self.right // self.block
-        self.blocks = 2 * self.per_bit
-        self.held = min(self.blocks, HELD_BYTES // (self.left * self.block * 4))
+        self.held = 2 * self.per_bit
+        self.packs = self.held // 2
         self.piece = min(512, self.chunk)
         self.pieces = self.block // self.piece
 
@@ -49,7 +52,7 @@
 
 def split(x):
     high = x.astype(BF16)
-    return high, (x - high.astype(F32)).astype(BF16)
+    return high, x - high.astype(F32)
 
 
 def piece_copy(sz, site, ring, sems, index):
@@ -68,9 +71,13 @@
     return extra + jnp.where(lane // sz.rows == group, wide, 0.0)
 
 
-def first_kernel(sz, bits_ref, start_ref, site, keep, give, fin_keep, fin_give, *rest):
-    highs, lows = rest[: sz.held], rest[sz.held : 2 * sz.held]
-    ring, spread, out, sems = rest[2 * sz.held :]
+def first_kernel(
+    sz, bits_ref, order_ref, start_ref, site, keep, give, fin_keep, fin_give, bits_out, order_out, scales, *rest
+):
+    bits_out[...] = bits_ref[...]
+    order_out[...] = order_ref[...]
+    highs, lows = rest[: sz.held], rest[sz.held : sz.held + sz.packs]
+    ring, spread, out, sems = rest[sz.held + sz.packs :]
     group = lax.axis_index("seg")
     bond = lax.axis_index("bond")
     core = bond % 2
@@ -133,10 +140,15 @@
                 index = b * sz.pieces + i
                 slot = index % RING
                 copy(index).wait()
-                high, low = split(ring[slot])
+                x = ring[slot]
+                high, low = split(x)
                 column = pl.multiple_of(i * sz.piece, sz.piece)
                 highs[b][:, pl.ds(column, sz.piece)] = high
-                lows[b][:, pl.ds(column, sz.piece)] = low
+                most = jnp.max(jnp.max(jnp.abs(x), axis=0, keepdims=True), axis=1, keepdims=True)
+                most = jnp.maximum(most, TINY)
+                column = pl.multiple_of(b % 2 * sz.block + i * sz.piece, sz.piece)
+                lows[b // 2][:, pl.ds(column, sz.piece)] = (low * (TOP * TOP / most)).astype(F8)
+                scales[pl.ds(index, 1), :] = jnp.broadcast_to(most / (TOP * TOP), (1, LANES))
 
                 @pl.when(index + RING < total)
                 def _():
@@ -163,30 +175,26 @@
 def site_kernel(sz, step, *refs):
     last = step == sz.segs - 1
     refs = list(refs)
-    bits_ref, site = refs[:2]
+    bits_ref, scales = refs[:2]
     messages = refs[2 : 2 + sz.half]
     refs = refs[2 + sz.half :]
-    highs, lows = refs[: sz.held], refs[sz.held : 2 * sz.held]
-    old_keep, old_give = refs[2 * sz.held : 2 * sz.held + 2]
-    refs = refs[2 * sz.held + 2 :]
+    highs, lows = refs[: sz.held], refs[sz.held : sz.held + sz.packs]
+    old_keep, old_give = refs[sz.held + sz.packs : sz.held + sz.packs + 2]
+    refs = refs[sz.held + sz.packs + 2 :]
     if last:
         fin_keep, fin_give = refs[:2]
         refs = refs[2:]
     else:
         keep, give, fin_keep, fin_give = refs[:4]
         refs = refs[4:]
-    ring, lhs_ref, out, sems = refs
+    lhs_ref, lhs8_ref, out = refs
     group = lax.axis_index("seg")
     bond = lax.axis_index("bond")
     core = bond % 2
     rows = 2**step
-    copy = functools.partial(piece_copy, sz, site, ring, sems)
 
     @pl.when(group == step)
     def _():
-        streamed = range(sz.held * sz.pieces, sz.blocks * sz.pieces)
-        for i in streamed[:RING]:
-            copy(i).start()
         total = messages[0][...]
         for m in messages[1:]:
             total = total + m[...]
@@ -196,40 +204,34 @@
         high, low = split(env)
         lhs_ref[...] = jnp.zeros_like(lhs_ref)
         lhs_ref[0:rows, :] = high.astype(F32)
-        lhs_ref[rows : 2 * rows, :] = low.astype(F32)
+        lhs_ref[rows : 2 * rows, :] = low
         lhs = lhs_ref[...].astype(BF16)
+        unit = jnp.maximum(jnp.max(jnp.abs(env), axis=1, keepdims=True), TINY) / TOP
+        scaled = env / unit
+        rough = scaled.astype(F8).astype(F32)
+        lhs8_ref[...] = jnp.zeros_like(lhs8_ref)
+        lhs8_ref[0:rows, :] = rough
+        lhs8_ref[rows : 2 * rows, :] = (scaled - rough) * 16.0
+        lhs8 = lhs8_ref[...].astype(F8)
         out[...] = jnp.zeros_like(out)
-
-        def product(w_high, w_low, bit, column, columns):
-            acc = jnp.dot(lhs, w_high, preferred_element_type=F32)
-            acc = acc + jnp.dot(lhs, w_low, preferred_element_type=F32)
-            amp = acc[0:rows] + acc[rows : 2 * rows]
-            size = min(columns, sz.chunk)
-            for start in range(0, columns, size):
-                pair, side = sz.place(column + start)
-                offset = (column + start) % sz.chunk
-                out[side, pair, bit * rows : (bit + 1) * rows, offset : offset + size] = amp[
-                    :, start : start + size
-                ]
-
-        def stream(index):
-            copy(index).wait()
-            w_high, w_low = split(ring[index % RING])
-            per = sz.right // sz.piece
-            product(w_high, w_low, index // per, (index % per) * sz.piece, sz.piece)
-            if index + RING in streamed:
-                copy(index + RING).start()
-
-        waiting = list(streamed)
-        share = -(-len(waiting) // max(sz.held, 1))
+        size = min(sz.piece, sz.block)
         for b in range(sz.held):
-            bit, column = b // sz.per_bit, (b % sz.per_bit) * sz.block
-            product(highs[b][...], lows[b][...], bit, column, sz.block)
-            for index in waiting[:share]:
-                stream(index)
-            waiting = waiting[share:]
-        for index in waiting:
-            stream(index)
+            bit = b // sz.per_bit
+            big = jnp.dot(lhs, highs[b][...], preferred_element_type=F32)
+            low = lows[b // 2][:, b % 2 * sz.block : (b % 2 + 1) * sz.block]
+            small = jnp.dot(lhs8, low, preferred_element_type=F32)
+            big = big[0:rows] + big[rows : 2 * rows]
+            small = (small[0:rows] + small[rows : 2 * rows] * (1.0 / 16.0)) * unit
+            for p in range(sz.pieces):
+                column = (b % sz.per_bit) * sz.block + p * size
+                pair, side = sz.place(column)
+                offset = column % sz.chunk
+                cut = slice(p * size, (p + 1) * size)
+                index = b * sz.pieces + p
+                scale = scales[index : index + 1, 0:1]
+                out[side, pair, bit * rows : (bit + 1) * rows, offset : offset + size] = (
+                    big[:, cut] + small[:, cut] * scale
+                )
 
         partial = place_norms(sz, env, step - 1) + jnp.where(bond == 0, norms, 0.0)
         row = jnp.where(bond == 0, bit_row(sz, bits_ref, group, taken), 0.0)
@@ -311,6 +313,10 @@
     return jax.ShapeDtypeStruct(dims, dtype)
 
 
+def in_vmem(x):
+    return pltpu.with_memory_space_constraint(x, pltpu.VMEM)
+
+
 def params(limit):
     return pltpu.CompilerParams(vmem_limit_bytes=limit)
 
@@ -321,22 +327,33 @@
     bits = bits.reshape(1, sz.rows)
     half, bonds = sz.half, sz.bonds
 
-    def swap_cores(x, segs):
-        return lax.ppermute(x, AXES, [(k * bonds + j, k * bonds + (j ^ 1)) for k in segs for j in range(bonds)])
-
-    def to_pair(x, t, segs, ahead):
-        pairs = [
-            (k * bonds + j, (k + ahead) * bonds + ((j // 2 + t) % half) * 2 + j % 2)
-            for k in segs
-            for j in range(bonds)
-        ]
-        return lax.ppermute(x, AXES, pairs)
+    def permute(x, target):
+        pairs = [(k * bonds + j, target(k, j)) for k in range(sz.segs) for j in range(bonds)]
+        return in_vmem(lax.ppermute(x, AXES, pairs))
+
+    def swap_cores(x):
+        return permute(x, lambda k, j: k * bonds + (j ^ 1))
+
+    def to_pair(x, t):
+        return permute(x, lambda k, j: k * bonds + (j // 2 + t) % half * 2 + j % 2)
+
+    def hand_over(sums, group):
+        alone = [t for t in range(half) if t not in RINGS]
+        came = {}
+        for t in alone + [t for t in RINGS if t < half]:
+            pairs = [
+                (k * bonds + j, (k + 1) % sz.segs * bonds + (j // 2 + t) % half * 2 + j % 2)
+                for k in ([group] if t in alone else range(sz.segs))
+                for j in range(bonds)
+            ]
+            came[t] = in_vmem(lax.ppermute(sums[t], AXES, pairs))
+        return [came[t] for t in range(half)]
 
     def add(keep, came):
         rows = keep.shape[1]
         return pl.pallas_call(
             functools.partial(add_kernel, sz),
-            out_shape=tuple(shape_of(rows, sz.width) for _ in range(half)),
+            out_shape=(pltpu.VMEM((rows, sz.width), F32),) * half,
             in_specs=[VMEM, VMEM],
             out_specs=(VMEM,) * half,
             compiler_params=params(MIB),
@@ -344,14 +361,20 @@
         )(keep, came)
 
     part = (sz.left, sz.block)
-    fins = (shape_of(half, sz.most, sz.width),) * 2
+    fins = (pltpu.VMEM((half, sz.most, sz.width), F32),) * 2
+    small = (pltpu.VMEM((1, sz.rows), jnp.int32),) * 2
     ring = pltpu.VMEM((RING, sz.left, sz.piece), F32)
     sems = pltpu.SemaphoreType.DMA((RING,))
     outs = pl.pallas_call(
         functools.partial(first_kernel, sz),
-        out_shape=(shape_of(half, 2, sz.width),) * 2 + fins + (pltpu.VMEM(part, BF16),) * (2 * sz.held),
-        in_specs=[VMEM, VMEM, ANY],
-        out_specs=(VMEM,) * (4 + 2 * sz.held),
+        out_shape=(pltpu.VMEM((half, 2, sz.width), F32),) * 2
+        + fins
+        + small
+        + (pltpu.VMEM((sz.held * sz.pieces, LANES), F32),)
+        + (pltpu.VMEM(part, BF16),) * sz.held
+        + (pltpu.VMEM((sz.left, 2 * sz.block), F8),) * sz.packs,
+        in_specs=[VMEM, VMEM, VMEM, ANY],
+        out_specs=(VMEM,) * (7 + sz.held + sz.packs),
         scratch_shapes=[
             ring,
             pltpu.VMEM((sz.left, LANES), F32),
@@ -360,42 +383,43 @@
         ],
         compiler_params=params(SCOPE),
         name="first_site",
-    )(bits, boundary.reshape(1, sz.left), site)
+    )(bits, order.reshape(1, sz.rows), boundary.reshape(1, sz.left), site)
+    outs = [in_vmem(x) for x in outs]
     keep, give, *fin = outs[:4]
-    held = [pltpu.with_memory_space_constraint(x, pltpu.VMEM) for x in outs[4:]]
+    bits, order, scales = outs[4:7]
+    held = outs[7:]
 
     for step in range(1, sz.segs):
-        sums = add(keep, swap_cores(give, [step - 1]))
-        messages = [to_pair(x, t, [step - 1], 1) for t, x in enumerate(sums)]
+        sums = add(keep, swap_cores(give))
+        messages = hand_over(sums, step - 1)
         rows = 2**step
         last = step == sz.segs - 1
-        shapes = fins if last else (shape_of(half, 2 * rows, sz.width),) * 2 + fins
-        given = 2 + half + 2 * sz.held
+        shapes = fins if last else (pltpu.VMEM((half, 2 * rows, sz.width), F32),) * 2 + fins
+        given = 2 + half + sz.held + sz.packs
         outs = pl.pallas_call(
             functools.partial(site_kernel, sz, step),
             out_shape=shapes,
-            in_specs=[VMEM, ANY] + [VMEM] * (half + 2 * sz.held + 2),
+            in_specs=[VMEM] * (given + 2),
             out_specs=(VMEM,) * len(shapes),
             input_output_aliases={given: len(shapes) - 2, given + 1: len(shapes) - 1},
             scratch_shapes=[
-                ring,
                 pltpu.VMEM((max(16, 2 * rows), sz.left), F32),
+                pltpu.VMEM((max(32, 2 * rows), sz.left), F32),
                 pltpu.VMEM((2, half, 2 * rows, sz.width), F32),
-                sems,
             ],
             compiler_params=params(SCOPE),
             name="site_" + str(step),
-        )(bits, site, *messages, *held, *fin)
+        )(bits, scales, *messages, *held, *fin)
+        outs = [in_vmem(x) for x in outs]
         fin = outs[-2:]
         if not last:
             keep, give = outs[:2]
 
-    every = range(sz.segs)
-    sums = add(fin[0], swap_cores(fin[1], every))
-    parts = [sums[0]] + [to_pair(sums[t], t, every, 0) for t in range(1, half)]
+    sums = add(fin[0], swap_cores(fin[1]))
+    parts = [in_vmem(sums[0])] + [to_pair(sums[t], t) for t in range(1, half)]
     tail = pl.pallas_call(
         functools.partial(norm_kernel, sz),
-        out_shape=shape_of(2, sz.extra),
+        out_shape=pltpu.VMEM((2, sz.extra), F32),
         in_specs=[VMEM] * half,
         out_specs=VMEM,
         compiler_params=params(2 * MIB),
@@ -403,13 +427,13 @@
     )(*parts)
     tail = pl.pallas_call(
         sum_kernel,
-        out_shape=shape_of(2, sz.extra),
+        out_shape=pltpu.VMEM((2, sz.extra), F32),
         in_specs=[VMEM] * 2,
         out_specs=VMEM,
         compiler_params=params(MIB),
         name="norms_pair",
-    )(tail, swap_cores(tail, every))
-    parts = [tail] + [to_pair(tail, t, every, 0) for t in range(1, half)]
+    )(in_vmem(tail), swap_cores(tail))
+    parts = [in_vmem(tail)] + [to_pair(tail, t) for t in range(1, half)]
     probs = pl.pallas_call(
         functools.partial(final_kernel, sz),
         out_shape=shape_of(1, sz.rows),
@@ -417,7 +441,7 @@
         out_specs=VMEM,
         compiler_params=params(MIB),
         name="probs",
-    )(order.reshape(1, sz.rows), *parts)
+    )(order, *parts)
     return probs.reshape(sz.rows, 1)
 
 

time: 129 us -> 96 us (0.74)
  waiting for transfers between devices: 65.4 us -> 27.6 us
  starting transfers between devices: 20.1 us -> 38.1 us
  Pallas kernels: 36.8 us -> 29.9 us
  local copies, waits for them, and re-layouts: 5.3 us -> 0 us
    ppermute x23, waiting for transfers between devices: 65.4 us -> 27.6 us  [the longest x11 17.1 us: permute(): return in_vmem(lax.ppermute(x, AXES, pairs))]
    ppermute x23, starting transfers between devices: 20.1 us -> 38.1 us  [the longest x12 30.2 us: hand_over(): came[t] = in_vmem(lax.ppermute(sums[t], AXES, pairs))]
    pallas_call x3, Pallas kernels: 18.2 us -> 7.01 us  [on_device(): pl.pallas_call(functools.partial(site_kernel, sz, step), out_shape=shapes...]
    unnamed x34 -> x0, local copies, waits for them, and re-layouts: 5.3 us -> none
    pallas_call x7, Pallas kernels: 17.9 us -> 22.1 us  [the longest x1 21.9 us: on_device(): pl.pallas_call(functools.partial(first_kernel, sz), out_shape=(pltpu.VMEM...]
  transfers between devices with their start and end apart: 23 -> 23, of which waited for: 11 -> 16; matrix products, arithmetic and copies ran while one was open for 0% -> 0% of each run, Pallas kernels for 0% -> 0%
where the time goes in v2:
time: 96 us; the launch traced here: 95.8 us
  starting transfers between devices  38.1 us (40%)
  Pallas kernels  29.9 us (31%)
  waiting for transfers between devices  27.6 us (29%)
    ppermute x12, starting transfers between devices, hand_over(): came[t] = in_vmem(lax.ppermute(sums[t], AXES, pairs))  30.2 us
    pallas_call x1, Pallas kernels, on_device(): pl.pallas_call(functools.partial(first_kernel, sz), out_shape=(pltpu.VMEM...  21.9 us
    ppermute x11, waiting for transfers between devices, permute(): return in_vmem(lax.ppermute(x, AXES, pairs))  17.1 us
    ppermute x12, waiting for transfers between devices, hand_over(): came[t] = in_vmem(lax.ppermute(sums[t], AXES, pairs))  10.5 us
    ppermute x11, starting transfers between devices, permute(): return in_vmem(lax.ppermute(x, AXES, pairs))  7.95 us
    pallas_call x3, Pallas kernels, on_device(): pl.pallas_call(functools.partial(site_kernel, sz, step), out_shape=shapes...  7.01 us
  transfers between devices with their start and end apart: 23, of which 16 were waited for; matrix products, arithmetic and copies ran while one was open for 0% of the time, Pallas kernels for 0%

profile of v2, /device:TPU:6, one launch (start us, length us, event | category | flops | bytes accessed | tf_op | source)
XLA Modules:
  0.0 95.8 jit_solution(5515603118754461198)
XLA Ops:
  0.0 21.9 %first_site.1 = (f32[4,2,1152]{2,1,0:T(2,128)S(1)}, f32[4,2,1152]{2,1,0:T(2,128)S(1)}, f32[4,16,1152]{2,1,0:T(8,128)S(1)}, f32[4,16,1152]{2,1,0:T(8,128)S(1)}, s...) custom-call(s32[1,32]{1,0:T(1,128)} %bitcast.6, ...), custom_call_target="tpu_custom_call" | custom-call | tf_op jit(solution)/shard_map/first_site/pallas_call | solution.py:368
  21.9 0.1 collective-permute-start
  22.0 1.2 %collective-permute-done.came = f32[4,2,1152]{2,1,0:T(2,128)S(1)} collective-permute-done((f32[4,2,1152]{2,1,0:T(2,128)S(1)}, f32[4,2,1152]{2,1,0:T(2,128)S(1)}, u32[]{:S(2)}, u32[]{:S(2)}) %collective-permute-start) | collective-permute-done | bytes 36896 | tf_op jit(solution)/shard_map/ppermute | solution.py:332
  23.2 0.7 collective-permute-start.1
  23.9 4.3 %collective-permute-start.2 = (f32[2,1152]{1,0:T(2,128)S(1)}, f32[2,1152]{1,0:T(2,128)S(1)}, u32[]{:S(2)}, u32[]{:S(2)}) collective-permute-start(f32[2,1152]{1,0:T(2,128)S(1)} %get-tuple-element.56), channel_id=1, source_target_pairs={{0,10},{1,11},{2,12},{3,13},{4,14},{5,15},{6,8},{7,9},{8,18},{9,19... | collective-permute-start | bytes 27656 | tf_op jit(solution)/shard_map/ppermute | solution.py:349
  28.2 1.4 %collective-permute-start.3 = (f32[2,1152]{1,0:T(2,128)S(1)}, f32[2,1152]{1,0:T(2,128)S(1)}, u32[]{:S(2)}, u32[]{:S(2)}) collective-permute-start(f32[2,1152]{1,0:T(2,128)S(1)} %get-tuple-element.57), channel_id=1, source_target_pairs={{0,12},{1,13},{2,14},{3,15},{4,8},{5,9},{6,10},{7,11},{8,20},{9,21... | collective-permute-start | bytes 27656 | tf_op jit(solution)/shard_map/ppermute | solution.py:349
  29.6 0.7 collective-permute-start.4
  30.2 0.0 collective-permute-done.1.refs_2_
  30.3 0.1 collective-permute-done.2.refs_3_
  30.3 3.3 %collective-permute-done.3.refs_4_ = f32[2,1152]{1,0:T(2,128)S(1)} collective-permute-done((f32[2,1152]{1,0:T(2,128)S(1)}, f32[2,1152]{1,0:T(2,128)S(1)}, u32[]{:S(2)}, u32[]{:S(2)}) %collective-permute-start.3) | collective-permute-done | bytes 9248 | tf_op jit(solution)/shard_map/ppermute | solution.py:349
  33.6 0.0 collective-permute-done.4.refs_5_
  33.6 0.1 site_1.1
  33.7 0.1 collective-permute-start.5
  33.8 1.3 %collective-permute-done.5.came = f32[4,4,1152]{2,1,0:T(4,128)S(1)} collective-permute-done((f32[4,4,1152]{2,1,0:T(4,128)S(1)}, f32[4,4,1152]{2,1,0:T(4,128)S(1)}, u32[]{:S(2)}, u32[]{:S(2)}) %collective-permute-start.5) | collective-permute-done | bytes 73760 | tf_op jit(solution)/shard_map/ppermute | solution.py:332
  35.1 0.7 collective-permute-start.6
  35.7 2.5 %collective-permute-start.7 = (f32[4,1152]{1,0:T(4,128)S(1)}, f32[4,1152]{1,0:T(4,128)S(1)}, u32[]{:S(2)}, u32[]{:S(2)}) collective-permute-start(f32[4,1152]{1,0:T(4,128)S(1)} %get-tuple-element.76), channel_id=1, source_target_pairs={{0,10},{1,11},{2,12},{3,13},{4,14},{5,15},{6,8},{7,9},{8,18},{9,19... | collective-permute-start | bytes 55304 | tf_op jit(solution)/shard_map/ppermute | solution.py:349
  38.2 12.3 %collective-permute-start.8 = (f32[4,1152]{1,0:T(4,128)S(1)}, f32[4,1152]{1,0:T(4,128)S(1)}, u32[]{:S(2)}, u32[]{:S(2)}) collective-permute-start(f32[4,1152]{1,0:T(4,128)S(1)} %get-tuple-element.77), channel_id=1, source_target_pairs={{0,12},{1,13},{2,14},{3,15},{4,8},{5,9},{6,10},{7,11},{8,20},{9,21... | collective-permute-start | bytes 55304 | tf_op jit(solution)/shard_map/ppermute | solution.py:349
  50.6 0.7 collective-permute-start.9
  51.2 0.0 collective-permute-done.6.refs_2_
  51.2 0.0 collective-permute-done.7.refs_3_
  51.2 0.8 collective-permute-done.8.refs_4_
  52.0 0.0 collective-permute-done.9.refs_5_
  52.0 0.1 site_2.1
  52.1 0.1 collective-permute-start.10
  52.2 1.4 %collective-permute-done.10.came = f32[4,8,1152]{2,1,0:T(8,128)S(1)} collective-permute-done((f32[4,8,1152]{2,1,0:T(8,128)S(1)}, f32[4,8,1152]{2,1,0:T(8,128)S(1)}, u32[]{:S(2)}, u32[]{:S(2)}) %collective-permute-start.10) | collective-permute-done | bytes 147488 | tf_op jit(solution)/shard_map/ppermute | solution.py:332
  53.5 1.3 %collective-permute-start.11 = (f32[8,1152]{1,0:T(8,128)S(1)}, f32[8,1152]{1,0:T(8,128)S(1)}, u32[]{:S(2)}, u32[]{:S(2)}) collective-permute-start(f32[8,1152]{1,0:T(8,128)S(1)} %get-tuple-element.83), channel_id=1, source_target_pairs={{16,24},{17,25},{18,26},{19,27},{20,28},{21,29},{22,30},{23,31}} | collective-permute-start | bytes 110600 | tf_op jit(solution)/shard_map/ppermute | solution.py:349
  54.9 1.7 %collective-permute-start.12 = (f32[8,1152]{1,0:T(8,128)S(1)}, f32[8,1152]{1,0:T(8,128)S(1)}, u32[]{:S(2)}, u32[]{:S(2)}) collective-permute-start(f32[8,1152]{1,0:T(8,128)S(1)} %get-tuple-element.84), channel_id=1, source_target_pairs={{0,10},{1,11},{2,12},{3,13},{4,14},{5,15},{6,8},{7,9},{8,18},{9,19... | collective-permute-start | bytes 110600 | tf_op jit(solution)/shard_map/ppermute | solution.py:349
  56.5 2.8 %collective-permute-start.13 = (f32[8,1152]{1,0:T(8,128)S(1)}, f32[8,1152]{1,0:T(8,128)S(1)}, u32[]{:S(2)}, u32[]{:S(2)}) collective-permute-start(f32[8,1152]{1,0:T(8,128)S(1)} %get-tuple-element.85), channel_id=1, source_target_pairs={{0,12},{1,13},{2,14},{3,15},{4,8},{5,9},{6,10},{7,11},{8,20},{9,21... | collective-permute-start | bytes 110600 | tf_op jit(solution)/shard_map/ppermute | solution.py:349
  59.3 1.3 %collective-permute-start.14 = (f32[8,1152]{1,0:T(8,128)S(1)}, f32[8,1152]{1,0:T(8,128)S(1)}, u32[]{:S(2)}, u32[]{:S(2)}) collective-permute-start(f32[8,1152]{1,0:T(8,128)S(1)} %get-tuple-element.86), channel_id=1, source_target_pairs={{16,30},{17,31},{18,24},{19,25},{20,26},{21,27},{22,28},{23,29}} | collective-permute-start | bytes 110600 | tf_op jit(solution)/shard_map/ppermute | solution.py:349
  60.6 3.2 %collective-permute-done.11.refs_2_ = f32[8,1152]{1,0:T(8,128)S(1)} collective-permute-done((f32[8,1152]{1,0:T(8,128)S(1)}, f32[8,1152]{1,0:T(8,128)S(1)}, u32[]{:S(2)}, u32[]{:S(2)}) %collective-permute-start.11) | collective-permute-done | bytes 36896 | tf_op jit(solution)/shard_map/ppermute | solution.py:349
  63.8 1.9 %collective-permute-done.12.refs_3_ = f32[8,1152]{1,0:T(8,128)S(1)} collective-permute-done((f32[8,1152]{1,0:T(8,128)S(1)}, f32[8,1152]{1,0:T(8,128)S(1)}, u32[]{:S(2)}, u32[]{:S(2)}) %collective-permute-start.12) | collective-permute-done | bytes 36896 | tf_op jit(solution)/shard_map/ppermute | solution.py:349
  65.7 1.2 %collective-permute-done.13.refs_4_ = f32[8,1152]{1,0:T(8,128)S(1)} collective-permute-done((f32[8,1152]{1,0:T(8,128)S(1)}, f32[8,1152]{1,0:T(8,128)S(1)}, u32[]{:S(2)}, u32[]{:S(2)}) %collective-permute-start.13) | collective-permute-done | bytes 36896 | tf_op jit(solution)/shard_map/ppermute | solution.py:349
  66.9 0.0 collective-permute-done.14.refs_5_
  66.9 6.9 %site_3.1 = (f32[4,16,1152]{2,1,0:T(8,128)S(1)}, f32[4,16,1152]{2,1,0:T(8,128)S(1)}) custom-call(s32[1,32]{1,0:T(1,128)S(1)} %get-tuple-element.51.refs_0_, f32[32,128]{1,0:T(8,128)S(1)} %get-tuple-element.52.refs_1_, f32[8,1152]{1,0:T(8,128)S(1)} %collective-permute-done.11.refs_2_, ...), custom_call_target="tpu_custom_call", output_to_operand_aliasing={{0}: (18, {}), {1}: (19, {})} | custom-call | tf_op jit(solution)/shard_map/site_3/pallas_call | solution.py:399
  73.8 0.1 collective-permute-start.15
  73.9 1.6 %collective-permute-done.15.came = f32[4,16,1152]{2,1,0:T(8,128)S(1)} collective-permute-done((f32[4,16,1152]{2,1,0:T(8,128)S(1)}, f32[4,16,1152]{2,1,0:T(8,128)S(1)}, u32[]{:S(2)}, u32[]{:S(2)}) %collective-permute-start.15) | collective-permute-done | bytes 294944 | tf_op jit(solution)/shard_map/ppermute | solution.py:332
  75.5 1.3 %collective-permute-start.16 = (f32[16,1152]{1,0:T(8,128)S(1)}, f32[16,1152]{1,0:T(8,128)S(1)}, u32[]{:S(2)}, u32[]{:S(2)}) collective-permute-start(f32[16,1152]{1,0:T(8,128)S(1)} %get-tuple-element.92), channel_id=1, source_target_pairs={{0,2},{1,3},{2,4},{3,5},{4,6},{5,7},{6,0},{7,1},{8,10},{9,11},{10,... | collective-permute-start | bytes 221192 | tf_op jit(solution)/shard_map/ppermute | solution.py:332
  76.7 1.1 %collective-permute-start.17 = (f32[16,1152]{1,0:T(8,128)S(1)}, f32[16,1152]{1,0:T(8,128)S(1)}, u32[]{:S(2)}, u32[]{:S(2)}) collective-permute-start(f32[16,1152]{1,0:T(8,128)S(1)} %get-tuple-element.93), channel_id=1, source_target_pairs={{0,4},{1,5},{2,6},{3,7},{4,0},{5,1},{6,2},{7,3},{8,12},{9,13},{10,... | collective-permute-start | bytes 221192 | tf_op jit(solution)/shard_map/ppermute | solution.py:332
  77.9 1.7 %collective-permute-start.18 = (f32[16,1152]{1,0:T(8,128)S(1)}, f32[16,1152]{1,0:T(8,128)S(1)}, u32[]{:S(2)}, u32[]{:S(2)}) collective-permute-start(f32[16,1152]{1,0:T(8,128)S(1)} %get-tuple-element.94), channel_id=1, source_target_pairs={{0,6},{1,7},{2,0},{3,1},{4,2},{5,3},{6,4},{7,5},{8,14},{9,15},{10,... | collective-permute-start | bytes 221192 | tf_op jit(solution)/shard_map/ppermute | solution.py:332
  79.6 2.9 %collective-permute-done.16.refs_1_ = f32[16,1152]{1,0:T(8,128)S(1)} collective-permute-done((f32[16,1152]{1,0:T(8,128)S(1)}, f32[16,1152]{1,0:T(8,128)S(1)}, u32[]{:S(2)}, u32[]{:S(2)}) %collective-permute-start.16) | collective-permute-done | bytes 73760 | tf_op jit(solution)/shard_map/ppermute | solution.py:332
  82.5 2.4 %collective-permute-done.17.refs_2_ = f32[16,1152]{1,0:T(8,128)S(1)} collective-permute-done((f32[16,1152]{1,0:T(8,128)S(1)}, f32[16,1152]{1,0:T(8,128)S(1)}, u32[]{:S(2)}, u32[]{:S(2)}) %collective-permute-start.17) | collective-permute-done | bytes 73760 | tf_op jit(solution)/shard_map/ppermute | solution.py:332
  84.9 0.0 collective-permute-done.18.refs_3_
  84.9 0.1 norms.1.left
  85.0 0.0 collective-permute-start.19
  85.0 1.1 %collective-permute-done.19.right = f32[2,128]{1,0:T(2,128)S(1)} collective-permute-done((f32[2,128]{1,0:T(2,128)S(1)}, f32[2,128]{1,0:T(2,128)S(1)}, u32[]{:S(2)}, u32[]{:S(2)}) %collective-permute-start.19) | collective-permute-done | bytes 1056 | tf_op jit(solution)/shard_map/ppermute | solution.py:332
  86.2 2.3 %collective-permute-start.22 = (f32[2,128]{1,0:T(2,128)S(1)}, f32[2,128]{1,0:T(2,128)S(1)}, u32[]{:S(2)}, u32[]{:S(2)}) collective-permute-start(f32[2,128]{1,0:T(2,128)S(1)} %norms_pair.1.refs_0_), channel_id=1, source_target_pairs={{0,6},{1,7},{2,0},{3,1},{4,2},{5,3},{6,4},{7,5},{8,14},{9,15},{10,... | collective-permute-start | bytes 3080 | tf_op jit(solution)/shard_map/ppermute | solution.py:332
  88.4 1.2 %collective-permute-start.21 = (f32[2,128]{1,0:T(2,128)S(1)}, f32[2,128]{1,0:T(2,128)S(1)}, u32[]{:S(2)}, u32[]{:S(2)}) collective-permute-start(f32[2,128]{1,0:T(2,128)S(1)} %norms_pair.1.refs_0_), channel_id=1, source_target_pairs={{0,4},{1,5},{2,6},{3,7},{4,0},{5,1},{6,2},{7,3},{8,12},{9,13},{10,... | collective-permute-start | bytes 3080 | tf_op jit(solution)/shard_map/ppermute | solution.py:332
  89.7 0.0 collective-permute-start.20
  89.7 0.1 collective-permute-done.22.refs_3_
  89.7 3.1 %collective-permute-done.21.refs_2_ = f32[2,128]{1,0:T(2,128)S(1)} collective-permute-done((f32[2,128]{1,0:T(2,128)S(1)}, f32[2,128]{1,0:T(2,128)S(1)}, u32[]{:S(2)}, u32[]{:S(2)}) %collective-permute-start.21) | collective-permute-done | bytes 1056 | tf_op jit(solution)/shard_map/ppermute | solution.py:332
  92.9 2.1 %collective-permute-done.20.refs_1_ = f32[2,128]{1,0:T(2,128)S(1)} collective-permute-done((f32[2,128]{1,0:T(2,128)S(1)}, f32[2,128]{1,0:T(2,128)S(1)}, u32[]{:S(2)}, u32[]{:S(2)}) %collective-permute-start.20) | collective-permute-done | bytes 1056 | tf_op jit(solution)/shard_map/ppermute | solution.py:332
  95.0 0.7 probs.1
  (5 shorter events, 0.1 us)
Async XLA Ops:
  21.9 1.3 %collective-permute-start = (f32[4,2,1152]{2,1,0:T(2,128)S(1)}, f32[4,2,1152]{2,1,0:T(2,128)S(1)}, u32[]{:S(2)}, u32[]{:S(2)}) collective-permute-start(f32[4,2,1152]{2,1,0:T(2,128)S(1)} %get-tuple-element.54), channel_id=1, source_target_pairs={{0,1},{1,0},{2,3},{3,2},{4,5},{5,4},{6,7},{7,6},{8,9},{9,8},{10,11... | collective-permute-start | bytes 110600 | tf_op jit(solution)/shard_map/ppermute | solution.py:332
  23.2 7.0 %collective-permute-start.1 = (f32[2,1152]{1,0:T(2,128)S(1)}, f32[2,1152]{1,0:T(2,128)S(1)}, u32[]{:S(2)}, u32[]{:S(2)}) collective-permute-start(f32[2,1152]{1,0:T(2,128)S(1)} %get-tuple-element.55), channel_id=1, source_target_pairs={{0,8},{1,9},{2,10},{3,11},{4,12},{5,13},{6,14},{7,15}} | collective-permute-start | bytes 27656 | tf_op jit(solution)/shard_map/ppermute | solution.py:349
  23.9 6.4 %collective-permute-start.2 = (f32[2,1152]{1,0:T(2,128)S(1)}, f32[2,1152]{1,0:T(2,128)S(1)}, u32[]{:S(2)}, u32[]{:S(2)}) collective-permute-start(f32[2,1152]{1,0:T(2,128)S(1)} %get-tuple-element.56), channel_id=1, source_target_pairs={{0,10},{1,11},{2,12},{3,13},{4,14},{5,15},{6,8},{7,9},{8,18},{9,19... | collective-permute-start | bytes 27656 | tf_op jit(solution)/shard_map/ppermute | solution.py:349
  28.2 5.5 %collective-permute-start.3 = (f32[2,1152]{1,0:T(2,128)S(1)}, f32[2,1152]{1,0:T(2,128)S(1)}, u32[]{:S(2)}, u32[]{:S(2)}) collective-permute-start(f32[2,1152]{1,0:T(2,128)S(1)} %get-tuple-element.57), channel_id=1, source_target_pairs={{0,12},{1,13},{2,14},{3,15},{4,8},{5,9},{6,10},{7,11},{8,20},{9,21... | collective-permute-start | bytes 27656 | tf_op jit(solution)/shard_map/ppermute | solution.py:349
  29.6 4.1 %collective-permute-start.4 = (f32[2,1152]{1,0:T(2,128)S(1)}, f32[2,1152]{1,0:T(2,128)S(1)}, u32[]{:S(2)}, u32[]{:S(2)}) collective-permute-start(f32[2,1152]{1,0:T(2,128)S(1)} %get-tuple-element.58), channel_id=1, source_target_pairs={{0,14},{1,15},{2,8},{3,9},{4,10},{5,11},{6,12},{7,13}} | collective-permute-start | bytes 27656 | tf_op jit(solution)/shard_map/ppermute | solution.py:349
  33.7 1.3 %collective-permute-start.5 = (f32[4,4,1152]{2,1,0:T(4,128)S(1)}, f32[4,4,1152]{2,1,0:T(4,128)S(1)}, u32[]{:S(2)}, u32[]{:S(2)}) collective-permute-start(f32[4,4,1152]{2,1,0:T(4,128)S(1)} %get-tuple-element.74), channel_id=1, source_target_pairs={{0,1},{1,0},{2,3},{3,2},{4,5},{5,4},{6,7},{7,6},{8,9},{9,8},{10,11... | collective-permute-start | bytes 221192 | tf_op jit(solution)/shard_map/ppermute | solution.py:332
  35.1 16.2 %collective-permute-start.6 = (f32[4,1152]{1,0:T(4,128)S(1)}, f32[4,1152]{1,0:T(4,128)S(1)}, u32[]{:S(2)}, u32[]{:S(2)}) collective-permute-start(f32[4,1152]{1,0:T(4,128)S(1)} %get-tuple-element.75), channel_id=1, source_target_pairs={{8,16},{9,17},{10,18},{11,19},{12,20},{13,21},{14,22},{15,23}} | collective-permute-start | bytes 55304 | tf_op jit(solution)/shard_map/ppermute | solution.py:349
  35.7 15.5 %collective-permute-start.7 = (f32[4,1152]{1,0:T(4,128)S(1)}, f32[4,1152]{1,0:T(4,128)S(1)}, u32[]{:S(2)}, u32[]{:S(2)}) collective-permute-start(f32[4,1152]{1,0:T(4,128)S(1)} %get-tuple-element.76), channel_id=1, source_target_pairs={{0,10},{1,11},{2,12},{3,13},{4,14},{5,15},{6,8},{7,9},{8,18},{9,19... | collective-permute-start | bytes 55304 | tf_op jit(solution)/shard_map/ppermute | solution.py:349
  38.2 13.8 %collective-permute-start.8 = (f32[4,1152]{1,0:T(4,128)S(1)}, f32[4,1152]{1,0:T(4,128)S(1)}, u32[]{:S(2)}, u32[]{:S(2)}) collective-permute-start(f32[4,1152]{1,0:T(4,128)S(1)} %get-tuple-element.77), channel_id=1, source_target_pairs={{0,12},{1,13},{2,14},{3,15},{4,8},{5,9},{6,10},{7,11},{8,20},{9,21... | collective-permute-start | bytes 55304 | tf_op jit(solution)/shard_map/ppermute | solution.py:349
  50.6 1.5 %collective-permute-start.9 = (f32[4,1152]{1,0:T(4,128)S(1)}, f32[4,1152]{1,0:T(4,128)S(1)}, u32[]{:S(2)}, u32[]{:S(2)}) collective-permute-start(f32[4,1152]{1,0:T(4,128)S(1)} %get-tuple-element.78), channel_id=1, source_target_pairs={{8,22},{9,23},{10,16},{11,17},{12,18},{13,19},{14,20},{15,21}} | collective-permute-start | bytes 55304 | tf_op jit(solution)/shard_map/ppermute | solution.py:349
  52.1 1.4 %collective-permute-start.10 = (f32[4,8,1152]{2,1,0:T(8,128)S(1)}, f32[4,8,1152]{2,1,0:T(8,128)S(1)}, u32[]{:S(2)}, u32[]{:S(2)}) collective-permute-start(f32[4,8,1152]{2,1,0:T(8,128)S(1)} %get-tuple-element.82), channel_id=1, source_target_pairs={{0,1},{1,0},{2,3},{3,2},{4,5},{5,4},{6,7},{7,6},{8,9},{9,8},{10,11... | collective-permute-start | bytes 442376 | tf_op jit(solution)/shard_map/ppermute | solution.py:332
  53.5 10.3 %collective-permute-start.11 = (f32[8,1152]{1,0:T(8,128)S(1)}, f32[8,1152]{1,0:T(8,128)S(1)}, u32[]{:S(2)}, u32[]{:S(2)}) collective-permute-start(f32[8,1152]{1,0:T(8,128)S(1)} %get-tuple-element.83), channel_id=1, source_target_pairs={{16,24},{17,25},{18,26},{19,27},{20,28},{21,29},{22,30},{23,31}} | collective-permute-start | bytes 110600 | tf_op jit(solution)/shard_map/ppermute | solution.py:349
  54.9 10.9 %collective-permute-start.12 = (f32[8,1152]{1,0:T(8,128)S(1)}, f32[8,1152]{1,0:T(8,128)S(1)}, u32[]{:S(2)}, u32[]{:S(2)}) collective-permute-start(f32[8,1152]{1,0:T(8,128)S(1)} %get-tuple-element.84), channel_id=1, source_target_pairs={{0,10},{1,11},{2,12},{3,13},{4,14},{5,15},{6,8},{7,9},{8,18},{9,19... | collective-permute-start | bytes 110600 | tf_op jit(solution)/shard_map/ppermute | solution.py:349
  56.5 10.4 %collective-permute-start.13 = (f32[8,1152]{1,0:T(8,128)S(1)}, f32[8,1152]{1,0:T(8,128)S(1)}, u32[]{:S(2)}, u32[]{:S(2)}) collective-permute-start(f32[8,1152]{1,0:T(8,128)S(1)} %get-tuple-element.85), channel_id=1, source_target_pairs={{0,12},{1,13},{2,14},{3,15},{4,8},{5,9},{6,10},{7,11},{8,20},{9,21... | collective-permute-start | bytes 110600 | tf_op jit(solution)/shard_map/ppermute | solution.py:349
  59.3 7.6 %collective-permute-start.14 = (f32[8,1152]{1,0:T(8,128)S(1)}, f32[8,1152]{1,0:T(8,128)S(1)}, u32[]{:S(2)}, u32[]{:S(2)}) collective-permute-start(f32[8,1152]{1,0:T(8,128)S(1)} %get-tuple-element.86), channel_id=1, source_target_pairs={{16,30},{17,31},{18,24},{19,25},{20,26},{21,27},{22,28},{23,29}} | collective-permute-start | bytes 110600 | tf_op jit(solution)/shard_map/ppermute | solution.py:349
  73.8 1.6 %collective-permute-start.15 = (f32[4,16,1152]{2,1,0:T(8,128)S(1)}, f32[4,16,1152]{2,1,0:T(8,128)S(1)}, u32[]{:S(2)}, u32[]{:S(2)}) collective-permute-start(f32[4,16,1152]{2,1,0:T(8,128)S(1)} %get-tuple-element.90), channel_id=1, source_target_pairs={{0,1},{1,0},{2,3},{3,2},{4,5},{5,4},{6,7},{7,6},{8,9},{9,8},{10,11... | collective-permute-start | bytes 884744 | tf_op jit(solution)/shard_map/ppermute | solution.py:332
  75.5 7.0 %collective-permute-start.16 = (f32[16,1152]{1,0:T(8,128)S(1)}, f32[16,1152]{1,0:T(8,128)S(1)}, u32[]{:S(2)}, u32[]{:S(2)}) collective-permute-start(f32[16,1152]{1,0:T(8,128)S(1)} %get-tuple-element.92), channel_id=1, source_target_pairs={{0,2},{1,3},{2,4},{3,5},{4,6},{5,7},{6,0},{7,1},{8,10},{9,11},{10,... | collective-permute-start | bytes 221192 | tf_op jit(solution)/shard_map/ppermute | solution.py:332
  76.7 8.2 %collective-permute-start.17 = (f32[16,1152]{1,0:T(8,128)S(1)}, f32[16,1152]{1,0:T(8,128)S(1)}, u32[]{:S(2)}, u32[]{:S(2)}) collective-permute-start(f32[16,1152]{1,0:T(8,128)S(1)} %get-tuple-element.93), channel_id=1, source_target_pairs={{0,4},{1,5},{2,6},{3,7},{4,0},{5,1},{6,2},{7,3},{8,12},{9,13},{10,... | collective-permute-start | bytes 221192 | tf_op jit(solution)/shard_map/ppermute | solution.py:332
  77.9 7.0 %collective-permute-start.18 = (f32[16,1152]{1,0:T(8,128)S(1)}, f32[16,1152]{1,0:T(8,128)S(1)}, u32[]{:S(2)}, u32[]{:S(2)}) collective-permute-start(f32[16,1152]{1,0:T(8,128)S(1)} %get-tuple-element.94), channel_id=1, source_target_pairs={{0,6},{1,7},{2,0},{3,1},{4,2},{5,3},{6,4},{7,5},{8,14},{9,15},{10,... | collective-permute-start | bytes 221192 | tf_op jit(solution)/shard_map/ppermute | solution.py:332
  85.0 1.1 %collective-permute-start.19 = (f32[2,128]{1,0:T(2,128)S(1)}, f32[2,128]{1,0:T(2,128)S(1)}, u32[]{:S(2)}, u32[]{:S(2)}) collective-permute-start(f32[2,128]{1,0:T(2,128)S(1)} %norms.1.left), channel_id=1, source_target_pairs={{0,1},{1,0},{2,3},{3,2},{4,5},{5,4},{6,7},{7,6},{8,9},{9,8},{10,11... | collective-permute-start | bytes 3080 | tf_op jit(solution)/shard_map/ppermute | solution.py:332
  86.2 3.6 %collective-permute-start.22 = (f32[2,128]{1,0:T(2,128)S(1)}, f32[2,128]{1,0:T(2,128)S(1)}, u32[]{:S(2)}, u32[]{:S(2)}) collective-permute-start(f32[2,128]{1,0:T(2,128)S(1)} %norms_pair.1.refs_0_), channel_id=1, source_target_pairs={{0,6},{1,7},{2,0},{3,1},{4,2},{5,3},{6,4},{7,5},{8,14},{9,15},{10,... | collective-permute-start | bytes 3080 | tf_op jit(solution)/shard_map/ppermute | solution.py:332
  88.4 4.5 %collective-permute-start.21 = (f32[2,128]{1,0:T(2,128)S(1)}, f32[2,128]{1,0:T(2,128)S(1)}, u32[]{:S(2)}, u32[]{:S(2)}) collective-permute-start(f32[2,128]{1,0:T(2,128)S(1)} %norms_pair.1.refs_0_), channel_id=1, source_target_pairs={{0,4},{1,5},{2,6},{3,7},{4,0},{5,1},{6,2},{7,3},{8,12},{9,13},{10,... | collective-permute-start | bytes 3080 | tf_op jit(solution)/shard_map/ppermute | solution.py:332
  89.7 5.4 %collective-permute-start.20 = (f32[2,128]{1,0:T(2,128)S(1)}, f32[2,128]{1,0:T(2,128)S(1)}, u32[]{:S(2)}, u32[]{:S(2)}) collective-permute-start(f32[2,128]{1,0:T(2,128)S(1)} %norms_pair.1.refs_0_), channel_id=1, source_target_pairs={{0,2},{1,3},{2,4},{3,5},{4,6},{5,7},{6,0},{7,1},{8,10},{9,11},{10,... | collective-permute-start | bytes 3080 | tf_op jit(solution)/shard_map/ppermute | solution.py:332

commit v3 on v2

--- a/solution.py
+++ b/solution.py
@@ -13,13 +13,14 @@
 MIB = 2**20
 BLOCK = 2048
 RING = 4
-RINGS = (1, 2)
+RINGS = (3, 2)
 SCOPE = 43 * MIB // 4
 F32 = jnp.float32
 BF16 = jnp.bfloat16
 F8 = jnp.float8_e4m3fn
 TOP = 256.0
 TINY = 1e-30
+STRIP = 64
 VMEM = pl.BlockSpec(memory_space=pltpu.VMEM)
 ANY = pl.BlockSpec(memory_space=pl.ANY)
 
@@ -30,6 +31,8 @@
         self.segs = lax.axis_size("seg")
         self.bonds = lax.axis_size("bond")
         self.half = self.bonds // 2
+        near = [t for t in reversed(range(self.half)) if t not in RINGS]
+        self.turns = [t for t in RINGS if t < self.half] + near
         self.left, self.right = sites.shape[2], sites.shape[3]
         self.chunk = self.right // self.bonds
         assert self.chunk == self.left and self.bonds % 2 == 0
@@ -140,14 +143,19 @@
                 index = b * sz.pieces + i
                 slot = index % RING
                 copy(index).wait()
-                x = ring[slot]
-                high, low = split(x)
+                strips = [slice(r, r + STRIP) for r in range(0, sz.left, STRIP)]
+                most = jnp.abs(ring[slot, strips[0], :])
+                for strip in strips[1:]:
+                    most = jnp.maximum(most, jnp.abs(ring[slot, strip, :]))
+                most = jnp.max(jnp.max(most, axis=0, keepdims=True), axis=1, keepdims=True)
+                most = jnp.maximum(most, TINY)
+                grow = TOP * TOP / most
                 column = pl.multiple_of(i * sz.piece, sz.piece)
-                highs[b][:, pl.ds(column, sz.piece)] = high
-                most = jnp.max(jnp.max(jnp.abs(x), axis=0, keepdims=True), axis=1, keepdims=True)
-                most = jnp.maximum(most, TINY)
-                column = pl.multiple_of(b % 2 * sz.block + i * sz.piece, sz.piece)
-                lows[b // 2][:, pl.ds(column, sz.piece)] = (low * (TOP * TOP / most)).astype(F8)
+                packed = pl.multiple_of(b % 2 * sz.block + i * sz.piece, sz.piece)
+                for strip in strips:
+                    high, low = split(ring[slot, strip, :])
+                    highs[b][strip, pl.ds(column, sz.piece)] = high
+                    lows[b // 2][strip, pl.ds(packed, sz.piece)] = (low * grow).astype(F8)
                 scales[pl.ds(index, 1), :] = jnp.broadcast_to(most / (TOP * TOP), (1, LANES))
 
                 @pl.when(index + RING < total)
@@ -255,7 +263,7 @@
 
 def add_kernel(sz, keep, came, *outs):
     pair = lax.axis_index("bond") // 2
-    for t, out in enumerate(outs):
+    for t, out in zip(sz.turns, outs):
         target = lax.rem(pair + t, sz.half)
         out[...] = keep[target] + came[target]
 
@@ -338,16 +346,15 @@
         return permute(x, lambda k, j: k * bonds + (j // 2 + t) % half * 2 + j % 2)
 
     def hand_over(sums, group):
-        alone = [t for t in range(half) if t not in RINGS]
-        came = {}
-        for t in alone + [t for t in RINGS if t < half]:
+        came = []
+        for t, x in zip(sz.turns, sums):
             pairs = [
                 (k * bonds + j, (k + 1) % sz.segs * bonds + (j // 2 + t) % half * 2 + j % 2)
-                for k in ([group] if t in alone else range(sz.segs))
+                for k in (range(sz.segs) if t in RINGS and group > 0 else [group])
                 for j in range(bonds)
             ]
-            came[t] = in_vmem(lax.ppermute(sums[t], AXES, pairs))
-        return [came[t] for t in range(half)]
+            came.append(in_vmem(lax.ppermute(x, AXES, pairs)))
+        return came
 
     def add(keep, came):
         rows = keep.shape[1]
@@ -416,7 +423,7 @@
             keep, give = outs[:2]
 
     sums = add(fin[0], swap_cores(fin[1]))
-    parts = [in_vmem(sums[0])] + [to_pair(sums[t], t) for t in range(1, half)]
+    parts = [to_pair(x, t) if t else in_vmem(x) for t, x in zip(sz.turns, sums)]
     tail = pl.pallas_call(
         functools.partial(norm_kernel, sz),
         out_shape=pltpu.VMEM((2, sz.extra), F32),

time: 96 us -> 91.6 us (0.954)
  waiting for transfers between devices: 27.6 us -> 22.2 us
    ppermute x12, waiting for transfers between devices: 10.5 us -> 6.32 us  [hand_over(): came.append(in_vmem(lax.ppermute(x, AXES, pairs)))]
    ppermute x11, waiting for transfers between devices: 17.1 us -> 15.9 us  [permute(): return in_vmem(lax.ppermute(x, AXES, pairs))]
  transfers between devices with their start and end apart: 23 -> 23, of which waited for: 16 -> 14; matrix products, arithmetic and copies ran while one was open for 0% -> 0% of each run, Pallas kernels for 0% -> 0%
where the time goes in v3:
time: 91.6 us; the launch traced here: 91.4 us
  starting transfers between devices  38.7 us (42%)
  Pallas kernels  30.3 us (33%)
  waiting for transfers between devices  22.2 us (24%)
    ppermute x12, starting transfers between devices, hand_over(): came.append(in_vmem(lax.ppermute(x, AXES, pairs)))  30.8 us
    pallas_call x1, Pallas kernels, on_device(): pl.pallas_call(functools.partial(first_kernel, sz), out_shape=(pltpu.VMEM...  22 us
    ppermute x11, waiting for transfers between devices, permute(): return in_vmem(lax.ppermute(x, AXES, pairs))  15.9 us
    ppermute x11, starting transfers between devices, permute(): return in_vmem(lax.ppermute(x, AXES, pairs))  7.92 us
    pallas_call x3, Pallas kernels, on_device(): pl.pallas_call(functools.partial(site_kernel, sz, step), out_shape=shapes...  7.38 us
    ppermute x12, waiting for transfers between devices, hand_over(): came.append(in_vmem(lax.ppermute(x, AXES, pairs)))  6.32 us
  transfers between devices with their start and end apart: 23, of which 14 were waited for; matrix products, arithmetic and copies ran while one was open for 0% of the time, Pallas kernels for 0%

profile of v3, /device:TPU:6, one launch (start us, length us, event | category | flops | bytes accessed | tf_op | source)
XLA Modules:
  0.0 91.4 jit_solution(14910024769447462653)
XLA Ops:
  0.0 22.0 %first_site.1 = (f32[4,2,1152]{2,1,0:T(2,128)S(1)}, f32[4,2,1152]{2,1,0:T(2,128)S(1)}, f32[4,16,1152]{2,1,0:T(8,128)S(1)}, f32[4,16,1152]{2,1,0:T(8,128)S(1)}, s...) custom-call(s32[1,32]{1,0:T(1,128)} %bitcast.6, ...), custom_call_target="tpu_custom_call" | custom-call | tf_op jit(solution)/shard_map/first_site/pallas_call | solution.py:375
  22.0 0.1 collective-permute-start
  22.1 1.2 %collective-permute-done.came = f32[4,2,1152]{2,1,0:T(2,128)S(1)} collective-permute-done((f32[4,2,1152]{2,1,0:T(2,128)S(1)}, f32[4,2,1152]{2,1,0:T(2,128)S(1)}, u32[]{:S(2)}, u32[]{:S(2)}) %collective-permute-start) | collective-permute-done | bytes 36896 | tf_op jit(solution)/shard_map/ppermute | solution.py:340
  23.3 0.7 collective-permute-start.1
  24.0 0.7 collective-permute-start.2
  24.6 0.7 collective-permute-start.3
  25.3 0.7 collective-permute-start.4
  26.0 0.0 collective-permute-done.1.refs_2_
  26.0 0.0 collective-permute-done.2.refs_3_
  26.0 0.0 collective-permute-done.3.refs_4_
  26.0 0.0 collective-permute-done.4.refs_5_
  26.0 0.3 site_1.1
  26.3 0.2 collective-permute-start.5
  26.5 1.1 %collective-permute-done.5.came = f32[4,4,1152]{2,1,0:T(4,128)S(1)} collective-permute-done((f32[4,4,1152]{2,1,0:T(4,128)S(1)}, f32[4,4,1152]{2,1,0:T(4,128)S(1)}, u32[]{:S(2)}, u32[]{:S(2)}) %collective-permute-start.5) | collective-permute-done | bytes 73760 | tf_op jit(solution)/shard_map/ppermute | solution.py:340
  27.6 9.3 %collective-permute-start.6 = (f32[4,1152]{1,0:T(4,128)S(1)}, f32[4,1152]{1,0:T(4,128)S(1)}, u32[]{:S(2)}, u32[]{:S(2)}) collective-permute-start(f32[4,1152]{1,0:T(4,128)S(1)} %get-tuple-element.75), channel_id=1, source_target_pairs={{0,14},{1,15},{2,8},{3,9},{4,10},{5,11},{6,12},{7,13},{8,22},{9,23... | collective-permute-start | bytes 55304 | tf_op jit(solution)/shard_map/ppermute | solution.py:356
  36.9 10.0 %collective-permute-start.7 = (f32[4,1152]{1,0:T(4,128)S(1)}, f32[4,1152]{1,0:T(4,128)S(1)}, u32[]{:S(2)}, u32[]{:S(2)}) collective-permute-start(f32[4,1152]{1,0:T(4,128)S(1)} %get-tuple-element.76), channel_id=1, source_target_pairs={{0,12},{1,13},{2,14},{3,15},{4,8},{5,9},{6,10},{7,11},{8,20},{9,21... | collective-permute-start | bytes 55304 | tf_op jit(solution)/shard_map/ppermute | solution.py:356
  46.9 0.7 collective-permute-start.8
  47.6 0.7 collective-permute-start.9
  48.3 0.0 collective-permute-done.6.refs_2_
  48.3 0.1 collective-permute-done.7.refs_3_
  48.4 0.0 collective-permute-done.8.refs_4_
  48.4 0.0 collective-permute-done.9.refs_5_
  48.4 0.2 site_2.1
  48.6 0.1 collective-permute-start.10
  48.7 1.4 %collective-permute-done.10.came = f32[4,8,1152]{2,1,0:T(8,128)S(1)} collective-permute-done((f32[4,8,1152]{2,1,0:T(8,128)S(1)}, f32[4,8,1152]{2,1,0:T(8,128)S(1)}, u32[]{:S(2)}, u32[]{:S(2)}) %collective-permute-start.10) | collective-permute-done | bytes 147488 | tf_op jit(solution)/shard_map/ppermute | solution.py:340
  50.1 4.9 %collective-permute-start.11 = (f32[8,1152]{1,0:T(8,128)S(1)}, f32[8,1152]{1,0:T(8,128)S(1)}, u32[]{:S(2)}, u32[]{:S(2)}) collective-permute-start(f32[8,1152]{1,0:T(8,128)S(1)} %get-tuple-element.83), channel_id=1, source_target_pairs={{0,14},{1,15},{2,8},{3,9},{4,10},{5,11},{6,12},{7,13},{8,22},{9,23... | collective-permute-start | bytes 110600 | tf_op jit(solution)/shard_map/ppermute | solution.py:356
  55.0 0.1 collective-permute-start.12
  55.1 1.3 %collective-permute-start.13 = (f32[8,1152]{1,0:T(8,128)S(1)}, f32[8,1152]{1,0:T(8,128)S(1)}, u32[]{:S(2)}, u32[]{:S(2)}) collective-permute-start(f32[8,1152]{1,0:T(8,128)S(1)} %get-tuple-element.85), channel_id=1, source_target_pairs={{16,26},{17,27},{18,28},{19,29},{20,30},{21,31},{22,24},{23,25}} | collective-permute-start | bytes 110600 | tf_op jit(solution)/shard_map/ppermute | solution.py:356
  56.3 1.3 %collective-permute-start.14 = (f32[8,1152]{1,0:T(8,128)S(1)}, f32[8,1152]{1,0:T(8,128)S(1)}, u32[]{:S(2)}, u32[]{:S(2)}) collective-permute-start(f32[8,1152]{1,0:T(8,128)S(1)} %get-tuple-element.86), channel_id=1, source_target_pairs={{16,24},{17,25},{18,26},{19,27},{20,28},{21,29},{22,30},{23,31}} | collective-permute-start | bytes 110600 | tf_op jit(solution)/shard_map/ppermute | solution.py:356
  57.6 3.3 %collective-permute-done.11.refs_2_ = f32[8,1152]{1,0:T(8,128)S(1)} collective-permute-done((f32[8,1152]{1,0:T(8,128)S(1)}, f32[8,1152]{1,0:T(8,128)S(1)}, u32[]{:S(2)}, u32[]{:S(2)}) %collective-permute-start.11) | collective-permute-done | bytes 36896 | tf_op jit(solution)/shard_map/ppermute | solution.py:356
  60.9 1.7 %collective-permute-done.12.refs_3_ = f32[8,1152]{1,0:T(8,128)S(1)} collective-permute-done((f32[8,1152]{1,0:T(8,128)S(1)}, f32[8,1152]{1,0:T(8,128)S(1)}, u32[]{:S(2)}, u32[]{:S(2)}) %collective-permute-start.12) | collective-permute-done | bytes 36896 | tf_op jit(solution)/shard_map/ppermute | solution.py:356
  62.7 1.0 %collective-permute-done.13.refs_4_ = f32[8,1152]{1,0:T(8,128)S(1)} collective-permute-done((f32[8,1152]{1,0:T(8,128)S(1)}, f32[8,1152]{1,0:T(8,128)S(1)}, u32[]{:S(2)}, u32[]{:S(2)}) %collective-permute-start.13) | collective-permute-done | bytes 36896 | tf_op jit(solution)/shard_map/ppermute | solution.py:356
  63.7 0.1 collective-permute-done.14.refs_5_
  63.8 6.9 %site_3.1 = (f32[4,16,1152]{2,1,0:T(8,128)S(1)}, f32[4,16,1152]{2,1,0:T(8,128)S(1)}) custom-call(s32[1,32]{1,0:T(1,128)S(1)} %get-tuple-element.51.refs_0_, f32[32,128]{1,0:T(8,128)S(1)} %get-tuple-element.52.refs_1_, f32[8,1152]{1,0:T(8,128)S(1)} %collective-permute-done.11.refs_2_, ...), custom_call_target="tpu_custom_call", output_to_operand_aliasing={{0}: (18, {}), {1}: (19, {})} | custom-call | tf_op jit(solution)/shard_map/site_3/pallas_call | solution.py:406
  70.7 0.1 collective-permute-start.15
  70.8 1.6 %collective-permute-done.15.came = f32[4,16,1152]{2,1,0:T(8,128)S(1)} collective-permute-done((f32[4,16,1152]{2,1,0:T(8,128)S(1)}, f32[4,16,1152]{2,1,0:T(8,128)S(1)}, u32[]{:S(2)}, u32[]{:S(2)}) %collective-permute-start.15) | collective-permute-done | bytes 294944 | tf_op jit(solution)/shard_map/ppermute | solution.py:340
  72.4 1.7 %collective-permute-start.16 = (f32[16,1152]{1,0:T(8,128)S(1)}, f32[16,1152]{1,0:T(8,128)S(1)}, u32[]{:S(2)}, u32[]{:S(2)}) collective-permute-start(f32[16,1152]{1,0:T(8,128)S(1)} %get-tuple-element.91), channel_id=1, source_target_pairs={{0,6},{1,7},{2,0},{3,1},{4,2},{5,3},{6,4},{7,5},{8,14},{9,15},{10,... | collective-permute-start | bytes 221192 | tf_op jit(solution)/shard_map/ppermute | solution.py:340
  74.1 0.4 collective-permute-start.17
  74.5 1.4 %collective-permute-start.18 = (f32[16,1152]{1,0:T(8,128)S(1)}, f32[16,1152]{1,0:T(8,128)S(1)}, u32[]{:S(2)}, u32[]{:S(2)}) collective-permute-start(f32[16,1152]{1,0:T(8,128)S(1)} %get-tuple-element.93), channel_id=1, source_target_pairs={{0,2},{1,3},{2,4},{3,5},{4,6},{5,7},{6,0},{7,1},{8,10},{9,11},{10,... | collective-permute-start | bytes 221192 | tf_op jit(solution)/shard_map/ppermute | solution.py:340
  75.9 0.9 %collective-permute-done.16.refs_0_ = f32[16,1152]{1,0:T(8,128)S(1)} collective-permute-done((f32[16,1152]{1,0:T(8,128)S(1)}, f32[16,1152]{1,0:T(8,128)S(1)}, u32[]{:S(2)}, u32[]{:S(2)}) %collective-permute-start.16) | collective-permute-done | bytes 73760 | tf_op jit(solution)/shard_map/ppermute | solution.py:340
  76.8 5.2 %collective-permute-done.17.refs_1_ = f32[16,1152]{1,0:T(8,128)S(1)} collective-permute-done((f32[16,1152]{1,0:T(8,128)S(1)}, f32[16,1152]{1,0:T(8,128)S(1)}, u32[]{:S(2)}, u32[]{:S(2)}) %collective-permute-start.17) | collective-permute-done | bytes 73760 | tf_op jit(solution)/shard_map/ppermute | solution.py:340
  82.0 0.0 collective-permute-done.18.refs_2_
  82.0 0.1 norms.1.left
  82.1 0.0 collective-permute-start.19
  82.2 1.1 %collective-permute-done.19.right = f32[2,128]{1,0:T(2,128)S(1)} collective-permute-done((f32[2,128]{1,0:T(2,128)S(1)}, f32[2,128]{1,0:T(2,128)S(1)}, u32[]{:S(2)}, u32[]{:S(2)}) %collective-permute-start.19) | collective-permute-done | bytes 1056 | tf_op jit(solution)/shard_map/ppermute | solution.py:340
  83.3 1.4 %collective-permute-start.22 = (f32[2,128]{1,0:T(2,128)S(1)}, f32[2,128]{1,0:T(2,128)S(1)}, u32[]{:S(2)}, u32[]{:S(2)}) collective-permute-start(f32[2,128]{1,0:T(2,128)S(1)} %norms_pair.1.refs_0_), channel_id=1, source_target_pairs={{0,6},{1,7},{2,0},{3,1},{4,2},{5,3},{6,4},{7,5},{8,14},{9,15},{10,... | collective-permute-start | bytes 3080 | tf_op jit(solution)/shard_map/ppermute | solution.py:340
  84.7 0.6 collective-permute-start.21
  85.3 2.0 %collective-permute-start.20 = (f32[2,128]{1,0:T(2,128)S(1)}, f32[2,128]{1,0:T(2,128)S(1)}, u32[]{:S(2)}, u32[]{:S(2)}) collective-permute-start(f32[2,128]{1,0:T(2,128)S(1)} %norms_pair.1.refs_0_), channel_id=1, source_target_pairs={{0,2},{1,3},{2,4},{3,5},{4,6},{5,7},{6,0},{7,1},{8,10},{9,11},{10,... | collective-permute-start | bytes 3080 | tf_op jit(solution)/shard_map/ppermute | solution.py:340
  87.3 0.0 collective-permute-done.22.refs_3_
  87.3 1.9 %collective-permute-done.21.refs_2_ = f32[2,128]{1,0:T(2,128)S(1)} collective-permute-done((f32[2,128]{1,0:T(2,128)S(1)}, f32[2,128]{1,0:T(2,128)S(1)}, u32[]{:S(2)}, u32[]{:S(2)}) %collective-permute-start.21) | collective-permute-done | bytes 1056 | tf_op jit(solution)/shard_map/ppermute | solution.py:340
  89.2 1.5 %collective-permute-done.20.refs_1_ = f32[2,128]{1,0:T(2,128)S(1)} collective-permute-done((f32[2,128]{1,0:T(2,128)S(1)}, f32[2,128]{1,0:T(2,128)S(1)}, u32[]{:S(2)}, u32[]{:S(2)}) %collective-permute-start.20) | collective-permute-done | bytes 1056 | tf_op jit(solution)/shard_map/ppermute | solution.py:340
  90.6 0.7 probs.1
  (5 shorter events, 0.1 us)
Async XLA Ops:
  22.0 1.3 %collective-permute-start = (f32[4,2,1152]{2,1,0:T(2,128)S(1)}, f32[4,2,1152]{2,1,0:T(2,128)S(1)}, u32[]{:S(2)}, u32[]{:S(2)}) collective-permute-start(f32[4,2,1152]{2,1,0:T(2,128)S(1)} %get-tuple-element.54), channel_id=1, source_target_pairs={{0,1},{1,0},{2,3},{3,2},{4,5},{5,4},{6,7},{7,6},{8,9},{9,8},{10,11... | collective-permute-start | bytes 110600 | tf_op jit(solution)/shard_map/ppermute | solution.py:340
  23.3 2.7 %collective-permute-start.1 = (f32[2,1152]{1,0:T(2,128)S(1)}, f32[2,1152]{1,0:T(2,128)S(1)}, u32[]{:S(2)}, u32[]{:S(2)}) collective-permute-start(f32[2,1152]{1,0:T(2,128)S(1)} %get-tuple-element.55), channel_id=1, source_target_pairs={{0,14},{1,15},{2,8},{3,9},{4,10},{5,11},{6,12},{7,13}} | collective-permute-start | bytes 27656 | tf_op jit(solution)/shard_map/ppermute | solution.py:356
  24.0 2.0 %collective-permute-start.2 = (f32[2,1152]{1,0:T(2,128)S(1)}, f32[2,1152]{1,0:T(2,128)S(1)}, u32[]{:S(2)}, u32[]{:S(2)}) collective-permute-start(f32[2,1152]{1,0:T(2,128)S(1)} %get-tuple-element.56), channel_id=1, source_target_pairs={{0,12},{1,13},{2,14},{3,15},{4,8},{5,9},{6,10},{7,11}} | collective-permute-start | bytes 27656 | tf_op jit(solution)/shard_map/ppermute | solution.py:356
  24.6 1.4 %collective-permute-start.3 = (f32[2,1152]{1,0:T(2,128)S(1)}, f32[2,1152]{1,0:T(2,128)S(1)}, u32[]{:S(2)}, u32[]{:S(2)}) collective-permute-start(f32[2,1152]{1,0:T(2,128)S(1)} %get-tuple-element.57), channel_id=1, source_target_pairs={{0,10},{1,11},{2,12},{3,13},{4,14},{5,15},{6,8},{7,9}} | collective-permute-start | bytes 27656 | tf_op jit(solution)/shard_map/ppermute | solution.py:356
  25.3 0.7 collective-permute-start.4
  26.3 1.3 %collective-permute-start.5 = (f32[4,4,1152]{2,1,0:T(4,128)S(1)}, f32[4,4,1152]{2,1,0:T(4,128)S(1)}, u32[]{:S(2)}, u32[]{:S(2)}) collective-permute-start(f32[4,4,1152]{2,1,0:T(4,128)S(1)} %get-tuple-element.74), channel_id=1, source_target_pairs={{0,1},{1,0},{2,3},{3,2},{4,5},{5,4},{6,7},{7,6},{8,9},{9,8},{10,11... | collective-permute-start | bytes 221192 | tf_op jit(solution)/shard_map/ppermute | solution.py:340
  27.6 20.6 %collective-permute-start.6 = (f32[4,1152]{1,0:T(4,128)S(1)}, f32[4,1152]{1,0:T(4,128)S(1)}, u32[]{:S(2)}, u32[]{:S(2)}) collective-permute-start(f32[4,1152]{1,0:T(4,128)S(1)} %get-tuple-element.75), channel_id=1, source_target_pairs={{0,14},{1,15},{2,8},{3,9},{4,10},{5,11},{6,12},{7,13},{8,22},{9,23... | collective-permute-start | bytes 55304 | tf_op jit(solution)/shard_map/ppermute | solution.py:356
  36.9 11.5 %collective-permute-start.7 = (f32[4,1152]{1,0:T(4,128)S(1)}, f32[4,1152]{1,0:T(4,128)S(1)}, u32[]{:S(2)}, u32[]{:S(2)}) collective-permute-start(f32[4,1152]{1,0:T(4,128)S(1)} %get-tuple-element.76), channel_id=1, source_target_pairs={{0,12},{1,13},{2,14},{3,15},{4,8},{5,9},{6,10},{7,11},{8,20},{9,21... | collective-permute-start | bytes 55304 | tf_op jit(solution)/shard_map/ppermute | solution.py:356
  46.9 1.5 %collective-permute-start.8 = (f32[4,1152]{1,0:T(4,128)S(1)}, f32[4,1152]{1,0:T(4,128)S(1)}, u32[]{:S(2)}, u32[]{:S(2)}) collective-permute-start(f32[4,1152]{1,0:T(4,128)S(1)} %get-tuple-element.77), channel_id=1, source_target_pairs={{8,18},{9,19},{10,20},{11,21},{12,22},{13,23},{14,16},{15,17}} | collective-permute-start | bytes 55304 | tf_op jit(solution)/shard_map/ppermute | solution.py:356
  47.6 0.8 collective-permute-start.9
  48.6 1.4 %collective-permute-start.10 = (f32[4,8,1152]{2,1,0:T(8,128)S(1)}, f32[4,8,1152]{2,1,0:T(8,128)S(1)}, u32[]{:S(2)}, u32[]{:S(2)}) collective-permute-start(f32[4,8,1152]{2,1,0:T(8,128)S(1)} %get-tuple-element.82), channel_id=1, source_target_pairs={{0,1},{1,0},{2,3},{3,2},{4,5},{5,4},{6,7},{7,6},{8,9},{9,8},{10,11... | collective-permute-start | bytes 442376 | tf_op jit(solution)/shard_map/ppermute | solution.py:340
  50.1 10.8 %collective-permute-start.11 = (f32[8,1152]{1,0:T(8,128)S(1)}, f32[8,1152]{1,0:T(8,128)S(1)}, u32[]{:S(2)}, u32[]{:S(2)}) collective-permute-start(f32[8,1152]{1,0:T(8,128)S(1)} %get-tuple-element.83), channel_id=1, source_target_pairs={{0,14},{1,15},{2,8},{3,9},{4,10},{5,11},{6,12},{7,13},{8,22},{9,23... | collective-permute-start | bytes 110600 | tf_op jit(solution)/shard_map/ppermute | solution.py:356
  55.0 7.7 %collective-permute-start.12 = (f32[8,1152]{1,0:T(8,128)S(1)}, f32[8,1152]{1,0:T(8,128)S(1)}, u32[]{:S(2)}, u32[]{:S(2)}) collective-permute-start(f32[8,1152]{1,0:T(8,128)S(1)} %get-tuple-element.84), channel_id=1, source_target_pairs={{0,12},{1,13},{2,14},{3,15},{4,8},{5,9},{6,10},{7,11},{8,20},{9,21... | collective-permute-start | bytes 110600 | tf_op jit(solution)/shard_map/ppermute | solution.py:356
  55.1 8.6 %collective-permute-start.13 = (f32[8,1152]{1,0:T(8,128)S(1)}, f32[8,1152]{1,0:T(8,128)S(1)}, u32[]{:S(2)}, u32[]{:S(2)}) collective-permute-start(f32[8,1152]{1,0:T(8,128)S(1)} %get-tuple-element.85), channel_id=1, source_target_pairs={{16,26},{17,27},{18,28},{19,29},{20,30},{21,31},{22,24},{23,25}} | collective-permute-start | bytes 110600 | tf_op jit(solution)/shard_map/ppermute | solution.py:356
  56.3 7.5 %collective-permute-start.14 = (f32[8,1152]{1,0:T(8,128)S(1)}, f32[8,1152]{1,0:T(8,128)S(1)}, u32[]{:S(2)}, u32[]{:S(2)}) collective-permute-start(f32[8,1152]{1,0:T(8,128)S(1)} %get-tuple-element.86), channel_id=1, source_target_pairs={{16,24},{17,25},{18,26},{19,27},{20,28},{21,29},{22,30},{23,31}} | collective-permute-start | bytes 110600 | tf_op jit(solution)/shard_map/ppermute | solution.py:356
  70.7 1.6 %collective-permute-start.15 = (f32[4,16,1152]{2,1,0:T(8,128)S(1)}, f32[4,16,1152]{2,1,0:T(8,128)S(1)}, u32[]{:S(2)}, u32[]{:S(2)}) collective-permute-start(f32[4,16,1152]{2,1,0:T(8,128)S(1)} %get-tuple-element.90), channel_id=1, source_target_pairs={{0,1},{1,0},{2,3},{3,2},{4,5},{5,4},{6,7},{7,6},{8,9},{9,8},{10,11... | collective-permute-start | bytes 884744 | tf_op jit(solution)/shard_map/ppermute | solution.py:340
  72.4 4.4 %collective-permute-start.16 = (f32[16,1152]{1,0:T(8,128)S(1)}, f32[16,1152]{1,0:T(8,128)S(1)}, u32[]{:S(2)}, u32[]{:S(2)}) collective-permute-start(f32[16,1152]{1,0:T(8,128)S(1)} %get-tuple-element.91), channel_id=1, source_target_pairs={{0,6},{1,7},{2,0},{3,1},{4,2},{5,3},{6,4},{7,5},{8,14},{9,15},{10,... | collective-permute-start | bytes 221192 | tf_op jit(solution)/shard_map/ppermute | solution.py:340
  74.1 8.0 %collective-permute-start.17 = (f32[16,1152]{1,0:T(8,128)S(1)}, f32[16,1152]{1,0:T(8,128)S(1)}, u32[]{:S(2)}, u32[]{:S(2)}) collective-permute-start(f32[16,1152]{1,0:T(8,128)S(1)} %get-tuple-element.92), channel_id=1, source_target_pairs={{0,4},{1,5},{2,6},{3,7},{4,0},{5,1},{6,2},{7,3},{8,12},{9,13},{10,... | collective-permute-start | bytes 221192 | tf_op jit(solution)/shard_map/ppermute | solution.py:340
  74.5 7.6 %collective-permute-start.18 = (f32[16,1152]{1,0:T(8,128)S(1)}, f32[16,1152]{1,0:T(8,128)S(1)}, u32[]{:S(2)}, u32[]{:S(2)}) collective-permute-start(f32[16,1152]{1,0:T(8,128)S(1)} %get-tuple-element.93), channel_id=1, source_target_pairs={{0,2},{1,3},{2,4},{3,5},{4,6},{5,7},{6,0},{7,1},{8,10},{9,11},{10,... | collective-permute-start | bytes 221192 | tf_op jit(solution)/shard_map/ppermute | solution.py:340
  82.1 1.1 %collective-permute-start.19 = (f32[2,128]{1,0:T(2,128)S(1)}, f32[2,128]{1,0:T(2,128)S(1)}, u32[]{:S(2)}, u32[]{:S(2)}) collective-permute-start(f32[2,128]{1,0:T(2,128)S(1)} %norms.1.left), channel_id=1, source_target_pairs={{0,1},{1,0},{2,3},{3,2},{4,5},{5,4},{6,7},{7,6},{8,9},{9,8},{10,11... | collective-permute-start | bytes 3080 | tf_op jit(solution)/shard_map/ppermute | solution.py:340
  83.3 4.0 %collective-permute-start.22 = (f32[2,128]{1,0:T(2,128)S(1)}, f32[2,128]{1,0:T(2,128)S(1)}, u32[]{:S(2)}, u32[]{:S(2)}) collective-permute-start(f32[2,128]{1,0:T(2,128)S(1)} %norms_pair.1.refs_0_), channel_id=1, source_target_pairs={{0,6},{1,7},{2,0},{3,1},{4,2},{5,3},{6,4},{7,5},{8,14},{9,15},{10,... | collective-permute-start | bytes 3080 | tf_op jit(solution)/shard_map/ppermute | solution.py:340
  84.7 4.5 %collective-permute-start.21 = (f32[2,128]{1,0:T(2,128)S(1)}, f32[2,128]{1,0:T(2,128)S(1)}, u32[]{:S(2)}, u32[]{:S(2)}) collective-permute-start(f32[2,128]{1,0:T(2,128)S(1)} %norms_pair.1.refs_0_), channel_id=1, source_target_pairs={{0,4},{1,5},{2,6},{3,7},{4,0},{5,1},{6,2},{7,3},{8,12},{9,13},{10,... | collective-permute-start | bytes 3080 | tf_op jit(solution)/shard_map/ppermute | solution.py:340
  85.3 5.4 %collective-permute-start.20 = (f32[2,128]{1,0:T(2,128)S(1)}, f32[2,128]{1,0:T(2,128)S(1)}, u32[]{:S(2)}, u32[]{:S(2)}) collective-permute-start(f32[2,128]{1,0:T(2,128)S(1)} %norms_pair.1.refs_0_), channel_id=1, source_target_pairs={{0,2},{1,3},{2,4},{3,5},{4,6},{5,7},{6,0},{7,1},{8,10},{9,11},{10,... | collective-permute-start | bytes 3080 | tf_op jit(solution)/shard_map/ppermute | solution.py:340

commit v4 on v3

--- a/solution.py
+++ b/solution.py
@@ -14,6 +14,7 @@
 BLOCK = 2048
 RING = 4
 RINGS = (3, 2)
+INNER = (1, 3, 2)
 SCOPE = 43 * MIB // 4
 F32 = jnp.float32
 BF16 = jnp.bfloat16
@@ -33,6 +34,8 @@
         self.half = self.bonds // 2
         near = [t for t in reversed(range(self.half)) if t not in RINGS]
         self.turns = [t for t in RINGS if t < self.half] + near
+        assert self.half & (self.half - 1) == 0
+        self.inner = sorted(range(1, self.half), key=lambda m: INNER.index(m) if m in INNER else -1)
         self.left, self.right = sites.shape[2], sites.shape[3]
         self.chunk = self.right // self.bonds
         assert self.chunk == self.left and self.bonds % 2 == 0
@@ -261,10 +264,13 @@
         fin_give[...] = old_give[...]
 
 
-def add_kernel(sz, keep, came, *outs):
+def add_kernel(sz, ahead, keep, came, *outs):
     pair = lax.axis_index("bond") // 2
-    for t, out in zip(sz.turns, outs):
-        target = lax.rem(pair + t, sz.half)
+    if ahead:
+        targets = [lax.rem(pair + t, sz.half) for t in sz.turns]
+    else:
+        targets = [lax.bitwise_xor(pair, m) for m in [*sz.inner, 0]]
+    for target, out in zip(targets, outs):
         out[...] = keep[target] + came[target]
 
 
@@ -342,8 +348,8 @@
     def swap_cores(x):
         return permute(x, lambda k, j: k * bonds + (j ^ 1))
 
-    def to_pair(x, t):
-        return permute(x, lambda k, j: k * bonds + (j // 2 + t) % half * 2 + j % 2)
+    def to_pair(x, m):
+        return permute(x, lambda k, j: k * bonds + (j // 2 ^ m) * 2 + j % 2)
 
     def hand_over(sums, group):
         came = []
@@ -356,10 +362,10 @@
             came.append(in_vmem(lax.ppermute(x, AXES, pairs)))
         return came
 
-    def add(keep, came):
+    def add(keep, came, ahead):
         rows = keep.shape[1]
         return pl.pallas_call(
-            functools.partial(add_kernel, sz),
+            functools.partial(add_kernel, sz, ahead),
             out_shape=(pltpu.VMEM((rows, sz.width), F32),) * half,
             in_specs=[VMEM, VMEM],
             out_specs=(VMEM,) * half,
@@ -397,7 +403,7 @@
     held = outs[7:]
 
     for step in range(1, sz.segs):
-        sums = add(keep, swap_cores(give))
+        sums = add(keep, swap_cores(give), True)
         messages = hand_over(sums, step - 1)
         rows = 2**step
         last = step == sz.segs - 1
@@ -422,8 +428,8 @@
         if not last:
             keep, give = outs[:2]
 
-    sums = add(fin[0], swap_cores(fin[1]))
-    parts = [to_pair(x, t) if t else in_vmem(x) for t, x in zip(sz.turns, sums)]
+    sums = add(fin[0], swap_cores(fin[1]), False)
+    parts = [to_pair(x, m) for m, x in zip(sz.inner, sums)] + [in_vmem(sums[-1])]
     tail = pl.pallas_call(
         functools.partial(norm_kernel, sz),
         out_shape=pltpu.VMEM((2, sz.extra), F32),
@@ -440,7 +446,7 @@
         compiler_params=params(MIB),
         name="norms_pair",
     )(in_vmem(tail), swap_cores(tail))
-    parts = [in_vmem(tail)] + [to_pair(tail, t) for t in range(1, half)]
+    parts = [in_vmem(tail)] + [to_pair(tail, m) for m in sz.inner]
     probs = pl.pallas_call(
         functools.partial(final_kernel, sz),
         out_shape=shape_of(1, sz.rows),

time: 91.6 us -> 90.6 us (0.989)
  transfers between devices with their start and end apart: 23 -> 23, of which waited for: 14 -> 15; matrix products, arithmetic and copies ran while one was open for 0% -> 0% of each run, Pallas kernels for 0% -> 0%
where the time goes in v4:
time: 90.6 us; the launch traced here: 90.2 us
  starting transfers between devices  38.3 us (42%)
  Pallas kernels  30.3 us (33%)
  waiting for transfers between devices  21.5 us (24%)
    ppermute x12, starting transfers between devices, hand_over(): came.append(in_vmem(lax.ppermute(x, AXES, pairs)))  30.8 us
    pallas_call x1, Pallas kernels, on_device(): pl.pallas_call(functools.partial(first_kernel, sz), out_shape=(pltpu.VMEM...  22 us
    ppermute x11, waiting for transfers between devices, permute(): return in_vmem(lax.ppermute(x, AXES, pairs))  15.2 us
    ppermute x11, starting transfers between devices, permute(): return in_vmem(lax.ppermute(x, AXES, pairs))  7.48 us
    pallas_call x3, Pallas kernels, on_device(): pl.pallas_call(functools.partial(site_kernel, sz, step), out_shape=shapes...  7.38 us
    ppermute x12, waiting for transfers between devices, hand_over(): came.append(in_vmem(lax.ppermute(x, AXES, pairs)))  6.32 us
  transfers between devices with their start and end apart: 23, of which 15 were waited for; matrix products, arithmetic and copies ran while one was open for 0% of the time, Pallas kernels for 0%

profile of v4, /device:TPU:6, one launch (start us, length us, event | category | flops | bytes accessed | tf_op | source)
XLA Modules:
  0.0 90.2 jit_solution(6117955647605753264)
XLA Ops:
  0.0 22.0 %first_site.1 = (f32[4,2,1152]{2,1,0:T(2,128)S(1)}, f32[4,2,1152]{2,1,0:T(2,128)S(1)}, f32[4,16,1152]{2,1,0:T(8,128)S(1)}, f32[4,16,1152]{2,1,0:T(8,128)S(1)}, s...) custom-call(s32[1,32]{1,0:T(1,128)} %bitcast.6, ...), custom_call_target="tpu_custom_call" | custom-call | tf_op jit(solution)/shard_map/first_site/pallas_call | solution.py:381
  22.0 0.1 collective-permute-start
  22.1 1.2 %collective-permute-done.came = f32[4,2,1152]{2,1,0:T(2,128)S(1)} collective-permute-done((f32[4,2,1152]{2,1,0:T(2,128)S(1)}, f32[4,2,1152]{2,1,0:T(2,128)S(1)}, u32[]{:S(2)}, u32[]{:S(2)}) %collective-permute-start) | collective-permute-done | bytes 36896 | tf_op jit(solution)/shard_map/ppermute | solution.py:346
  23.3 0.7 collective-permute-start.1
  24.0 0.7 collective-permute-start.2
  24.6 0.7 collective-permute-start.3
  25.3 0.7 collective-permute-start.4
  26.0 0.0 collective-permute-done.1.refs_2_
  26.0 0.0 collective-permute-done.2.refs_3_
  26.0 0.0 collective-permute-done.3.refs_4_
  26.0 0.0 collective-permute-done.4.refs_5_
  26.0 0.3 site_1.1
  26.3 0.2 collective-permute-start.5
  26.5 1.1 %collective-permute-done.5.came = f32[4,4,1152]{2,1,0:T(4,128)S(1)} collective-permute-done((f32[4,4,1152]{2,1,0:T(4,128)S(1)}, f32[4,4,1152]{2,1,0:T(4,128)S(1)}, u32[]{:S(2)}, u32[]{:S(2)}) %collective-permute-start.5) | collective-permute-done | bytes 73760 | tf_op jit(solution)/shard_map/ppermute | solution.py:346
  27.6 9.3 %collective-permute-start.6 = (f32[4,1152]{1,0:T(4,128)S(1)}, f32[4,1152]{1,0:T(4,128)S(1)}, u32[]{:S(2)}, u32[]{:S(2)}) collective-permute-start(f32[4,1152]{1,0:T(4,128)S(1)} %get-tuple-element.75), channel_id=1, source_target_pairs={{0,14},{1,15},{2,8},{3,9},{4,10},{5,11},{6,12},{7,13},{8,22},{9,23... | collective-permute-start | bytes 55304 | tf_op jit(solution)/shard_map/ppermute | solution.py:362
  36.9 10.0 %collective-permute-start.7 = (f32[4,1152]{1,0:T(4,128)S(1)}, f32[4,1152]{1,0:T(4,128)S(1)}, u32[]{:S(2)}, u32[]{:S(2)}) collective-permute-start(f32[4,1152]{1,0:T(4,128)S(1)} %get-tuple-element.76), channel_id=1, source_target_pairs={{0,12},{1,13},{2,14},{3,15},{4,8},{5,9},{6,10},{7,11},{8,20},{9,21... | collective-permute-start | bytes 55304 | tf_op jit(solution)/shard_map/ppermute | solution.py:362
  46.9 0.7 collective-permute-start.8
  47.6 0.7 collective-permute-start.9
  48.3 0.0 collective-permute-done.6.refs_2_
  48.3 0.1 collective-permute-done.7.refs_3_
  48.4 0.0 collective-permute-done.8.refs_4_
  48.4 0.0 collective-permute-done.9.refs_5_
  48.4 0.2 site_2.1
  48.6 0.1 collective-permute-start.10
  48.7 1.4 %collective-permute-done.10.came = f32[4,8,1152]{2,1,0:T(8,128)S(1)} collective-permute-done((f32[4,8,1152]{2,1,0:T(8,128)S(1)}, f32[4,8,1152]{2,1,0:T(8,128)S(1)}, u32[]{:S(2)}, u32[]{:S(2)}) %collective-permute-start.10) | collective-permute-done | bytes 147488 | tf_op jit(solution)/shard_map/ppermute | solution.py:346
  50.1 4.9 %collective-permute-start.11 = (f32[8,1152]{1,0:T(8,128)S(1)}, f32[8,1152]{1,0:T(8,128)S(1)}, u32[]{:S(2)}, u32[]{:S(2)}) collective-permute-start(f32[8,1152]{1,0:T(8,128)S(1)} %get-tuple-element.83), channel_id=1, source_target_pairs={{0,14},{1,15},{2,8},{3,9},{4,10},{5,11},{6,12},{7,13},{8,22},{9,23... | collective-permute-start | bytes 110600 | tf_op jit(solution)/shard_map/ppermute | solution.py:362
  55.0 0.1 collective-permute-start.12
  55.1 1.3 %collective-permute-start.13 = (f32[8,1152]{1,0:T(8,128)S(1)}, f32[8,1152]{1,0:T(8,128)S(1)}, u32[]{:S(2)}, u32[]{:S(2)}) collective-permute-start(f32[8,1152]{1,0:T(8,128)S(1)} %get-tuple-element.85), channel_id=1, source_target_pairs={{16,26},{17,27},{18,28},{19,29},{20,30},{21,31},{22,24},{23,25}} | collective-permute-start | bytes 110600 | tf_op jit(solution)/shard_map/ppermute | solution.py:362
  56.3 1.3 %collective-permute-start.14 = (f32[8,1152]{1,0:T(8,128)S(1)}, f32[8,1152]{1,0:T(8,128)S(1)}, u32[]{:S(2)}, u32[]{:S(2)}) collective-permute-start(f32[8,1152]{1,0:T(8,128)S(1)} %get-tuple-element.86), channel_id=1, source_target_pairs={{16,24},{17,25},{18,26},{19,27},{20,28},{21,29},{22,30},{23,31}} | collective-permute-start | bytes 110600 | tf_op jit(solution)/shard_map/ppermute | solution.py:362
  57.6 3.3 %collective-permute-done.11.refs_2_ = f32[8,1152]{1,0:T(8,128)S(1)} collective-permute-done((f32[8,1152]{1,0:T(8,128)S(1)}, f32[8,1152]{1,0:T(8,128)S(1)}, u32[]{:S(2)}, u32[]{:S(2)}) %collective-permute-start.11) | collective-permute-done | bytes 36896 | tf_op jit(solution)/shard_map/ppermute | solution.py:362
  60.9 1.7 %collective-permute-done.12.refs_3_ = f32[8,1152]{1,0:T(8,128)S(1)} collective-permute-done((f32[8,1152]{1,0:T(8,128)S(1)}, f32[8,1152]{1,0:T(8,128)S(1)}, u32[]{:S(2)}, u32[]{:S(2)}) %collective-permute-start.12) | collective-permute-done | bytes 36896 | tf_op jit(solution)/shard_map/ppermute | solution.py:362
  62.7 1.0 %collective-permute-done.13.refs_4_ = f32[8,1152]{1,0:T(8,128)S(1)} collective-permute-done((f32[8,1152]{1,0:T(8,128)S(1)}, f32[8,1152]{1,0:T(8,128)S(1)}, u32[]{:S(2)}, u32[]{:S(2)}) %collective-permute-start.13) | collective-permute-done | bytes 36896 | tf_op jit(solution)/shard_map/ppermute | solution.py:362
  63.7 0.1 collective-permute-done.14.refs_5_
  63.8 6.9 %site_3.1 = (f32[4,16,1152]{2,1,0:T(8,128)S(1)}, f32[4,16,1152]{2,1,0:T(8,128)S(1)}) custom-call(s32[1,32]{1,0:T(1,128)S(1)} %get-tuple-element.51.refs_0_, f32[32,128]{1,0:T(8,128)S(1)} %get-tuple-element.52.refs_1_, f32[8,1152]{1,0:T(8,128)S(1)} %collective-permute-done.11.refs_2_, ...), custom_call_target="tpu_custom_call", output_to_operand_aliasing={{0}: (18, {}), {1}: (19, {})} | custom-call | tf_op jit(solution)/shard_map/site_3/pallas_call | solution.py:412
  70.7 0.1 collective-permute-start.15
  70.8 1.6 %collective-permute-done.15.came = f32[4,16,1152]{2,1,0:T(8,128)S(1)} collective-permute-done((f32[4,16,1152]{2,1,0:T(8,128)S(1)}, f32[4,16,1152]{2,1,0:T(8,128)S(1)}, u32[]{:S(2)}, u32[]{:S(2)}) %collective-permute-start.15) | collective-permute-done | bytes 294944 | tf_op jit(solution)/shard_map/ppermute | solution.py:346
  72.4 0.6 collective-permute-start.16
  73.0 2.3 %collective-permute-start.17 = (f32[16,1152]{1,0:T(8,128)S(1)}, f32[16,1152]{1,0:T(8,128)S(1)}, u32[]{:S(2)}, u32[]{:S(2)}) collective-permute-start(f32[16,1152]{1,0:T(8,128)S(1)} %get-tuple-element.92), channel_id=1, source_target_pairs={{0,6},{1,7},{2,4},{3,5},{4,2},{5,3},{6,0},{7,1},{8,14},{9,15},{10,... | collective-permute-start | bytes 221192 | tf_op jit(solution)/shard_map/ppermute | solution.py:346
  75.3 0.6 collective-permute-start.18
  75.9 0.9 collective-permute-done.16.refs_0_
  76.8 3.3 %collective-permute-done.17.refs_1_ = f32[16,1152]{1,0:T(8,128)S(1)} collective-permute-done((f32[16,1152]{1,0:T(8,128)S(1)}, f32[16,1152]{1,0:T(8,128)S(1)}, u32[]{:S(2)}, u32[]{:S(2)}) %collective-permute-start.17) | collective-permute-done | bytes 73760 | tf_op jit(solution)/shard_map/ppermute | solution.py:346
  80.1 2.8 %collective-permute-done.18.refs_2_ = f32[16,1152]{1,0:T(8,128)S(1)} collective-permute-done((f32[16,1152]{1,0:T(8,128)S(1)}, f32[16,1152]{1,0:T(8,128)S(1)}, u32[]{:S(2)}, u32[]{:S(2)}) %collective-permute-start.18) | collective-permute-done | bytes 73760 | tf_op jit(solution)/shard_map/ppermute | solution.py:346
  82.9 0.1 norms.1.left
  83.0 0.0 collective-permute-start.19
  83.0 1.1 %collective-permute-done.19.right = f32[2,128]{1,0:T(2,128)S(1)} collective-permute-done((f32[2,128]{1,0:T(2,128)S(1)}, f32[2,128]{1,0:T(2,128)S(1)}, u32[]{:S(2)}, u32[]{:S(2)}) %collective-permute-start.19) | collective-permute-done | bytes 1056 | tf_op jit(solution)/shard_map/ppermute | solution.py:346
  84.1 0.0 collective-permute-start.22
  84.1 1.8 %collective-permute-start.21 = (f32[2,128]{1,0:T(2,128)S(1)}, f32[2,128]{1,0:T(2,128)S(1)}, u32[]{:S(2)}, u32[]{:S(2)}) collective-permute-start(f32[2,128]{1,0:T(2,128)S(1)} %norms_pair.1.refs_0_), channel_id=1, source_target_pairs={{0,6},{1,7},{2,4},{3,5},{4,2},{5,3},{6,0},{7,1},{8,14},{9,15},{10,... | collective-permute-start | bytes 3080 | tf_op jit(solution)/shard_map/ppermute | solution.py:346
  85.9 1.7 %collective-permute-start.20 = (f32[2,128]{1,0:T(2,128)S(1)}, f32[2,128]{1,0:T(2,128)S(1)}, u32[]{:S(2)}, u32[]{:S(2)}) collective-permute-start(f32[2,128]{1,0:T(2,128)S(1)} %norms_pair.1.refs_0_), channel_id=1, source_target_pairs={{0,2},{1,3},{2,0},{3,1},{4,6},{5,7},{6,4},{7,5},{8,10},{9,11},{10,... | collective-permute-start | bytes 3080 | tf_op jit(solution)/shard_map/ppermute | solution.py:346
  87.6 1.0 %collective-permute-done.22.refs_3_ = f32[2,128]{1,0:T(2,128)S(1)} collective-permute-done((f32[2,128]{1,0:T(2,128)S(1)}, f32[2,128]{1,0:T(2,128)S(1)}, u32[]{:S(2)}, u32[]{:S(2)}) %collective-permute-start.22) | collective-permute-done | bytes 1056 | tf_op jit(solution)/shard_map/ppermute | solution.py:346
  88.6 0.9 collective-permute-done.21.refs_2_
  89.5 0.0 collective-permute-done.20.refs_1_
  89.5 0.7 probs.1
  (5 shorter events, 0.1 us)
Async XLA Ops:
  22.0 1.3 %collective-permute-start = (f32[4,2,1152]{2,1,0:T(2,128)S(1)}, f32[4,2,1152]{2,1,0:T(2,128)S(1)}, u32[]{:S(2)}, u32[]{:S(2)}) collective-permute-start(f32[4,2,1152]{2,1,0:T(2,128)S(1)} %get-tuple-element.54), channel_id=1, source_target_pairs={{0,1},{1,0},{2,3},{3,2},{4,5},{5,4},{6,7},{7,6},{8,9},{9,8},{10,11... | collective-permute-start | bytes 110600 | tf_op jit(solution)/shard_map/ppermute | solution.py:346
  23.3 2.7 %collective-permute-start.1 = (f32[2,1152]{1,0:T(2,128)S(1)}, f32[2,1152]{1,0:T(2,128)S(1)}, u32[]{:S(2)}, u32[]{:S(2)}) collective-permute-start(f32[2,1152]{1,0:T(2,128)S(1)} %get-tuple-element.55), channel_id=1, source_target_pairs={{0,14},{1,15},{2,8},{3,9},{4,10},{5,11},{6,12},{7,13}} | collective-permute-start | bytes 27656 | tf_op jit(solution)/shard_map/ppermute | solution.py:362
  24.0 2.0 %collective-permute-start.2 = (f32[2,1152]{1,0:T(2,128)S(1)}, f32[2,1152]{1,0:T(2,128)S(1)}, u32[]{:S(2)}, u32[]{:S(2)}) collective-permute-start(f32[2,1152]{1,0:T(2,128)S(1)} %get-tuple-element.56), channel_id=1, source_target_pairs={{0,12},{1,13},{2,14},{3,15},{4,8},{5,9},{6,10},{7,11}} | collective-permute-start | bytes 27656 | tf_op jit(solution)/shard_map/ppermute | solution.py:362
  24.6 1.4 %collective-permute-start.3 = (f32[2,1152]{1,0:T(2,128)S(1)}, f32[2,1152]{1,0:T(2,128)S(1)}, u32[]{:S(2)}, u32[]{:S(2)}) collective-permute-start(f32[2,1152]{1,0:T(2,128)S(1)} %get-tuple-element.57), channel_id=1, source_target_pairs={{0,10},{1,11},{2,12},{3,13},{4,14},{5,15},{6,8},{7,9}} | collective-permute-start | bytes 27656 | tf_op jit(solution)/shard_map/ppermute | solution.py:362
  25.3 0.7 collective-permute-start.4
  26.3 1.3 %collective-permute-start.5 = (f32[4,4,1152]{2,1,0:T(4,128)S(1)}, f32[4,4,1152]{2,1,0:T(4,128)S(1)}, u32[]{:S(2)}, u32[]{:S(2)}) collective-permute-start(f32[4,4,1152]{2,1,0:T(4,128)S(1)} %get-tuple-element.74), channel_id=1, source_target_pairs={{0,1},{1,0},{2,3},{3,2},{4,5},{5,4},{6,7},{7,6},{8,9},{9,8},{10,11... | collective-permute-start | bytes 221192 | tf_op jit(solution)/shard_map/ppermute | solution.py:346
  27.6 20.6 %collective-permute-start.6 = (f32[4,1152]{1,0:T(4,128)S(1)}, f32[4,1152]{1,0:T(4,128)S(1)}, u32[]{:S(2)}, u32[]{:S(2)}) collective-permute-start(f32[4,1152]{1,0:T(4,128)S(1)} %get-tuple-element.75), channel_id=1, source_target_pairs={{0,14},{1,15},{2,8},{3,9},{4,10},{5,11},{6,12},{7,13},{8,22},{9,23... | collective-permute-start | bytes 55304 | tf_op jit(solution)/shard_map/ppermute | solution.py:362
  36.9 11.5 %collective-permute-start.7 = (f32[4,1152]{1,0:T(4,128)S(1)}, f32[4,1152]{1,0:T(4,128)S(1)}, u32[]{:S(2)}, u32[]{:S(2)}) collective-permute-start(f32[4,1152]{1,0:T(4,128)S(1)} %get-tuple-element.76), channel_id=1, source_target_pairs={{0,12},{1,13},{2,14},{3,15},{4,8},{5,9},{6,10},{7,11},{8,20},{9,21... | collective-permute-start | bytes 55304 | tf_op jit(solution)/shard_map/ppermute | solution.py:362
  46.9 1.5 %collective-permute-start.8 = (f32[4,1152]{1,0:T(4,128)S(1)}, f32[4,1152]{1,0:T(4,128)S(1)}, u32[]{:S(2)}, u32[]{:S(2)}) collective-permute-start(f32[4,1152]{1,0:T(4,128)S(1)} %get-tuple-element.77), channel_id=1, source_target_pairs={{8,18},{9,19},{10,20},{11,21},{12,22},{13,23},{14,16},{15,17}} | collective-permute-start | bytes 55304 | tf_op jit(solution)/shard_map/ppermute | solution.py:362
  47.6 0.8 collective-permute-start.9
  48.6 1.4 %collective-permute-start.10 = (f32[4,8,1152]{2,1,0:T(8,128)S(1)}, f32[4,8,1152]{2,1,0:T(8,128)S(1)}, u32[]{:S(2)}, u32[]{:S(2)}) collective-permute-start(f32[4,8,1152]{2,1,0:T(8,128)S(1)} %get-tuple-element.82), channel_id=1, source_target_pairs={{0,1},{1,0},{2,3},{3,2},{4,5},{5,4},{6,7},{7,6},{8,9},{9,8},{10,11... | collective-permute-start | bytes 442376 | tf_op jit(solution)/shard_map/ppermute | solution.py:346
  50.1 10.8 %collective-permute-start.11 = (f32[8,1152]{1,0:T(8,128)S(1)}, f32[8,1152]{1,0:T(8,128)S(1)}, u32[]{:S(2)}, u32[]{:S(2)}) collective-permute-start(f32[8,1152]{1,0:T(8,128)S(1)} %get-tuple-element.83), channel_id=1, source_target_pairs={{0,14},{1,15},{2,8},{3,9},{4,10},{5,11},{6,12},{7,13},{8,22},{9,23... | collective-permute-start | bytes 110600 | tf_op jit(solution)/shard_map/ppermute | solution.py:362
  55.0 7.7 %collective-permute-start.12 = (f32[8,1152]{1,0:T(8,128)S(1)}, f32[8,1152]{1,0:T(8,128)S(1)}, u32[]{:S(2)}, u32[]{:S(2)}) collective-permute-start(f32[8,1152]{1,0:T(8,128)S(1)} %get-tuple-element.84), channel_id=1, source_target_pairs={{0,12},{1,13},{2,14},{3,15},{4,8},{5,9},{6,10},{7,11},{8,20},{9,21... | collective-permute-start | bytes 110600 | tf_op jit(solution)/shard_map/ppermute | solution.py:362
  55.1 8.6 %collective-permute-start.13 = (f32[8,1152]{1,0:T(8,128)S(1)}, f32[8,1152]{1,0:T(8,128)S(1)}, u32[]{:S(2)}, u32[]{:S(2)}) collective-permute-start(f32[8,1152]{1,0:T(8,128)S(1)} %get-tuple-element.85), channel_id=1, source_target_pairs={{16,26},{17,27},{18,28},{19,29},{20,30},{21,31},{22,24},{23,25}} | collective-permute-start | bytes 110600 | tf_op jit(solution)/shard_map/ppermute | solution.py:362
  56.3 7.5 %collective-permute-start.14 = (f32[8,1152]{1,0:T(8,128)S(1)}, f32[8,1152]{1,0:T(8,128)S(1)}, u32[]{:S(2)}, u32[]{:S(2)}) collective-permute-start(f32[8,1152]{1,0:T(8,128)S(1)} %get-tuple-element.86), channel_id=1, source_target_pairs={{16,24},{17,25},{18,26},{19,27},{20,28},{21,29},{22,30},{23,31}} | collective-permute-start | bytes 110600 | tf_op jit(solution)/shard_map/ppermute | solution.py:362
  70.7 1.6 %collective-permute-start.15 = (f32[4,16,1152]{2,1,0:T(8,128)S(1)}, f32[4,16,1152]{2,1,0:T(8,128)S(1)}, u32[]{:S(2)}, u32[]{:S(2)}) collective-permute-start(f32[4,16,1152]{2,1,0:T(8,128)S(1)} %get-tuple-element.90), channel_id=1, source_target_pairs={{0,1},{1,0},{2,3},{3,2},{4,5},{5,4},{6,7},{7,6},{8,9},{9,8},{10,11... | collective-permute-start | bytes 884744 | tf_op jit(solution)/shard_map/ppermute | solution.py:346
  72.4 4.4 %collective-permute-start.16 = (f32[16,1152]{1,0:T(8,128)S(1)}, f32[16,1152]{1,0:T(8,128)S(1)}, u32[]{:S(2)}, u32[]{:S(2)}) collective-permute-start(f32[16,1152]{1,0:T(8,128)S(1)} %get-tuple-element.91), channel_id=1, source_target_pairs={{0,2},{1,3},{2,0},{3,1},{4,6},{5,7},{6,4},{7,5},{8,10},{9,11},{10,... | collective-permute-start | bytes 221192 | tf_op jit(solution)/shard_map/ppermute | solution.py:346
  73.0 7.1 %collective-permute-start.17 = (f32[16,1152]{1,0:T(8,128)S(1)}, f32[16,1152]{1,0:T(8,128)S(1)}, u32[]{:S(2)}, u32[]{:S(2)}) collective-permute-start(f32[16,1152]{1,0:T(8,128)S(1)} %get-tuple-element.92), channel_id=1, source_target_pairs={{0,6},{1,7},{2,4},{3,5},{4,2},{5,3},{6,0},{7,1},{8,14},{9,15},{10,... | collective-permute-start | bytes 221192 | tf_op jit(solution)/shard_map/ppermute | solution.py:346
  75.3 7.6 %collective-permute-start.18 = (f32[16,1152]{1,0:T(8,128)S(1)}, f32[16,1152]{1,0:T(8,128)S(1)}, u32[]{:S(2)}, u32[]{:S(2)}) collective-permute-start(f32[16,1152]{1,0:T(8,128)S(1)} %get-tuple-element.93), channel_id=1, source_target_pairs={{0,4},{1,5},{2,6},{3,7},{4,0},{5,1},{6,2},{7,3},{8,12},{9,13},{10,... | collective-permute-start | bytes 221192 | tf_op jit(solution)/shard_map/ppermute | solution.py:346
  83.0 1.1 %collective-permute-start.19 = (f32[2,128]{1,0:T(2,128)S(1)}, f32[2,128]{1,0:T(2,128)S(1)}, u32[]{:S(2)}, u32[]{:S(2)}) collective-permute-start(f32[2,128]{1,0:T(2,128)S(1)} %norms.1.left), channel_id=1, source_target_pairs={{0,1},{1,0},{2,3},{3,2},{4,5},{5,4},{6,7},{7,6},{8,9},{9,8},{10,11... | collective-permute-start | bytes 3080 | tf_op jit(solution)/shard_map/ppermute | solution.py:346
  84.1 4.5 %collective-permute-start.22 = (f32[2,128]{1,0:T(2,128)S(1)}, f32[2,128]{1,0:T(2,128)S(1)}, u32[]{:S(2)}, u32[]{:S(2)}) collective-permute-start(f32[2,128]{1,0:T(2,128)S(1)} %norms_pair.1.refs_0_), channel_id=1, source_target_pairs={{0,4},{1,5},{2,6},{3,7},{4,0},{5,1},{6,2},{7,3},{8,12},{9,13},{10,... | collective-permute-start | bytes 3080 | tf_op jit(solution)/shard_map/ppermute | solution.py:346
  84.1 5.4 %collective-permute-start.21 = (f32[2,128]{1,0:T(2,128)S(1)}, f32[2,128]{1,0:T(2,128)S(1)}, u32[]{:S(2)}, u32[]{:S(2)}) collective-permute-start(f32[2,128]{1,0:T(2,128)S(1)} %norms_pair.1.refs_0_), channel_id=1, source_target_pairs={{0,6},{1,7},{2,4},{3,5},{4,2},{5,3},{6,0},{7,1},{8,14},{9,15},{10,... | collective-permute-start | bytes 3080 | tf_op jit(solution)/shard_map/ppermute | solution.py:346
  85.9 3.6 %collective-permute-start.20 = (f32[2,128]{1,0:T(2,128)S(1)}, f32[2,128]{1,0:T(2,128)S(1)}, u32[]{:S(2)}, u32[]{:S(2)}) collective-permute-start(f32[2,128]{1,0:T(2,128)S(1)} %norms_pair.1.refs_0_), channel_id=1, source_target_pairs={{0,2},{1,3},{2,0},{3,1},{4,6},{5,7},{6,4},{7,5},{8,10},{9,11},{10,... | collective-permute-start | bytes 3080 | tf_op jit(solution)/shard_map/ppermute | solution.py:346

commit v5 on v4

--- a/solution.py
+++ b/solution.py
@@ -224,7 +224,7 @@
         lhs8_ref[0:rows, :] = rough
         lhs8_ref[rows : 2 * rows, :] = (scaled - rough) * 16.0
         lhs8 = lhs8_ref[...].astype(F8)
-        out[...] = jnp.zeros_like(out)
+        out[:, :, :, sz.chunk :] = jnp.zeros((2, sz.half, 2 * rows, sz.extra), F32)
         size = min(sz.piece, sz.block)
         for b in range(sz.held):
             bit = b // sz.per_bit

time: 90.6 us -> 90.6 us (level)
  no operation moved by 1% of the time
where the time goes in v5:
time: 90.6 us; the launch traced here: 90.2 us
  starting transfers between devices  38.3 us (42%)
  Pallas kernels  30.3 us (33%)
  waiting for transfers between devices  21.5 us (24%)
    ppermute x12, starting transfers between devices, hand_over(): came.append(in_vmem(lax.ppermute(x, AXES, pairs)))  30.8 us
    pallas_call x1, Pallas kernels, on_device(): pl.pallas_call(functools.partial(first_kernel, sz), out_shape=(pltpu.VMEM...  22 us
    ppermute x11, waiting for transfers between devices, permute(): return in_vmem(lax.ppermute(x, AXES, pairs))  15.2 us
    ppermute x11, starting transfers between devices, permute(): return in_vmem(lax.ppermute(x, AXES, pairs))  7.48 us
    pallas_call x3, Pallas kernels, on_device(): pl.pallas_call(functools.partial(site_kernel, sz, step), out_shape=shapes...  7.37 us
    ppermute x12, waiting for transfers between devices, hand_over(): came.append(in_vmem(lax.ppermute(x, AXES, pairs)))  6.31 us
  transfers between devices with their start and end apart: 23, of which 15 were waited for; matrix products, arithmetic and copies ran while one was open for 0% of the time, Pallas kernels for 0%

profile of v5, /device:TPU:6, one launch (start us, length us, event | category | flops | bytes accessed | tf_op | source)
XLA Modules:
  0.0 90.2 jit_solution(3546947360714474580)
XLA Ops:
  0.0 22.0 %first_site.1 = (f32[4,2,1152]{2,1,0:T(2,128)S(1)}, f32[4,2,1152]{2,1,0:T(2,128)S(1)}, f32[4,16,1152]{2,1,0:T(8,128)S(1)}, f32[4,16,1152]{2,1,0:T(8,128)S(1)}, s...) custom-call(s32[1,32]{1,0:T(1,128)} %bitcast.6, ...), custom_call_target="tpu_custom_call" | custom-call | tf_op jit(solution)/shard_map/first_site/pallas_call | solution.py:381
  22.0 0.1 collective-permute-start
  22.1 1.2 %collective-permute-done.came = f32[4,2,1152]{2,1,0:T(2,128)S(1)} collective-permute-done((f32[4,2,1152]{2,1,0:T(2,128)S(1)}, f32[4,2,1152]{2,1,0:T(2,128)S(1)}, u32[]{:S(2)}, u32[]{:S(2)}) %collective-permute-start) | collective-permute-done | bytes 36896 | tf_op jit(solution)/shard_map/ppermute | solution.py:346
  23.3 0.7 collective-permute-start.1
  24.0 0.7 collective-permute-start.2
  24.6 0.7 collective-permute-start.3
  25.3 0.7 collective-permute-start.4
  26.0 0.0 collective-permute-done.1.refs_2_
  26.0 0.0 collective-permute-done.2.refs_3_
  26.0 0.0 collective-permute-done.3.refs_4_
  26.0 0.0 collective-permute-done.4.refs_5_
  26.0 0.3 site_1.1
  26.3 0.2 collective-permute-start.5
  26.5 1.1 %collective-permute-done.5.came = f32[4,4,1152]{2,1,0:T(4,128)S(1)} collective-permute-done((f32[4,4,1152]{2,1,0:T(4,128)S(1)}, f32[4,4,1152]{2,1,0:T(4,128)S(1)}, u32[]{:S(2)}, u32[]{:S(2)}) %collective-permute-start.5) | collective-permute-done | bytes 73760 | tf_op jit(solution)/shard_map/ppermute | solution.py:346
  27.6 9.3 %collective-permute-start.6 = (f32[4,1152]{1,0:T(4,128)S(1)}, f32[4,1152]{1,0:T(4,128)S(1)}, u32[]{:S(2)}, u32[]{:S(2)}) collective-permute-start(f32[4,1152]{1,0:T(4,128)S(1)} %get-tuple-element.75), channel_id=1, source_target_pairs={{0,14},{1,15},{2,8},{3,9},{4,10},{5,11},{6,12},{7,13},{8,22},{9,23... | collective-permute-start | bytes 55304 | tf_op jit(solution)/shard_map/ppermute | solution.py:362
  36.9 10.0 %collective-permute-start.7 = (f32[4,1152]{1,0:T(4,128)S(1)}, f32[4,1152]{1,0:T(4,128)S(1)}, u32[]{:S(2)}, u32[]{:S(2)}) collective-permute-start(f32[4,1152]{1,0:T(4,128)S(1)} %get-tuple-element.76), channel_id=1, source_target_pairs={{0,12},{1,13},{2,14},{3,15},{4,8},{5,9},{6,10},{7,11},{8,20},{9,21... | collective-permute-start | bytes 55304 | tf_op jit(solution)/shard_map/ppermute | solution.py:362
  46.9 0.7 collective-permute-start.8
  47.6 0.7 collective-permute-start.9
  48.3 0.0 collective-permute-done.6.refs_2_
  48.3 0.1 collective-permute-done.7.refs_3_
  48.4 0.0 collective-permute-done.8.refs_4_
  48.4 0.0 collective-permute-done.9.refs_5_
  48.4 0.2 site_2.1
  48.6 0.1 collective-permute-start.10
  48.7 1.4 %collective-permute-done.10.came = f32[4,8,1152]{2,1,0:T(8,128)S(1)} collective-permute-done((f32[4,8,1152]{2,1,0:T(8,128)S(1)}, f32[4,8,1152]{2,1,0:T(8,128)S(1)}, u32[]{:S(2)}, u32[]{:S(2)}) %collective-permute-start.10) | collective-permute-done | bytes 147488 | tf_op jit(solution)/shard_map/ppermute | solution.py:346
  50.1 4.9 %collective-permute-start.11 = (f32[8,1152]{1,0:T(8,128)S(1)}, f32[8,1152]{1,0:T(8,128)S(1)}, u32[]{:S(2)}, u32[]{:S(2)}) collective-permute-start(f32[8,1152]{1,0:T(8,128)S(1)} %get-tuple-element.83), channel_id=1, source_target_pairs={{0,14},{1,15},{2,8},{3,9},{4,10},{5,11},{6,12},{7,13},{8,22},{9,23... | collective-permute-start | bytes 110600 | tf_op jit(solution)/shard_map/ppermute | solution.py:362
  55.0 0.1 collective-permute-start.12
  55.0 1.3 %collective-permute-start.13 = (f32[8,1152]{1,0:T(8,128)S(1)}, f32[8,1152]{1,0:T(8,128)S(1)}, u32[]{:S(2)}, u32[]{:S(2)}) collective-permute-start(f32[8,1152]{1,0:T(8,128)S(1)} %get-tuple-element.85), channel_id=1, source_target_pairs={{16,26},{17,27},{18,28},{19,29},{20,30},{21,31},{22,24},{23,25}} | collective-permute-start | bytes 110600 | tf_op jit(solution)/shard_map/ppermute | solution.py:362
  56.3 1.3 %collective-permute-start.14 = (f32[8,1152]{1,0:T(8,128)S(1)}, f32[8,1152]{1,0:T(8,128)S(1)}, u32[]{:S(2)}, u32[]{:S(2)}) collective-permute-start(f32[8,1152]{1,0:T(8,128)S(1)} %get-tuple-element.86), channel_id=1, source_target_pairs={{16,24},{17,25},{18,26},{19,27},{20,28},{21,29},{22,30},{23,31}} | collective-permute-start | bytes 110600 | tf_op jit(solution)/shard_map/ppermute | solution.py:362
  57.6 3.3 %collective-permute-done.11.refs_2_ = f32[8,1152]{1,0:T(8,128)S(1)} collective-permute-done((f32[8,1152]{1,0:T(8,128)S(1)}, f32[8,1152]{1,0:T(8,128)S(1)}, u32[]{:S(2)}, u32[]{:S(2)}) %collective-permute-start.11) | collective-permute-done | bytes 36896 | tf_op jit(solution)/shard_map/ppermute | solution.py:362
  60.9 1.7 %collective-permute-done.12.refs_3_ = f32[8,1152]{1,0:T(8,128)S(1)} collective-permute-done((f32[8,1152]{1,0:T(8,128)S(1)}, f32[8,1152]{1,0:T(8,128)S(1)}, u32[]{:S(2)}, u32[]{:S(2)}) %collective-permute-start.12) | collective-permute-done | bytes 36896 | tf_op jit(solution)/shard_map/ppermute | solution.py:362
  62.6 1.1 %collective-permute-done.13.refs_4_ = f32[8,1152]{1,0:T(8,128)S(1)} collective-permute-done((f32[8,1152]{1,0:T(8,128)S(1)}, f32[8,1152]{1,0:T(8,128)S(1)}, u32[]{:S(2)}, u32[]{:S(2)}) %collective-permute-start.13) | collective-permute-done | bytes 36896 | tf_op jit(solution)/shard_map/ppermute | solution.py:362
  63.7 0.1 collective-permute-done.14.refs_5_
  63.8 6.9 %site_3.1 = (f32[4,16,1152]{2,1,0:T(8,128)S(1)}, f32[4,16,1152]{2,1,0:T(8,128)S(1)}) custom-call(s32[1,32]{1,0:T(1,128)S(1)} %get-tuple-element.51.refs_0_, f32[32,128]{1,0:T(8,128)S(1)} %get-tuple-element.52.refs_1_, f32[8,1152]{1,0:T(8,128)S(1)} %collective-permute-done.11.refs_2_, ...), custom_call_target="tpu_custom_call", output_to_operand_aliasing={{0}: (18, {}), {1}: (19, {})} | custom-call | tf_op jit(solution)/shard_map/site_3/pallas_call | solution.py:412
  70.7 0.1 collective-permute-start.15
  70.8 1.6 %collective-permute-done.15.came = f32[4,16,1152]{2,1,0:T(8,128)S(1)} collective-permute-done((f32[4,16,1152]{2,1,0:T(8,128)S(1)}, f32[4,16,1152]{2,1,0:T(8,128)S(1)}, u32[]{:S(2)}, u32[]{:S(2)}) %collective-permute-start.15) | collective-permute-done | bytes 294944 | tf_op jit(solution)/shard_map/ppermute | solution.py:346
  72.4 0.6 collective-permute-start.16
  73.0 2.3 %collective-permute-start.17 = (f32[16,1152]{1,0:T(8,128)S(1)}, f32[16,1152]{1,0:T(8,128)S(1)}, u32[]{:S(2)}, u32[]{:S(2)}) collective-permute-start(f32[16,1152]{1,0:T(8,128)S(1)} %get-tuple-element.92), channel_id=1, source_target_pairs={{0,6},{1,7},{2,4},{3,5},{4,2},{5,3},{6,0},{7,1},{8,14},{9,15},{10,... | collective-permute-start | bytes 221192 | tf_op jit(solution)/shard_map/ppermute | solution.py:346
  75.3 0.6 collective-permute-start.18
  75.9 0.9 collective-permute-done.16.refs_0_
  76.8 3.3 %collective-permute-done.17.refs_1_ = f32[16,1152]{1,0:T(8,128)S(1)} collective-permute-done((f32[16,1152]{1,0:T(8,128)S(1)}, f32[16,1152]{1,0:T(8,128)S(1)}, u32[]{:S(2)}, u32[]{:S(2)}) %collective-permute-start.17) | collective-permute-done | bytes 73760 | tf_op jit(solution)/shard_map/ppermute | solution.py:346
  80.1 2.8 %collective-permute-done.18.refs_2_ = f32[16,1152]{1,0:T(8,128)S(1)} collective-permute-done((f32[16,1152]{1,0:T(8,128)S(1)}, f32[16,1152]{1,0:T(8,128)S(1)}, u32[]{:S(2)}, u32[]{:S(2)}) %collective-permute-start.18) | collective-permute-done | bytes 73760 | tf_op jit(solution)/shard_map/ppermute | solution.py:346
  82.8 0.1 norms.1.left
  83.0 0.0 collective-permute-start.19
  83.0 1.1 %collective-permute-done.19.right = f32[2,128]{1,0:T(2,128)S(1)} collective-permute-done((f32[2,128]{1,0:T(2,128)S(1)}, f32[2,128]{1,0:T(2,128)S(1)}, u32[]{:S(2)}, u32[]{:S(2)}) %collective-permute-start.19) | collective-permute-done | bytes 1056 | tf_op jit(solution)/shard_map/ppermute | solution.py:346
  84.1 0.0 collective-permute-start.22
  84.1 1.8 %collective-permute-start.21 = (f32[2,128]{1,0:T(2,128)S(1)}, f32[2,128]{1,0:T(2,128)S(1)}, u32[]{:S(2)}, u32[]{:S(2)}) collective-permute-start(f32[2,128]{1,0:T(2,128)S(1)} %norms_pair.1.refs_0_), channel_id=1, source_target_pairs={{0,6},{1,7},{2,4},{3,5},{4,2},{5,3},{6,0},{7,1},{8,14},{9,15},{10,... | collective-permute-start | bytes 3080 | tf_op jit(solution)/shard_map/ppermute | solution.py:346
  85.9 1.7 %collective-permute-start.20 = (f32[2,128]{1,0:T(2,128)S(1)}, f32[2,128]{1,0:T(2,128)S(1)}, u32[]{:S(2)}, u32[]{:S(2)}) collective-permute-start(f32[2,128]{1,0:T(2,128)S(1)} %norms_pair.1.refs_0_), channel_id=1, source_target_pairs={{0,2},{1,3},{2,0},{3,1},{4,6},{5,7},{6,4},{7,5},{8,10},{9,11},{10,... | collective-permute-start | bytes 3080 | tf_op jit(solution)/shard_map/ppermute | solution.py:346
  87.6 1.0 %collective-permute-done.22.refs_3_ = f32[2,128]{1,0:T(2,128)S(1)} collective-permute-done((f32[2,128]{1,0:T(2,128)S(1)}, f32[2,128]{1,0:T(2,128)S(1)}, u32[]{:S(2)}, u32[]{:S(2)}) %collective-permute-start.22) | collective-permute-done | bytes 1056 | tf_op jit(solution)/shard_map/ppermute | solution.py:346
  88.6 0.9 %collective-permute-done.21.refs_2_ = f32[2,128]{1,0:T(2,128)S(1)} collective-permute-done((f32[2,128]{1,0:T(2,128)S(1)}, f32[2,128]{1,0:T(2,128)S(1)}, u32[]{:S(2)}, u32[]{:S(2)}) %collective-permute-start.21) | collective-permute-done | bytes 1056 | tf_op jit(solution)/shard_map/ppermute | solution.py:346
  89.5 0.0 collective-permute-done.20.refs_1_
  89.5 0.7 probs.1
  (5 shorter events, 0.1 us)
Async XLA Ops:
  22.0 1.3 %collective-permute-start = (f32[4,2,1152]{2,1,0:T(2,128)S(1)}, f32[4,2,1152]{2,1,0:T(2,128)S(1)}, u32[]{:S(2)}, u32[]{:S(2)}) collective-permute-start(f32[4,2,1152]{2,1,0:T(2,128)S(1)} %get-tuple-element.54), channel_id=1, source_target_pairs={{0,1},{1,0},{2,3},{3,2},{4,5},{5,4},{6,7},{7,6},{8,9},{9,8},{10,11... | collective-permute-start | bytes 110600 | tf_op jit(solution)/shard_map/ppermute | solution.py:346
  23.3 2.7 %collective-permute-start.1 = (f32[2,1152]{1,0:T(2,128)S(1)}, f32[2,1152]{1,0:T(2,128)S(1)}, u32[]{:S(2)}, u32[]{:S(2)}) collective-permute-start(f32[2,1152]{1,0:T(2,128)S(1)} %get-tuple-element.55), channel_id=1, source_target_pairs={{0,14},{1,15},{2,8},{3,9},{4,10},{5,11},{6,12},{7,13}} | collective-permute-start | bytes 27656 | tf_op jit(solution)/shard_map/ppermute | solution.py:362
  24.0 2.0 %collective-permute-start.2 = (f32[2,1152]{1,0:T(2,128)S(1)}, f32[2,1152]{1,0:T(2,128)S(1)}, u32[]{:S(2)}, u32[]{:S(2)}) collective-permute-start(f32[2,1152]{1,0:T(2,128)S(1)} %get-tuple-element.56), channel_id=1, source_target_pairs={{0,12},{1,13},{2,14},{3,15},{4,8},{5,9},{6,10},{7,11}} | collective-permute-start | bytes 27656 | tf_op jit(solution)/shard_map/ppermute | solution.py:362
  24.6 1.4 %collective-permute-start.3 = (f32[2,1152]{1,0:T(2,128)S(1)}, f32[2,1152]{1,0:T(2,128)S(1)}, u32[]{:S(2)}, u32[]{:S(2)}) collective-permute-start(f32[2,1152]{1,0:T(2,128)S(1)} %get-tuple-element.57), channel_id=1, source_target_pairs={{0,10},{1,11},{2,12},{3,13},{4,14},{5,15},{6,8},{7,9}} | collective-permute-start | bytes 27656 | tf_op jit(solution)/shard_map/ppermute | solution.py:362
  25.3 0.7 collective-permute-start.4
  26.3 1.3 %collective-permute-start.5 = (f32[4,4,1152]{2,1,0:T(4,128)S(1)}, f32[4,4,1152]{2,1,0:T(4,128)S(1)}, u32[]{:S(2)}, u32[]{:S(2)}) collective-permute-start(f32[4,4,1152]{2,1,0:T(4,128)S(1)} %get-tuple-element.74), channel_id=1, source_target_pairs={{0,1},{1,0},{2,3},{3,2},{4,5},{5,4},{6,7},{7,6},{8,9},{9,8},{10,11... | collective-permute-start | bytes 221192 | tf_op jit(solution)/shard_map/ppermute | solution.py:346
  27.6 20.6 %collective-permute-start.6 = (f32[4,1152]{1,0:T(4,128)S(1)}, f32[4,1152]{1,0:T(4,128)S(1)}, u32[]{:S(2)}, u32[]{:S(2)}) collective-permute-start(f32[4,1152]{1,0:T(4,128)S(1)} %get-tuple-element.75), channel_id=1, source_target_pairs={{0,14},{1,15},{2,8},{3,9},{4,10},{5,11},{6,12},{7,13},{8,22},{9,23... | collective-permute-start | bytes 55304 | tf_op jit(solution)/shard_map/ppermute | solution.py:362
  36.9 11.5 %collective-permute-start.7 = (f32[4,1152]{1,0:T(4,128)S(1)}, f32[4,1152]{1,0:T(4,128)S(1)}, u32[]{:S(2)}, u32[]{:S(2)}) collective-permute-start(f32[4,1152]{1,0:T(4,128)S(1)} %get-tuple-element.76), channel_id=1, source_target_pairs={{0,12},{1,13},{2,14},{3,15},{4,8},{5,9},{6,10},{7,11},{8,20},{9,21... | collective-permute-start | bytes 55304 | tf_op jit(solution)/shard_map/ppermute | solution.py:362
  46.9 1.5 %collective-permute-start.8 = (f32[4,1152]{1,0:T(4,128)S(1)}, f32[4,1152]{1,0:T(4,128)S(1)}, u32[]{:S(2)}, u32[]{:S(2)}) collective-permute-start(f32[4,1152]{1,0:T(4,128)S(1)} %get-tuple-element.77), channel_id=1, source_target_pairs={{8,18},{9,19},{10,20},{11,21},{12,22},{13,23},{14,16},{15,17}} | collective-permute-start | bytes 55304 | tf_op jit(solution)/shard_map/ppermute | solution.py:362
  47.6 0.8 collective-permute-start.9
  48.6 1.4 %collective-permute-start.10 = (f32[4,8,1152]{2,1,0:T(8,128)S(1)}, f32[4,8,1152]{2,1,0:T(8,128)S(1)}, u32[]{:S(2)}, u32[]{:S(2)}) collective-permute-start(f32[4,8,1152]{2,1,0:T(8,128)S(1)} %get-tuple-element.82), channel_id=1, source_target_pairs={{0,1},{1,0},{2,3},{3,2},{4,5},{5,4},{6,7},{7,6},{8,9},{9,8},{10,11... | collective-permute-start | bytes 442376 | tf_op jit(solution)/shard_map/ppermute | solution.py:346
  50.1 10.8 %collective-permute-start.11 = (f32[8,1152]{1,0:T(8,128)S(1)}, f32[8,1152]{1,0:T(8,128)S(1)}, u32[]{:S(2)}, u32[]{:S(2)}) collective-permute-start(f32[8,1152]{1,0:T(8,128)S(1)} %get-tuple-element.83), channel_id=1, source_target_pairs={{0,14},{1,15},{2,8},{3,9},{4,10},{5,11},{6,12},{7,13},{8,22},{9,23... | collective-permute-start | bytes 110600 | tf_op jit(solution)/shard_map/ppermute | solution.py:362
  55.0 7.7 %collective-permute-start.12 = (f32[8,1152]{1,0:T(8,128)S(1)}, f32[8,1152]{1,0:T(8,128)S(1)}, u32[]{:S(2)}, u32[]{:S(2)}) collective-permute-start(f32[8,1152]{1,0:T(8,128)S(1)} %get-tuple-element.84), channel_id=1, source_target_pairs={{0,12},{1,13},{2,14},{3,15},{4,8},{5,9},{6,10},{7,11},{8,20},{9,21... | collective-permute-start | bytes 110600 | tf_op jit(solution)/shard_map/ppermute | solution.py:362
  55.0 8.6 %collective-permute-start.13 = (f32[8,1152]{1,0:T(8,128)S(1)}, f32[8,1152]{1,0:T(8,128)S(1)}, u32[]{:S(2)}, u32[]{:S(2)}) collective-permute-start(f32[8,1152]{1,0:T(8,128)S(1)} %get-tuple-element.85), channel_id=1, source_target_pairs={{16,26},{17,27},{18,28},{19,29},{20,30},{21,31},{22,24},{23,25}} | collective-permute-start | bytes 110600 | tf_op jit(solution)/shard_map/ppermute | solution.py:362
  56.3 7.5 %collective-permute-start.14 = (f32[8,1152]{1,0:T(8,128)S(1)}, f32[8,1152]{1,0:T(8,128)S(1)}, u32[]{:S(2)}, u32[]{:S(2)}) collective-permute-start(f32[8,1152]{1,0:T(8,128)S(1)} %get-tuple-element.86), channel_id=1, source_target_pairs={{16,24},{17,25},{18,26},{19,27},{20,28},{21,29},{22,30},{23,31}} | collective-permute-start | bytes 110600 | tf_op jit(solution)/shard_map/ppermute | solution.py:362
  70.7 1.6 %collective-permute-start.15 = (f32[4,16,1152]{2,1,0:T(8,128)S(1)}, f32[4,16,1152]{2,1,0:T(8,128)S(1)}, u32[]{:S(2)}, u32[]{:S(2)}) collective-permute-start(f32[4,16,1152]{2,1,0:T(8,128)S(1)} %get-tuple-element.90), channel_id=1, source_target_pairs={{0,1},{1,0},{2,3},{3,2},{4,5},{5,4},{6,7},{7,6},{8,9},{9,8},{10,11... | collective-permute-start | bytes 884744 | tf_op jit(solution)/shard_map/ppermute | solution.py:346
  72.4 4.4 %collective-permute-start.16 = (f32[16,1152]{1,0:T(8,128)S(1)}, f32[16,1152]{1,0:T(8,128)S(1)}, u32[]{:S(2)}, u32[]{:S(2)}) collective-permute-start(f32[16,1152]{1,0:T(8,128)S(1)} %get-tuple-element.91), channel_id=1, source_target_pairs={{0,2},{1,3},{2,0},{3,1},{4,6},{5,7},{6,4},{7,5},{8,10},{9,11},{10,... | collective-permute-start | bytes 221192 | tf_op jit(solution)/shard_map/ppermute | solution.py:346
  73.0 7.1 %collective-permute-start.17 = (f32[16,1152]{1,0:T(8,128)S(1)}, f32[16,1152]{1,0:T(8,128)S(1)}, u32[]{:S(2)}, u32[]{:S(2)}) collective-permute-start(f32[16,1152]{1,0:T(8,128)S(1)} %get-tuple-element.92), channel_id=1, source_target_pairs={{0,6},{1,7},{2,4},{3,5},{4,2},{5,3},{6,0},{7,1},{8,14},{9,15},{10,... | collective-permute-start | bytes 221192 | tf_op jit(solution)/shard_map/ppermute | solution.py:346
  75.3 7.6 %collective-permute-start.18 = (f32[16,1152]{1,0:T(8,128)S(1)}, f32[16,1152]{1,0:T(8,128)S(1)}, u32[]{:S(2)}, u32[]{:S(2)}) collective-permute-start(f32[16,1152]{1,0:T(8,128)S(1)} %get-tuple-element.93), channel_id=1, source_target_pairs={{0,4},{1,5},{2,6},{3,7},{4,0},{5,1},{6,2},{7,3},{8,12},{9,13},{10,... | collective-permute-start | bytes 221192 | tf_op jit(solution)/shard_map/ppermute | solution.py:346
  83.0 1.1 %collective-permute-start.19 = (f32[2,128]{1,0:T(2,128)S(1)}, f32[2,128]{1,0:T(2,128)S(1)}, u32[]{:S(2)}, u32[]{:S(2)}) collective-permute-start(f32[2,128]{1,0:T(2,128)S(1)} %norms.1.left), channel_id=1, source_target_pairs={{0,1},{1,0},{2,3},{3,2},{4,5},{5,4},{6,7},{7,6},{8,9},{9,8},{10,11... | collective-permute-start | bytes 3080 | tf_op jit(solution)/shard_map/ppermute | solution.py:346
  84.1 4.5 %collective-permute-start.22 = (f32[2,128]{1,0:T(2,128)S(1)}, f32[2,128]{1,0:T(2,128)S(1)}, u32[]{:S(2)}, u32[]{:S(2)}) collective-permute-start(f32[2,128]{1,0:T(2,128)S(1)} %norms_pair.1.refs_0_), channel_id=1, source_target_pairs={{0,4},{1,5},{2,6},{3,7},{4,0},{5,1},{6,2},{7,3},{8,12},{9,13},{10,... | collective-permute-start | bytes 3080 | tf_op jit(solution)/shard_map/ppermute | solution.py:346
  84.1 5.4 %collective-permute-start.21 = (f32[2,128]{1,0:T(2,128)S(1)}, f32[2,128]{1,0:T(2,128)S(1)}, u32[]{:S(2)}, u32[]{:S(2)}) collective-permute-start(f32[2,128]{1,0:T(2,128)S(1)} %norms_pair.1.refs_0_), channel_id=1, source_target_pairs={{0,6},{1,7},{2,4},{3,5},{4,2},{5,3},{6,0},{7,1},{8,14},{9,15},{10,... | collective-permute-start | bytes 3080 | tf_op jit(solution)/shard_map/ppermute | solution.py:346
  85.9 3.6 %collective-permute-start.20 = (f32[2,128]{1,0:T(2,128)S(1)}, f32[2,128]{1,0:T(2,128)S(1)}, u32[]{:S(2)}, u32[]{:S(2)}) collective-permute-start(f32[2,128]{1,0:T(2,128)S(1)} %norms_pair.1.refs_0_), channel_id=1, source_target_pairs={{0,2},{1,3},{2,0},{3,1},{4,6},{5,7},{6,4},{7,5},{8,10},{9,11},{10,... | collective-permute-start | bytes 3080 | tf_op jit(solution)/shard_map/ppermute | solution.py:346
